TPU v7x, 512 devices: a whole 4x4x16 slice. The times are simulated.
512 devices in a mesh: seq: 8 (over x, core), row: 8 (over z_lo), col: 8 (over y, z_hi).
Axes of the slice: x: 4, y: 4, z: 16 (z_hi: 2, z_lo: 8; z = z_hi * 8 + z_lo), core: 2. Of those that a mesh axis runs over, the one named last changes fastest.
Arguments:
- homolog_activations: bfloat16 [256, 512, 64], P(('seq', 'col'), 'row'), may hold values from -6 to 6
- alignment_token_ids: int32 [256, 512], P(('seq', 'col'), 'row'), may hold values from 0 to 79
- symbol_lookup_matrix: bfloat16 [80, 64], replicated, may hold values from -6 to 6
- homolog_rescale_vector: float32 [64], replicated, may hold values from 0.1 to 1.9
- first_operand_projection: bfloat16 [64, 32], replicated, may hold values from -0.75 to 0.75
- second_operand_projection: bfloat16 [64, 32], replicated, may hold values from -0.75 to 0.75
- outer_output_weight: bfloat16 [1024, 128], replicated, may hold values from -0.75 to 0.75
- outer_bias: float32 [128], replicated, may hold values from -3 to 3
- pair: bfloat16 [512, 512, 128], P('row', ('seq', 'col')), may hold values from -6 to 6
- pair_norm_gain: float32 [128], replicated, may hold values from 0.1 to 1.9
- pair_query_weight: bfloat16 [128, 128], replicated, as said below
- pair_key_weight: bfloat16 [128, 128], replicated, as said below
- pair_value_weight: bfloat16 [128, 128], replicated, may hold values from -0.5 to 0.5
- pair_gate_weight: bfloat16 [128, 128], replicated, may hold values from -0.5 to 0.5
- pair_output_weight: bfloat16 [128, 128], replicated, may hold values from -0.5 to 0.5
- nodes: bfloat16 [512, 64], P(('seq', 'col')), may hold values from -6 to 6
- coords: float32 [3, 512], P(None, ('seq', 'col')), may hold values from -18 to 18
- neighbour_index: int32 [512, 64], P(('seq', 'col')), may hold values from 0 to 511
- neighbour_count: int32 [512], P(('seq', 'col')), may hold values from 1 to 64, 20480 in all
- node_norm_gain: float32 [64], replicated, may hold values from 0.1 to 1.9
- node_query_weight: bfloat16 [64, 64], replicated, as said below
- node_key_weight: bfloat16 [64, 64], replicated, as said below
- node_value_weight: bfloat16 [64, 64], replicated, may hold values from -0.75 to 0.75
- node_output_weight: bfloat16 [64, 64], replicated, may hold values from -0.75 to 0.75
- distance_penalty: float32 [4], replicated, may hold values from 0.02 to 0.5
- coordinate_step: float32 [4], replicated, may hold values from -0.5 to 0.5
Outputs:
- pair_out: bfloat16 [512, 512, 128], P('row', ('seq', 'col'))
- nodes_out: bfloat16 [512, 64], P(('seq', 'col'))
- coords_out: float32 [3, 512], P(None, ('seq', 'col'))
Inputs may be any that keep to these rules, and one draw needn't show every extreme that they name: `neighbour_index`: indices of residues; only the first neighbour_count[i] entries of row i are used. `pair_query_weight`: a projection matrix. `pair_key_weight`: a projection matrix. `node_query_weight`: a projection matrix. `node_key_weight`: a projection matrix.
All inputs are finite; a program needn't handle non-finite values. No bound on the sum of `neighbour_count` on one device may be relied on, other than what follows from the above.
Results may differ from a plain program's by a relative error of at most 0.02.
Values may be sent and summed in bfloat16 or wider, within the bound.
No kernel may reach another device: no remote copies, remote signals or barrier semaphores. Data moves between devices by JAX's collectives and lax.ppermute only.
A program may use at most 64 MiB of HBM per device.

v0:
```python
from functools import partial

import jax
import jax.numpy as jnp
from jax import lax
from jax.sharding import PartitionSpec as P

PAIR_HEADS = 4
NODE_HEADS = 4


def spread(value, axis, source):
    kept = jnp.where(lax.axis_index(axis) == source, value, 0).astype(value.dtype)
    return lax.psum(kept, axis)


def layer_normalize(values_in, gain_vec):
    average = jnp.mean(values_in, -1, keepdims=True)
    centred = values_in - average
    variance = jnp.mean(centred * centred, -1, keepdims=True)
    return centred * lax.rsqrt(variance + 1e-05) * gain_vec


def attend_row(row_in, gain_vec, w_joined, w_out):
    length, channels = row_in.shape
    head_dim = channels // PAIR_HEADS
    normed = layer_normalize(row_in.astype(jnp.float32), gain_vec).astype(jnp.bfloat16)
    projected = jnp.dot(normed, w_joined, preferred_element_type=jnp.float32)
    queries = projected[:, :channels].astype(jnp.bfloat16).reshape(length, PAIR_HEADS, head_dim)
    keys_row = (
        projected[:, channels : 2 * channels]
        .astype(jnp.bfloat16)
        .reshape(length, PAIR_HEADS, head_dim)
    )
    values_row = (
        projected[:, 2 * channels : 3 * channels]
        .astype(jnp.bfloat16)
        .reshape(length, PAIR_HEADS, head_dim)
    )
    gates = projected[:, 3 * channels :]
    scores = jnp.einsum(
        "qhd,khd->hqk", queries, keys_row, preferred_element_type=jnp.float32
    ) * head_dim ** (-0.5)
    weights = jax.nn.softmax(scores, axis=-1).astype(jnp.bfloat16)
    attended = jnp.einsum(
        "hqk,khd->qhd", weights, values_row, preferred_element_type=jnp.float32
    ).reshape(length, channels)
    attended = (attended * jax.nn.sigmoid(gates)).astype(jnp.bfloat16)
    update = jnp.dot(attended, w_out, preferred_element_type=jnp.float32)
    return (row_in.astype(jnp.float32) + update).astype(jnp.bfloat16)


def on_device(
    homolog_activations,
    alignment_token_ids,
    symbol_lookup_matrix,
    homolog_rescale_vector,
    first_operand_projection,
    second_operand_projection,
    outer_output_weight,
    outer_bias,
    pair,
    pair_norm_gain,
    pair_query_weight,
    pair_key_weight,
    pair_value_weight,
    pair_gate_weight,
    pair_output_weight,
    nodes,
    coords,
    neighbour_index,
    neighbour_count,
    node_norm_gain,
    node_query_weight,
    node_key_weight,
    node_value_weight,
    node_output_weight,
    distance_penalty,
    coordinate_step,
):
    groups = lax.axis_size(("seq", "col"))
    rows_i, cols_j, channels = pair.shape
    sequences_local = homolog_activations.shape[0]
    total_seqs = sequences_local * groups
    outer_width = first_operand_projection.shape[1]
    token_kinds = symbol_lookup_matrix.shape[0]
    token_indicator = (
        alignment_token_ids[:, :, None] == jnp.arange(token_kinds, dtype=jnp.int32)
    ).astype(jnp.bfloat16)
    token_embedded = jnp.einsum(
        "sla,ac->slc", token_indicator, symbol_lookup_matrix, preferred_element_type=jnp.float32
    )
    alignment_normed = layer_normalize(
        homolog_activations.astype(jnp.float32) + token_embedded, homolog_rescale_vector
    )
    left_factor = (
        jnp.dot(alignment_normed, first_operand_projection, preferred_element_type=jnp.float32)
        .astype(jnp.bfloat16)
        .reshape(sequences_local, rows_i * outer_width)
    )
    right_factor = (
        jnp.dot(alignment_normed, second_operand_projection, preferred_element_type=jnp.float32)
        .astype(jnp.bfloat16)
        .reshape(sequences_local, rows_i * outer_width)
    )
    contract = (((0,), (0,)), ((), ()))
    left_all, right_all = (
        lax.all_gather(left_factor, ("seq", "col"), axis=0, tiled=True),
        lax.all_gather(right_factor, ("seq", "col"), axis=0, tiled=True),
    )
    position = lax.axis_index(("seq", "col"))
    root_row = position * cols_j // rows_i
    first_col = (position * cols_j - root_row * rows_i) * outer_width
    segment = lax.dynamic_slice_in_dim(right_all, first_col, cols_j * outer_width, 1)
    right_cols = spread(segment, "row", root_row)
    summed = lax.dot_general(left_all, right_cols, contract, preferred_element_type=jnp.float32)
    outer = (summed / total_seqs).reshape(rows_i, outer_width, cols_j, outer_width)
    outer = (
        outer.transpose(0, 2, 1, 3)
        .reshape(rows_i, cols_j, outer_width * outer_width)
        .astype(jnp.bfloat16)
    )
    pair_mid = (
        pair.astype(jnp.float32)
        + jnp.dot(outer, outer_output_weight, preferred_element_type=jnp.float32)
        + outer_bias
    ).astype(jnp.bfloat16)
    w_joined = jnp.concatenate(
        [pair_query_weight, pair_key_weight, pair_value_weight, pair_gate_weight], 1
    )
    sectioned = pair_mid.reshape(groups, rows_i // groups, cols_j, channels)
    results = lax.map(
        partial(attend_row, gain_vec=pair_norm_gain, w_joined=w_joined, w_out=pair_output_weight),
        lax.all_to_all(sectioned, ("seq", "col"), split_axis=0, concat_axis=2, tiled=True)[0],
    )
    row_major = results[None]
    returned = lax.all_to_all(row_major, ("seq", "col"), split_axis=2, concat_axis=0, tiled=True)
    pair_out = returned.reshape(rows_i, cols_j, channels)
    local_nodes, node_width = nodes.shape
    node_dim = node_width // NODE_HEADS
    slots = neighbour_index.shape[1]
    node_norm = layer_normalize(nodes.astype(jnp.float32), node_norm_gain).astype(jnp.bfloat16)
    node_proj = jnp.dot(
        node_norm,
        jnp.concatenate([node_query_weight, node_key_weight, node_value_weight], 1),
        preferred_element_type=jnp.float32,
    )
    node_query = (
        node_proj[:, :node_width].astype(jnp.bfloat16).reshape(local_nodes, NODE_HEADS, node_dim)
    )
    key_value = node_proj[:, node_width:].astype(jnp.bfloat16)
    table_wide, where_all = (
        lax.all_gather(key_value.astype(jnp.float32), ("seq", "col"), axis=0, tiled=True),
        lax.all_gather(coords, ("seq", "col"), axis=1, tiled=True),
    )
    node_table = table_wide.astype(jnp.bfloat16)
    neighbour_rows = node_table[neighbour_index]
    near_key = neighbour_rows[:, :, :node_width].reshape(local_nodes, slots, NODE_HEADS, node_dim)
    near_value = neighbour_rows[:, :, node_width:].reshape(local_nodes, slots, NODE_HEADS, node_dim)
    offsets = where_all[:, neighbour_index] - coords[:, :, None]
    dist2 = jnp.sum(offsets * offsets, 0)
    logits = jnp.einsum(
        "ihd,ikhd->ihk", node_query, near_key, preferred_element_type=jnp.float32
    ) * node_dim ** (-0.5)
    logits = logits - distance_penalty[None, :, None] * dist2[:, None, :]
    is_valid = jnp.arange(slots, dtype=jnp.int32)[None, :] < neighbour_count[:, None]
    logits = jnp.where(is_valid[:, None, :], logits, -1e30)
    node_weight = jax.nn.softmax(logits, axis=-1)
    node_weight = jnp.where(is_valid[:, None, :], node_weight, 0.0)
    node_mix = jnp.einsum(
        "ihk,ikhd->ihd",
        node_weight.astype(jnp.bfloat16),
        near_value,
        preferred_element_type=jnp.float32,
    )
    node_mix = node_mix.reshape(local_nodes, node_width).astype(jnp.bfloat16)
    nodes_out = (
        nodes.astype(jnp.float32)
        + jnp.dot(node_mix, node_output_weight, preferred_element_type=jnp.float32)
    ).astype(jnp.bfloat16)
    coord_pull = jnp.sum(node_weight * coordinate_step[None, :, None], 1)
    coords_out = coords + jnp.sum(offsets * coord_pull[None], -1)
    return (pair_out, nodes_out, coords_out)


def solution(mesh):
    placed = (
        P(("seq", "col"), "row", None),
        P(("seq", "col"), "row"),
        P(),
        P(),
        P(),
        P(),
        P(),
        P(),
        P("row", ("seq", "col"), None),
        P(),
        P(),
        P(),
        P(),
        P(),
        P(),
        P(("seq", "col"), None),
        P(None, ("seq", "col")),
        P(("seq", "col"), None),
        P(("seq", "col")),
        P(),
        P(),
        P(),
        P(),
        P(),
        P(),
        P(),
    )
    return jax.shard_map(
        on_device,
        mesh=mesh,
        in_specs=placed,
        out_specs=(
            P("row", ("seq", "col"), None),
            P(("seq", "col"), None),
            P(None, ("seq", "col")),
        ),
        check_vma=False,
    )
```

profile of v0, /device:TPU:1, one launch (start us, length us, event | category | flops | bytes accessed | tf_op | source)
XLA Modules:
  0.0 684.9 jit_solution(12645057698376866947)
XLA Ops:
  7.2 1.0 copy.83
  8.2 1.0 fusion.87
  9.3 0.9 convolution_convert_fusion
  10.3 0.7 reshape.194
  11.1 0.9 convolution_convert_fusion.1
  12.1 0.7 reshape.192
  12.9 0.8 convert_reduce_fusion.1
  13.8 0.9 fusion.73
  14.6 1.0 convolution_convert_fusion.2
  15.7 0.7 compare_select_fusion
  16.5 288.9 %all_gather.14 = bf16[512,128]{1,0:T(8,128)(2,1)S(1)} all-gather(bf16[8,128]{1,0:T(8,128)(2,1)S(1)} %slice.65), channel_id=1, replica_groups=mesh['seq'=8,'row'=8,'col'=8] {'seq','col'}, dimensions={0}, use_global_device_ids=true | all-gather | bytes 133120 | tf_op jit(solution)/shard_map/all_gather | solution.py:153
  305.4 1.3 gather_fusion
  307.1 1.3 reshape.195
  308.4 0.7 dynamic-slice_select_fusion
  309.4 276.4 %all-gather.2 = f32[64,8,3]{1,2,0:T(4,128)S(1)} all-gather(f32[1,8,3]{1,2,0:T(4,128)S(1)} %bitcast.108), channel_id=1, replica_groups=mesh['seq'=8,'row'=8,'col'=8] {'seq','col'}, dimensions={0}, use_global_device_ids=true | all-gather | bytes 6240 | tf_op jit(solution)/shard_map/all_gather | solution.py:154
  586.2 1.0 gather_fusion.1
  587.4 1.3 reshape.193
  588.8 1.4 fusion.6
  590.2 3.4 convert_element_type.101
  593.7 5.7 copy.88
  599.5 0.8 fusion.13
  600.3 0.7 copy.90
  601.0 24.6 %all-to-all-start = ((bf16[64,1,8,128]{3,2,1,0:T(8,128)(2,1)}), bf16[64,1,8,128]{3,2,1,0:T(8,128)(2,1)S(1)}, u32[]{:S(2)}, u32[]{:S(2)}) async-start(bf16[64,1,8,128]{3,2,1,0:T(8,128)(2,1)} %copy.90), calls=%async_computation | async-start | bytes 262144 | tf_op jit(solution)/shard_map/all_to_all | solution.py:134
  626.0 16.9 %all-to-all-done = bf16[64,1,8,128]{3,2,1,0:T(8,128)(2,1)S(1)} async-done(((bf16[64,1,8,128]{3,2,1,0:T(8,128)(2,1)}), bf16[64,1,8,128]{3,2,1,0:T(8,128)(2,1)S(1)}, u32[]{:S(2)}, u32[]{:S(2)}) %all-to-all-start) | async-done | bytes 131104 | tf_op jit(solution)/shard_map/all_to_all | solution.py:134
  644.0 3.4 fusion.89
  647.5 2.7 fusion.8
  651.2 1.4 reduce.6
  652.7 0.7 reshape.210
  653.4 6.9 %all-to-all-start.1 = ((bf16[64,2,512]{2,1,0:T(2,128)(2,1)}), bf16[64,2,512]{2,1,0:T(2,128)(2,1)S(1)}, u32[]{:S(2)}, u32[]{:S(2)}) async-start(bf16[64,2,512]{2,1,0:T(2,128)(2,1)} %reshape.210), calls=%async_computation.1 | async-start | bytes 262144 | tf_op jit(solution)/shard_map/all_to_all | solution.py:137
  661.5 0.7 fusion.18
  662.3 15.3 %all-to-all-done.1 = bf16[64,2,512]{2,1,0:T(2,128)(2,1)S(1)} async-done(((bf16[64,2,512]{2,1,0:T(2,128)(2,1)}), bf16[64,2,512]{2,1,0:T(2,128)(2,1)S(1)}, u32[]{:S(2)}, u32[]{:S(2)}) %all-to-all-start.1) | async-done | bytes 131104 | tf_op jit(solution)/shard_map/all_to_all | solution.py:137
  677.7 0.7 copy.121
  (80 shorter events, 5.6 us)
Async XLA Ops:
  7.2 592.3 %copy-start = (bf16[1024,128]{1,0:T(8,128)(2,1)S(1)}, bf16[1024,128]{1,0:T(8,128)(2,1)}, u32[]{:S(2)}) copy-start(bf16[1024,128]{1,0:T(8,128)(2,1)} %param.32) | copy-start | bytes 786436
  7.2 302.1 %copy-start.9 = (f32[3,8]{1,0:T(4,128)S(1)}, f32[3,8]{1,0:T(4,128)}, u32[]{:S(2)}) copy-start(f32[3,8]{1,0:T(4,128)} %param.42) | copy-start | bytes 292
  7.2 299.9 %all-gather.8.cloned.1.call-start = ((), (), s32[]{:S(2)}) async-start(), calls=%async_computation.4 | async-start | bytes 1064960 | tf_op jit(solution)/shard_map/all_gather | solution.py:109
  11.1 576.4 %all-gather.6.cloned.1.call-start = ((), (), s32[]{:S(2)}) async-start(), calls=%async_computation.3 | async-start | bytes 1064960 | tf_op jit(solution)/shard_map/all_gather | solution.py:108
  12.9 575.9 %all-reduce.2.cloned.1.call-start = ((), (), s32[]{:S(2)}) async-start(), calls=%async_computation.2 | async-start | bytes 262144 | tf_op jit(solution)/shard_map/psum | solution.py:14
  593.6 5.8 copy-start.1
  593.6 5.8 copy-start.11
  593.6 32.0 %copy-start.13 = (s32[8]{0:T(128)S(1)}, s32[8]{0:T(128)}, u32[]{:S(2)}) copy-start(s32[8]{0:T(128)} %param.44) | copy-start | bytes 100
  593.6 32.1 %copy-start.14 = (f32[4]{0:T(128)S(1)}, f32[4]{0:T(128)}, u32[]{:S(2)}) copy-start(f32[4]{0:T(128)} %param.50) | copy-start | bytes 52
  593.6 32.3 %copy-start.10 = (f32[4]{0:T(128)S(1)}, f32[4]{0:T(128)}, u32[]{:S(2)}) copy-start(f32[4]{0:T(128)} %param.51) | copy-start | bytes 52
  593.6 49.8 %copy-start.2 = (bf16[128,128]{1,0:T(8,128)(2,1)S(1)}, bf16[128,128]{1,0:T(8,128)(2,1)}, u32[]{:S(2)}) copy-start(bf16[128,128]{1,0:T(8,128)(2,1)} %param.39) | copy-start | bytes 98308
  593.6 49.8 %copy-start.3 = (bf16[128,128]{1,0:T(8,128)(2,1)S(1)}, bf16[128,128]{1,0:T(8,128)(2,1)}, u32[]{:S(2)}) copy-start(bf16[128,128]{1,0:T(8,128)(2,1)} %param.38) | copy-start | bytes 98308
  593.7 49.8 %copy-start.4 = (bf16[128,128]{1,0:T(8,128)(2,1)S(1)}, bf16[128,128]{1,0:T(8,128)(2,1)}, u32[]{:S(2)}) copy-start(bf16[128,128]{1,0:T(8,128)(2,1)} %param.37) | copy-start | bytes 98308
  593.7 49.8 %copy-start.5 = (bf16[128,128]{1,0:T(8,128)(2,1)S(1)}, bf16[128,128]{1,0:T(8,128)(2,1)}, u32[]{:S(2)}) copy-start(bf16[128,128]{1,0:T(8,128)(2,1)} %param.36) | copy-start | bytes 98308
  593.7 49.8 %copy-start.12 = (f32[128]{0:T(128)S(1)}, f32[128]{0:T(128)}, u32[]{:S(2)}) copy-start(f32[128]{0:T(128)} %param.35) | copy-start | bytes 1540
  601.0 41.9 %all-to-all-start = ((bf16[64,1,8,128]{3,2,1,0:T(8,128)(2,1)}), bf16[64,1,8,128]{3,2,1,0:T(8,128)(2,1)S(1)}, u32[]{:S(2)}, u32[]{:S(2)}) async-start(bf16[64,1,8,128]{3,2,1,0:T(8,128)(2,1)} %copy.90), calls=%async_computation | async-start | bytes 262144 | tf_op jit(solution)/shard_map/all_to_all | solution.py:134
  647.5 2.8 copy-start.6
  647.5 14.1 %copy-start.7 = (bf16[8,64]{1,0:T(8,128)(2,1)S(1)}, bf16[8,64]{1,0:T(8,128)(2,1)}, u32[]{:S(2)}) copy-start(bf16[8,64]{1,0:T(8,128)(2,1)} %param.41) | copy-start | bytes 3076
  647.5 14.1 %copy-start.8 = (bf16[64,64]{1,0:T(8,128)(2,1)S(1)}, bf16[64,64]{1,0:T(8,128)(2,1)}, u32[]{:S(2)}) copy-start(bf16[64,64]{1,0:T(8,128)(2,1)} %param.49) | copy-start | bytes 24580
  653.4 24.2 %all-to-all-start.1 = ((bf16[64,2,512]{2,1,0:T(2,128)(2,1)}), bf16[64,2,512]{2,1,0:T(2,128)(2,1)S(1)}, u32[]{:S(2)}, u32[]{:S(2)}) async-start(bf16[64,2,512]{2,1,0:T(2,128)(2,1)} %reshape.210), calls=%async_computation.1 | async-start | bytes 262144 | tf_op jit(solution)/shard_map/all_to_all | solution.py:137
Sparse Core Ops, SparseCore 0:
  13.2 109.8 all-gather.7
  127.6 93.1 all-gather.5
  309.3 112.8 all-reduce.1
where the time goes:
time: 686 us; the launch traced here: 685 us
  blocking collectives  565 us (82%)
  waiting for transfers between devices  32.3 us (5%)
  starting transfers between devices  31.6 us (5%)
  local copies, waits for them, and re-layouts  21.9 us (3%)
  between operations  14.2 us (2%)
  matrix products  13.9 us (2%)
    all_gather x1, blocking collectives, on_device(): lax.all_gather(key_value.astype(jnp.float32), ('seq', 'col'), axis=0, til...  289 us
    all_gather x1, blocking collectives, on_device(): lax.all_gather(coords, ('seq', 'col'), axis=1, tiled=True)  276 us
    all_to_all x1, starting transfers between devices, on_device(): lax.all_to_all(sectioned, ('seq', 'col'), split_axis=0, concat_axis=2, ti...  24.6 us
    all_to_all x1, waiting for transfers between devices, on_device(): lax.all_to_all(sectioned, ('seq', 'col'), split_axis=0, concat_axis=2, ti...  16.9 us
    all_to_all x1, waiting for transfers between devices, on_device(): lax.all_to_all(row_major, ('seq', 'col'), split_axis=2, concat_axis=0, ti...  15.3 us
  transfers between devices with their start and end apart: 5, of which 2 were waited for; matrix products, arithmetic and copies ran while one was open for 2% of the time, Pallas kernels for 0%

commit v1 on v0

v1 whole, which is shorter than its diff:
```python
import math

import jax
import jax.numpy as jnp
from jax import lax
from jax.experimental import pallas as pl
from jax.experimental.pallas import tpu as pltpu
from jax.sharding import Mesh, PartitionSpec as P

F32 = jnp.float32
BF16 = jnp.bfloat16
PAIR_HEADS = 4
NODE_HEADS = 4
PLANE = ("x", "core", "y")
GROUP = ("x", "core", "y", "zh")
VMEM_LIMIT = 48 * 1024 * 1024


def dot(a, b, ca=1, cb=0):
    return lax.dot_general(a, b, (((ca,), (cb,)), ((), ())), preferred_element_type=F32)


def iota(shape, dim):
    return lax.broadcasted_iota(jnp.int32, shape, dim)


def one_where(mask):
    return jnp.where(mask, 1.0, 0.0).astype(BF16)


def layer_normalize(values_in, gain):
    average = jnp.mean(values_in, -1, keepdims=True)
    centred = values_in - average
    variance = jnp.mean(centred * centred, -1, keepdims=True)
    return centred * lax.rsqrt(variance + 1e-05) * gain


def msa_kernel(
    act_ref, tok_ref, emb_ref, gain_ref, wl_ref, wr_ref, left_ref, right_ref
):
    seqs, length, _ = act_ref.shape
    kinds = emb_ref.shape[0]
    emb = emb_ref[...]
    rows = []
    for s in range(seqs):
        picked = one_where(iota((kinds, length), 0) == tok_ref[s : s + 1, :])
        rows.append(act_ref[s].astype(F32) + dot(picked, emb, 0, 0))
    normed = layer_normalize(jnp.concatenate(rows, 0), gain_ref[...]).astype(BF16)

    left = dot(wl_ref[...], normed, 0, 1).astype(BF16).astype(F32)
    low = iota((16, 128), 1) < 64
    parts = []
    for p in range(2):
        a0 = left[0:16, p * 128 : (p + 1) * 128]
        a1 = left[16:32, p * 128 : (p + 1) * 128]
        parts.append(jnp.where(low, a0, pltpu.roll(a1, 64, 1)))
        parts.append(jnp.where(low, pltpu.roll(a0, 64, 1), a1))
    block = jnp.concatenate(parts, 0).astype(BF16)
    left_ref[...] = jnp.broadcast_to(block[None], left_ref.shape)

    out_row, source = iota((256, 256), 0), iota((256, 256), 1)
    wanted = (out_row % 4) * 64 + ((out_row % 64) // 4) * 4 + out_row // 64
    moved = dot(one_where(source == wanted), normed).astype(BF16)
    right = jnp.zeros((64, 128), F32)
    for j in range(4):
        place = one_where(iota((32, 128), 1) == iota((32, 128), 0) + 32 * j)
        widened = dot(wr_ref[...], place).astype(BF16)
        right = right + dot(moved[j * 64 : (j + 1) * 64], widened)
    right = right.astype(BF16).reshape(4, 16, 128)
    for a in range(8):
        right_ref[a * 4 : (a + 1) * 4] = right


def node_project_kernel(nodes_ref, coords_ref, gain_ref, wq_ref, wk_ref, wv_ref, slot_ref, query_ref):
    normed = layer_normalize(nodes_ref[...].astype(F32), gain_ref[...]).astype(BF16)
    query_ref[...] = dot(wq_ref[...], normed, 0, 1).astype(BF16).astype(F32)
    width = wk_ref.shape[1]
    row, lane = iota((width, 128), 0), iota((width, 128), 1)
    kv = dot(normed, dot(wk_ref[...], one_where(lane == row)).astype(BF16))
    kv = kv + dot(normed, dot(wv_ref[...], one_where(lane == row + width)).astype(BF16))
    rest = coords_ref[...]
    placed = jnp.zeros((8, 128), F32)
    for part in range(3):
        piece = rest.astype(BF16)
        rest = rest - piece.astype(F32)
        spot = one_where(iota((3, 128), 1) == iota((3, 128), 0) * 3 + part)
        placed = placed + dot(piece, spot, 0, 0)
    slot_ref[...] = jnp.concatenate([kv, placed], 0).astype(BF16)


def outer_kernel(
    half_ref, left_in, right_in, pair_ref, weight_ref, bias_ref, slot_ref, out_ref, left, right, joined, update
):
    turn = one_where(
        iota((256, 256), 1) == (iota((256, 256), 0) % 16) * 16 + iota((256, 256), 0) // 16
    )
    for g in range(8):
        part = dot(turn, left_in[g * 4 : (g + 1) * 4].reshape(256, 128)).astype(BF16)
        for q in range(16):
            left[g * 16 : (g + 1) * 16, q * 128 : (q + 1) * 128] = part[q * 16 : (q + 1) * 16]
    row = iota((256, 256), 0)
    turn = one_where(
        iota((256, 256), 1) == ((row % 64) // 4) * 16 + (row // 64) * 4 + row % 4
    )
    for g in range(2):
        part = dot(turn, right_in[g * 16 : (g + 1) * 16].reshape(256, 128)).astype(BF16)
        for q in range(4):
            right[g * 64 : (g + 1) * 64, q * 128 : (q + 1) * 128] = part[q * 64 : (q + 1) * 64]

    lane = iota((128, 128), 1)
    low, even = lane < 64, (lane // 32) % 2 == 0
    scale = 1.0 / 256.0
    for e in range(4):
        products = [
            dot(left[:, (4 * e + k) * 128 : (4 * e + k + 1) * 128], right[...], 0, 0) * scale
            for k in range(4)
        ]
        for jq in range(4):
            v0, v1, v2, v3 = [p[:, jq * 128 : (jq + 1) * 128] for p in products]
            t0 = jnp.where(low, v0, pltpu.roll(v2, 64, 1))
            t2 = jnp.where(low, pltpu.roll(v0, 64, 1), v2)
            t1 = jnp.where(low, v1, pltpu.roll(v3, 64, 1))
            t3 = jnp.where(low, pltpu.roll(v1, 64, 1), v3)
            a = [
                jnp.where(even, t0, pltpu.roll(t1, 32, 1)),
                jnp.where(even, pltpu.roll(t0, 96, 1), t1),
                jnp.where(even, t2, pltpu.roll(t3, 32, 1)),
                jnp.where(even, pltpu.roll(t2, 96, 1), t3),
            ]
            for j in range(4):
                block = a[j].astype(BF16)
                at = (jq * 4 + j) * 64
                joined[at : at + 64, e * 128 : (e + 1) * 128] = block[:64]
                joined[at : at + 64, (4 + e) * 128 : (5 + e) * 128] = block[64:]
    for j in range(16):
        update[:, j, :] = dot(joined[j * 64 : (j + 1) * 64], weight_ref[...])
    own = pl.multiple_of(half_ref[0] * 8, 8)
    update[:, pl.ds(own, 8), :] += pair_ref[...].astype(F32) + bias_ref[...].reshape(1, 1, 128)
    out_ref[:, 0:16, :] = update[...].astype(BF16)
    out_ref[:, 16:32, :] = jnp.broadcast_to(slot_ref[...][None], (64, 16, 128))


def attend_kernel(got_ref, gain_ref, wq_ref, wk_ref, wv_ref, wg_ref, wo_ref, out_ref, q_s, k_s, v_s, mid_s, gate_s):
    both = got_ref[:, 0:16, :].astype(F32).reshape(32, 2, 16, 128)
    pair_mid = (both[:, 0] + both[:, 1]).reshape(512, 128).astype(BF16).astype(F32)
    mid_s[...] = pair_mid
    normed = layer_normalize(pair_mid, gain_ref[...]).astype(BF16)
    q_s[...] = dot(normed, wq_ref[...]).astype(BF16)
    k_s[...] = dot(normed, wk_ref[...]).astype(BF16)
    v_s[...] = dot(normed, wv_ref[...]).astype(BF16)
    gate_s[...] = dot(normed, wg_ref[...])
    factor = 32 ** (-0.5) * math.log2(math.e)
    head_of = iota((512, 128), 1) // 32
    keys, values = k_s[...], v_s[...]
    zero, one = jnp.zeros((512, 128), BF16), jnp.ones((512, 128), BF16)
    head_keys = [jnp.where(head_of == h, keys, zero) for h in range(PAIR_HEADS)]
    head_values = [
        jnp.concatenate(
            [jnp.where(head_of == h, values, zero), jnp.where(head_of == h, one, zero)], 1
        )
        for h in range(PAIR_HEADS)
    ]
    for c in range(4):
        at = slice(c * 128, (c + 1) * 128)
        queries = q_s[at, :]
        total = jnp.zeros((128, 256), F32)
        for h in range(PAIR_HEADS):
            scores = dot(queries, head_keys[h], 1, 1)
            top = jnp.max(scores, -1, keepdims=True)
            weights = jnp.exp2((scores - top) * factor).astype(BF16)
            total = total + dot(weights, head_values[h])
        attended = total[:, :128] / total[:, 128:] * jax.nn.sigmoid(gate_s[at, :])
        result = mid_s[at, :] + dot(attended.astype(BF16), wo_ref[...])
        out_ref[c * 16 : (c + 1) * 16] = result.astype(BF16).reshape(16, 8, 128)


def node_kernel(
    count_ref, got_ref, index_ref, query_ref, nodes_ref, coords_ref, wo_ref, penalty_ref, step_ref, nodes_out, coords_out
):
    table = got_ref[:, 16:32, :].reshape(64, 2, 8, 128)
    kv_table = table[:, 0].reshape(512, 128)
    place_table = table[:, 1].reshape(512, 128)
    local, slots = index_ref.shape
    width, dim = nodes_ref.shape[1], nodes_ref.shape[1] // NODE_HEADS
    lane = iota((1, slots), 1)
    spot = iota((1, local), 1)
    mixed = jnp.zeros((width, local), F32)
    moved = jnp.zeros((3, local), F32)
    for i in range(local):
        picked = one_where(iota((512, slots), 0) == index_ref[i : i + 1, :])
        near = dot(kv_table, picked, 0, 0)
        where = dot(place_table, picked, 0, 0)
        position = [
            where[3 * c : 3 * c + 1] + where[3 * c + 1 : 3 * c + 2] + where[3 * c + 2 : 3 * c + 3]
            for c in range(3)
        ]
        offsets = jnp.concatenate(position, 0) - coords_ref[:, i : i + 1]
        dist2 = jnp.sum(offsets * offsets, 0, keepdims=True)
        products = near[:width] * query_ref[:, i : i + 1]
        logits = jnp.sum(products.reshape(NODE_HEADS, dim, slots), 1) * dim ** (-0.5)
        logits = logits - penalty_ref[...] * dist2
        valid = lane < count_ref[i]
        logits = jnp.where(valid, logits, -1e30)
        powers = jnp.exp(logits - jnp.max(logits, -1, keepdims=True))
        weight = powers / jnp.sum(powers, -1, keepdims=True)
        weight = jnp.where(valid, weight, 0.0)
        low = weight.astype(BF16).astype(F32)
        spread = jnp.broadcast_to(low[:, None, :], (NODE_HEADS, dim, slots)).reshape(width, slots)
        column = jnp.sum(near[width:] * spread, -1, keepdims=True)
        mixed = mixed + jnp.where(spot == i, column, 0.0)
        pull = jnp.sum(weight * step_ref[...], 0, keepdims=True)
        moved = moved + jnp.where(spot == i, jnp.sum(offsets * pull, -1, keepdims=True), 0.0)
    out = nodes_ref[...].astype(F32) + dot(mixed.astype(BF16), wo_ref[...], 0, 0)
    nodes_out[...] = out.astype(BF16)
    coords_out[...] = coords_ref[...] + moved


def call(body, out_shape, args, scratch=(), scalars=0, cost=None):
    spaces = [pltpu.SMEM] * scalars + [pltpu.VMEM] * (len(args) - scalars)
    out_specs = jax.tree.map(lambda _: pl.BlockSpec(memory_space=pltpu.VMEM), out_shape)
    return pl.pallas_call(
        body,
        out_shape=out_shape,
        in_specs=[pl.BlockSpec(memory_space=s) for s in spaces],
        out_specs=out_specs,
        scratch_shapes=list(scratch),
        compiler_params=pltpu.CompilerParams(vmem_limit_bytes=VMEM_LIMIT),
        cost_estimate=cost,
    )(*args)


def shape(dims, kind=BF16):
    return jax.ShapeDtypeStruct(dims, kind)


def on_device(
    homolog_activations,
    alignment_token_ids,
    symbol_lookup_matrix,
    homolog_rescale_vector,
    first_operand_projection,
    second_operand_projection,
    outer_output_weight,
    outer_bias,
    pair,
    pair_norm_gain,
    pair_query_weight,
    pair_key_weight,
    pair_value_weight,
    pair_gate_weight,
    pair_output_weight,
    nodes,
    coords,
    neighbour_index,
    neighbour_count,
    node_norm_gain,
    node_query_weight,
    node_key_weight,
    node_value_weight,
    node_output_weight,
    distance_penalty,
    coordinate_step,
):
    left, right = call(
        msa_kernel,
        (shape((32, 64, 128)), shape((32, 16, 128))),
        (
            homolog_activations,
            alignment_token_ids,
            symbol_lookup_matrix,
            homolog_rescale_vector.reshape(1, -1),
            first_operand_projection,
            second_operand_projection,
        ),
    )
    right = lax.all_to_all(right, PLANE, split_axis=0, concat_axis=0, tiled=True)
    left, right = lax.optimization_barrier((left, right))
    across = [(a * 8 + r, r * 8 + a) for a in range(8) for r in range(8)]
    right = lax.ppermute(right, ("x", "core", "row"), across)
    left = lax.all_to_all(left, PLANE, split_axis=0, concat_axis=0, tiled=True)
    slot, node_query = call(
        node_project_kernel,
        (shape((16, 128)), shape((64, 8), F32)),
        (
            nodes,
            coords,
            node_norm_gain.reshape(1, -1),
            node_query_weight,
            node_key_weight,
            node_value_weight,
        ),
    )
    partial_rows = call(
        outer_kernel,
        shape((64, 32, 128)),
        (
            lax.axis_index("zh").reshape(1).astype(jnp.int32),
            left,
            right,
            pair,
            outer_output_weight,
            outer_bias.reshape(1, -1),
            slot,
        ),
        scratch=(
            pltpu.VMEM((128, 2048), BF16),
            pltpu.VMEM((128, 512), BF16),
            pltpu.VMEM((1024, 1024), BF16),
            pltpu.VMEM((64, 16, 128), F32),
        ),
        scalars=1,
    )
    got = lax.all_to_all(partial_rows, GROUP, split_axis=0, concat_axis=0, tiled=True)
    row = call(
        attend_kernel,
        shape((64, 8, 128)),
        (
            got,
            pair_norm_gain.reshape(1, -1),
            pair_query_weight,
            pair_key_weight,
            pair_value_weight,
            pair_gate_weight,
            pair_output_weight,
        ),
        scratch=(
            pltpu.VMEM((512, 128), BF16),
            pltpu.VMEM((512, 128), BF16),
            pltpu.VMEM((512, 128), BF16),
            pltpu.VMEM((512, 128), F32),
            pltpu.VMEM((512, 128), F32),
        ),
    )
    pair_out = lax.all_to_all(row, GROUP, split_axis=0, concat_axis=0, tiled=True)
    nodes_out, coords_out = call(
        node_kernel,
        (shape(nodes.shape), shape(coords.shape, F32)),
        (
            neighbour_count,
            got,
            neighbour_index,
            node_query,
            nodes,
            coords,
            node_output_weight,
            distance_penalty.reshape(-1, 1),
            coordinate_step.reshape(-1, 1),
        ),
        scalars=1,
    )
    return (pair_out, nodes_out, coords_out)


def solution(mesh):
    fine = Mesh(mesh.devices.reshape(4, 2, 8, 4, 2), ("x", "core", "row", "y", "zh"))
    placed = (
        P(GROUP, "row", None),
        P(GROUP, "row"),
        P(),
        P(),
        P(),
        P(),
        P(),
        P(),
        P("row", GROUP, None),
        P(),
        P(),
        P(),
        P(),
        P(),
        P(),
        P(GROUP, None),
        P(None, GROUP),
        P(GROUP, None),
        P(GROUP),
        P(),
        P(),
        P(),
        P(),
        P(),
        P(),
        P(),
    )
    return jax.shard_map(
        on_device,
        mesh=fine,
        in_specs=placed,
        out_specs=(
            P("row", GROUP, None),
            P(GROUP, None),
            P(None, GROUP),
        ),
        check_vma=False,
    )
```

time: 686 us -> 132 us (0.19)
  the two profiles are of different devices: /device:TPU:1 before, /device:TPU:33 now
where the time goes in v1:
time: 132 us
  blocking collectives  80.8 us (61%)
  waiting for transfers between devices  22.8 us (17%)
  Pallas kernels  11.1 us (8%)
  starting transfers between devices  9.67 us (7%)
  local copies, waits for them, and re-layouts  6.51 us (5%)
    all_to_all x1, blocking collectives, on_device(): lax.all_to_all(partial_rows, GROUP, split_axis=0, concat_axis=0, tiled=True)  65.7 us
    all_to_all x1, blocking collectives, on_device(): lax.all_to_all(right, PLANE, split_axis=0, concat_axis=0, tiled=True)  15.1 us
    all_to_all x1, waiting for transfers between devices, on_device(): lax.all_to_all(row, GROUP, split_axis=0, concat_axis=0, tiled=True)  13.5 us
    pallas_call x5, Pallas kernels, call(): pl.pallas_call(body, out_shape=out_shape, in_specs=[pl.BlockSpec(memory_s...  11.1 us
    all_to_all x1, waiting for transfers between devices, on_device(): left = lax.all_to_all(left, PLANE, split_axis=0, concat_axis=0, tiled=True)  9.32 us
    unnamed x52, local copies, waits for them, and re-layouts  6.33 us
    all_to_all x1, starting transfers between devices, on_device(): lax.all_to_all(row, GROUP, split_axis=0, concat_axis=0, tiled=True)  4.81 us
    all_to_all x1, starting transfers between devices, on_device(): left = lax.all_to_all(left, PLANE, split_axis=0, concat_axis=0, tiled=True)  4.19 us
  transfers between devices with their start and end apart: 3, of which 2 were waited for; matrix products, arithmetic and copies ran while one was open for 0% of the time, Pallas kernels for 2%

profile of v1, /device:TPU:33, one launch (start us, length us, event | category | flops | bytes accessed | tf_op | source)
XLA Modules:
  0.0 131.8 jit_solution(1582261436105282415)
XLA Ops:
  0.7 0.8 copy.29.emb_ref
  1.5 0.1 copy.30.wl_ref
  1.6 0.8 copy.31.wr_ref
  2.4 0.6 copy-done.16
  3.1 1.5 %shard_map.265 = (bf16[32,64,128]{2,1,0:T(8,128)(2,1)}, bf16[32,16,128]{2,1,0:T(8,128)(2,1)S(1)}) custom-call(bf16[4,64,64]{2,1,0:T(8,128)(2,1)S(1)} %copy-done.2, s32[4,64]{1,0:T(4,128)S(1)} %copy-done.15, bf16[80,64]{1,0:T(8,128)(2,1)S(1)} %copy.29.emb_ref, f32[1,64]{1,0:T(1,128)S(1)} %bitcast.7, bf16[64,32]{1,0:T(8,128)(2,1)S(1)} %copy.30.wl_ref, ...), custom_call_target="tpu_custom_call" | custom-call | tf_op jit(solution)/shard_map/pallas_call | solution.py:221
  4.5 15.1 %all_to_all.20 = bf16[32,16,128]{2,1,0:T(8,128)(2,1)S(1)} all-to-all(bf16[32,16,128]{2,1,0:T(8,128)(2,1)S(1)} %get-tuple-element.12), channel_id=1, replica_groups=mesh['x'=4,'core'=2,'row'=8,'y'=4,'zh'=2] {'x','core','y'}, dimensions={0} | all-to-all | bytes 262144 | tf_op jit(solution)/shard_map/all_to_all | solution.py:276
  19.7 0.0 copy-start.1
  19.7 4.2 %all-to-all-start.1 = ((bf16[32,64,128]{2,1,0:T(8,128)(2,1)}), bf16[32,64,128]{2,1,0:T(8,128)(2,1)S(1)}, u32[]{:S(2)}, u32[]{:S(2)}) async-start(bf16[32,64,128]{2,1,0:T(8,128)(2,1)} %get-tuple-element.13), calls=%async_computation.1 | async-start | bytes 1048576 | tf_op jit(solution)/shard_map/all_to_all | solution.py:280
  23.9 0.7 collective-permute-start
  24.6 0.0 copy-start.13
  24.6 0.0 copy-start.12
  24.6 0.6 copy-done.13
  25.2 0.0 copy-done.12
  25.3 0.4 shard_map.266
  25.7 9.3 %all-to-all-done.1.left_in = bf16[32,64,128]{2,1,0:T(8,128)(2,1)S(1)} async-done(((bf16[32,64,128]{2,1,0:T(8,128)(2,1)}), bf16[32,64,128]{2,1,0:T(8,128)(2,1)S(1)}, u32[]{:S(2)}, u32[]{:S(2)}) %all-to-all-start.1) | async-done | bytes 524320 | tf_op jit(solution)/shard_map/all_to_all | solution.py:280
  35.0 0.6 copy-done.18
  35.7 2.8 %shard_map.267 = bf16[64,32,128]{2,1,0:T(8,128)(2,1)S(1)} custom-call(s32[1]{0:T(128)} %bitcast.half_ref, bf16[32,64,128]{2,1,0:T(8,128)(2,1)S(1)} %all-to-all-done.1.left_in, bf16[32,16,128]{2,1,0:T(8,128)(2,1)S(1)} %collective-permute-done.right_in, bf16[64,8,128]{2,1,0:T(8,128)(2,1)S(1)} %copy-done.1, bf16[1024,128]{1,0:T(8,128)(2,1)S(1)} %copy-done, ...), custom_call_target="tpu_custom_call" | custom-call | tf_op jit(solution)/shard_map/pallas_call | solution.py:221
  38.5 0.0 copy-start.3
  38.5 0.0 copy-start.6
  38.5 0.0 copy-start.7
  38.5 65.7 %all_to_all.21.got_ref = bf16[64,32,128]{2,1,0:T(8,128)(2,1)S(1)} all-to-all(bf16[64,32,128]{2,1,0:T(8,128)(2,1)S(1)} %shard_map.267), channel_id=1, replica_groups=mesh['x'=4,'core'=2,'row'=8,'y'=4,'zh'=2] {'x','core','y','zh'}, dimensions={0} | all-to-all | bytes 1048576 | tf_op jit(solution)/shard_map/all_to_all | solution.py:313
  104.3 0.6 copy-done.19
  104.9 4.0 %shard_map.268 = bf16[64,8,128]{2,1,0:T(8,128)(2,1)} custom-call(bf16[64,32,128]{2,1,0:T(8,128)(2,1)S(1)} %all_to_all.21.got_ref, f32[1,128]{1,0:T(1,128)S(1)} %bitcast.10, bf16[128,128]{1,0:T(8,128)(2,1)S(1)} %copy-done.3, bf16[128,128]{1,0:T(8,128)(2,1)S(1)} %copy-done.4, bf16[128,128]{1,0:T(8,128)(2,1)S(1)} %copy-done.5, bf16[128,128]{1,0:T(8,128)(2,1)S(1)} %copy-done.6, ...), custom_call_target="tpu_custom_call" | custom-call | tf_op jit(solution)/shard_map/pallas_call | solution.py:221
  108.9 4.8 %all-to-all-start.3 = ((bf16[64,8,128]{2,1,0:T(8,128)(2,1)}), bf16[64,8,128]{2,1,0:T(8,128)(2,1)S(1)}, u32[]{:S(2)}, u32[]{:S(2)}) async-start(bf16[64,8,128]{2,1,0:T(8,128)(2,1)} %shard_map.268), calls=%async_computation.3 | async-start | bytes 262144 | tf_op jit(solution)/shard_map/all_to_all | solution.py:334
  113.8 0.6 copy-done.22
  114.4 0.1 copy.32.penalty_ref
  114.5 0.1 copy.33.step_ref
  114.6 0.5 copy-done.14
  115.1 0.2 copy-done.20
  115.3 2.4 %shard_map.269 = (bf16[8,64]{1,0:T(8,128)(2,1)}, f32[3,8]{1,0:T(4,128)}) custom-call(s32[8]{0:T(128)S(1)} %copy-done.20, bf16[64,32,128]{2,1,0:T(8,128)(2,1)S(1)} %all_to_all.21.got_ref, s32[8,64]{1,0:T(8,128)S(1)} %copy-done.14, f32[64,8]{1,0:T(8,128)S(1)} %get-tuple-element.16.query_ref, bf16[8,64]{1,0:T(8,128)(2,1)S(1)} %copy-done.12, ...), custom_call_target="tpu_custom_call" | custom-call | tf_op jit(solution)/shard_map/pallas_call | solution.py:221
  117.6 13.5 %all-to-all-done.3 = bf16[64,8,128]{2,1,0:T(8,128)(2,1)S(1)} async-done(((bf16[64,8,128]{2,1,0:T(8,128)(2,1)}), bf16[64,8,128]{2,1,0:T(8,128)(2,1)S(1)}, u32[]{:S(2)}, u32[]{:S(2)}) %all-to-all-start.3) | async-done | bytes 131104 | tf_op jit(solution)/shard_map/all_to_all | solution.py:334
  131.1 0.7 copy.35
  (35 shorter events, 0.1 us)
Async XLA Ops:
  0.6 0.9 copy-start.21
  0.6 1.8 %copy-start.2 = (bf16[4,64,64]{2,1,0:T(8,128)(2,1)S(1)}, bf16[4,64,64]{2,1,0:T(8,128)(2,1)}, u32[]{:S(2)}) copy-start(bf16[4,64,64]{2,1,0:T(8,128)(2,1)} %act_ref.1) | copy-start | bytes 98308
  1.6 0.8 copy-start.15
  2.4 0.7 copy-start.16
  19.7 4.9 %copy-start.9 = (bf16[64,64]{1,0:T(8,128)(2,1)S(1)}, bf16[64,64]{1,0:T(8,128)(2,1)}, u32[]{:S(2)}) copy-start(bf16[64,64]{1,0:T(8,128)(2,1)} %wq_ref.2) | copy-start | bytes 24580
  19.7 5.0 %copy-start.10 = (bf16[64,64]{1,0:T(8,128)(2,1)S(1)}, bf16[64,64]{1,0:T(8,128)(2,1)}, u32[]{:S(2)}) copy-start(bf16[64,64]{1,0:T(8,128)(2,1)} %wk_ref.2) | copy-start | bytes 24580
  19.7 5.0 %copy-start.11 = (bf16[64,64]{1,0:T(8,128)(2,1)S(1)}, bf16[64,64]{1,0:T(8,128)(2,1)}, u32[]{:S(2)}) copy-start(bf16[64,64]{1,0:T(8,128)(2,1)} %wv_ref.2) | copy-start | bytes 24580
  19.7 15.3 %copy-start = (bf16[1024,128]{1,0:T(8,128)(2,1)S(1)}, bf16[1024,128]{1,0:T(8,128)(2,1)}, u32[]{:S(2)}) copy-start(bf16[1024,128]{1,0:T(8,128)(2,1)} %weight_ref.1) | copy-start | bytes 786436
  19.7 15.3 %copy-start.1 = (bf16[64,8,128]{2,1,0:T(8,128)(2,1)S(1)}, bf16[64,8,128]{2,1,0:T(8,128)(2,1)}, u32[]{:S(2)}) copy-start(bf16[64,8,128]{2,1,0:T(8,128)(2,1)} %pair_ref.1) | copy-start | bytes 393220
  19.7 15.3 %all-to-all-start.1 = ((bf16[32,64,128]{2,1,0:T(8,128)(2,1)}), bf16[32,64,128]{2,1,0:T(8,128)(2,1)S(1)}, u32[]{:S(2)}, u32[]{:S(2)}) async-start(bf16[32,64,128]{2,1,0:T(8,128)(2,1)} %get-tuple-element.13), calls=%async_computation.1 | async-start | bytes 1048576 | tf_op jit(solution)/shard_map/all_to_all | solution.py:280
  23.9 1.8 %collective-permute-start = (bf16[32,16,128]{2,1,0:T(8,128)(2,1)S(1)}, bf16[32,16,128]{2,1,0:T(8,128)(2,1)S(1)}, u32[]{:S(2)}, u32[]{:S(2)}) collective-permute-start(bf16[32,16,128]{2,1,0:T(8,128)(2,1)S(1)} %all_to_all.20), channel_id=1, source_target_pairs={{0,0},{8,64},{16,128},{24,192},{32,256},{40,320},{48,384},{56,448}... | collective-permute-start | bytes 393224 | tf_op jit(solution)/shard_map/ppermute | solution.py:279
  24.6 0.7 copy-start.13
  24.6 0.7 copy-start.12
  24.6 0.7 copy-start.17
  35.0 0.7 copy-start.18
  38.5 65.8 %copy-start.3 = (bf16[128,128]{1,0:T(8,128)(2,1)S(1)}, bf16[128,128]{1,0:T(8,128)(2,1)}, u32[]{:S(2)}) copy-start(bf16[128,128]{1,0:T(8,128)(2,1)} %wq_ref.3) | copy-start | bytes 98308
  38.5 65.8 %copy-start.4 = (bf16[128,128]{1,0:T(8,128)(2,1)S(1)}, bf16[128,128]{1,0:T(8,128)(2,1)}, u32[]{:S(2)}) copy-start(bf16[128,128]{1,0:T(8,128)(2,1)} %wk_ref.3) | copy-start | bytes 98308
  38.5 65.7 %copy-start.5 = (bf16[128,128]{1,0:T(8,128)(2,1)S(1)}, bf16[128,128]{1,0:T(8,128)(2,1)}, u32[]{:S(2)}) copy-start(bf16[128,128]{1,0:T(8,128)(2,1)} %wv_ref.3) | copy-start | bytes 98308
  38.5 65.7 %copy-start.6 = (bf16[128,128]{1,0:T(8,128)(2,1)S(1)}, bf16[128,128]{1,0:T(8,128)(2,1)}, u32[]{:S(2)}) copy-start(bf16[128,128]{1,0:T(8,128)(2,1)} %wg_ref.1) | copy-start | bytes 98308
  38.5 65.7 %copy-start.7 = (bf16[128,128]{1,0:T(8,128)(2,1)S(1)}, bf16[128,128]{1,0:T(8,128)(2,1)}, u32[]{:S(2)}) copy-start(bf16[128,128]{1,0:T(8,128)(2,1)} %wo_ref.2) | copy-start | bytes 98308
  104.2 0.7 copy-start.19
  108.9 5.6 %copy-start.23 = (f32[4]{0:T(128)S(1)}, f32[4]{0:T(128)}, u32[]{:S(2)}) copy-start(f32[4]{0:T(128)} %param.51) | copy-start | bytes 52
  108.9 5.7 %copy-start.8 = (bf16[64,64]{1,0:T(8,128)(2,1)S(1)}, bf16[64,64]{1,0:T(8,128)(2,1)}, u32[]{:S(2)}) copy-start(bf16[64,64]{1,0:T(8,128)(2,1)} %wo_ref.3) | copy-start | bytes 24580
  108.9 22.2 %all-to-all-start.3 = ((bf16[64,8,128]{2,1,0:T(8,128)(2,1)}), bf16[64,8,128]{2,1,0:T(8,128)(2,1)S(1)}, u32[]{:S(2)}, u32[]{:S(2)}) async-start(bf16[64,8,128]{2,1,0:T(8,128)(2,1)} %shard_map.268), calls=%async_computation.3 | async-start | bytes 262144 | tf_op jit(solution)/shard_map/all_to_all | solution.py:334
  113.7 0.7 copy-start.22
  114.4 0.7 copy-start.14
  114.6 0.7 copy-start.20

commit v2 on v1

--- a/solution.py
+++ b/solution.py
@@ -35,8 +35,41 @@
     return centred * lax.rsqrt(variance + 1e-05) * gain
 
 
-def msa_kernel(
-    act_ref, tok_ref, emb_ref, gain_ref, wl_ref, wr_ref, left_ref, right_ref
+def swap_lane_groups(v, low, even):
+    t0 = jnp.where(low, v[0], pltpu.roll(v[2], 64, 1))
+    t2 = jnp.where(low, pltpu.roll(v[0], 64, 1), v[2])
+    t1 = jnp.where(low, v[1], pltpu.roll(v[3], 64, 1))
+    t3 = jnp.where(low, pltpu.roll(v[1], 64, 1), v[3])
+    return (
+        jnp.where(even, t0, pltpu.roll(t1, 32, 1)),
+        jnp.where(even, pltpu.roll(t0, 96, 1), t1),
+        jnp.where(even, t2, pltpu.roll(t3, 32, 1)),
+        jnp.where(even, pltpu.roll(t2, 96, 1), t3),
+    )
+
+
+def lane_masks(rows):
+    lane = iota((rows, 128), 1)
+    return lane < 64, (lane // 32) % 2 == 0
+
+
+def first_kernel(
+    half_ref,
+    act_ref,
+    tok_ref,
+    emb_ref,
+    gain_ref,
+    pair_ref,
+    nodes_ref,
+    coords_ref,
+    node_gain_ref,
+    wq_ref,
+    wk_ref,
+    wv_ref,
+    swap_ref,
+    normed_ref,
+    slot_ref,
+    query_ref,
 ):
     seqs, length, _ = act_ref.shape
     kinds = emb_ref.shape[0]
@@ -46,38 +79,16 @@
         picked = one_where(iota((kinds, length), 0) == tok_ref[s : s + 1, :])
         rows.append(act_ref[s].astype(F32) + dot(picked, emb, 0, 0))
     normed = layer_normalize(jnp.concatenate(rows, 0), gain_ref[...]).astype(BF16)
-
-    left = dot(wl_ref[...], normed, 0, 1).astype(BF16).astype(F32)
-    low = iota((16, 128), 1) < 64
-    parts = []
-    for p in range(2):
-        a0 = left[0:16, p * 128 : (p + 1) * 128]
-        a1 = left[16:32, p * 128 : (p + 1) * 128]
-        parts.append(jnp.where(low, a0, pltpu.roll(a1, 64, 1)))
-        parts.append(jnp.where(low, pltpu.roll(a0, 64, 1), a1))
-    block = jnp.concatenate(parts, 0).astype(BF16)
-    left_ref[...] = jnp.broadcast_to(block[None], left_ref.shape)
-
-    out_row, source = iota((256, 256), 0), iota((256, 256), 1)
-    wanted = (out_row % 4) * 64 + ((out_row % 64) // 4) * 4 + out_row // 64
-    moved = dot(one_where(source == wanted), normed).astype(BF16)
-    right = jnp.zeros((64, 128), F32)
-    for j in range(4):
-        place = one_where(iota((32, 128), 1) == iota((32, 128), 0) + 32 * j)
-        widened = dot(wr_ref[...], place).astype(BF16)
-        right = right + dot(moved[j * 64 : (j + 1) * 64], widened)
-    right = right.astype(BF16).reshape(4, 16, 128)
-    for a in range(8):
-        right_ref[a * 4 : (a + 1) * 4] = right
-
-
-def node_project_kernel(nodes_ref, coords_ref, gain_ref, wq_ref, wk_ref, wv_ref, slot_ref, query_ref):
-    normed = layer_normalize(nodes_ref[...].astype(F32), gain_ref[...]).astype(BF16)
+    normed_ref[...] = normed
+    row, lane = iota((64, 128), 0), iota((64, 128), 1)
+    packed = dot(normed[:128], one_where(lane == row)) + dot(normed[128:], one_where(lane == row + 64))
+    swap_ref[0:128] = packed.astype(BF16)
+    swap_ref[128:384] = pair_ref[:, 1 - half_ref[0]].reshape(256, 128)
+
+    normed = layer_normalize(nodes_ref[...].astype(F32), node_gain_ref[...]).astype(BF16)
     query_ref[...] = dot(wq_ref[...], normed, 0, 1).astype(BF16).astype(F32)
-    width = wk_ref.shape[1]
-    row, lane = iota((width, 128), 0), iota((width, 128), 1)
     kv = dot(normed, dot(wk_ref[...], one_where(lane == row)).astype(BF16))
-    kv = kv + dot(normed, dot(wv_ref[...], one_where(lane == row + width)).astype(BF16))
+    kv = kv + dot(normed, dot(wv_ref[...], one_where(lane == row + 64)).astype(BF16))
     rest = coords_ref[...]
     placed = jnp.zeros((8, 128), F32)
     for part in range(3):
@@ -85,64 +96,121 @@
         rest = rest - piece.astype(F32)
         spot = one_where(iota((3, 128), 1) == iota((3, 128), 0) * 3 + part)
         placed = placed + dot(piece, spot, 0, 0)
-    slot_ref[...] = jnp.concatenate([kv, placed], 0).astype(BF16)
-
-
-def outer_kernel(
-    half_ref, left_in, right_in, pair_ref, weight_ref, bias_ref, slot_ref, out_ref, left, right, joined, update
+    slot = jnp.concatenate([kv, placed], 0).astype(BF16)
+    slot_ref[...] = slot
+    swap_ref[384:400] = slot
+
+
+def spread_kernel(half_ref, normed_ref, slot_ref, pair_ref, got_ref, wl_ref, wr_ref, out_ref):
+    half = half_ref[0]
+    mine = half == 0
+    row, lane = iota((128, 64), 0), iota((128, 64), 1)
+    packed = got_ref[0:128]
+    theirs = jnp.concatenate(
+        [dot(packed, one_where(row == lane)), dot(packed, one_where(row == lane + 64))], 0
+    )
+    own = normed_ref[...].astype(F32)
+    planes = [
+        jnp.where(mine, own, theirs).astype(BF16),
+        jnp.where(mine, theirs, own).astype(BF16),
+    ]
+
+    row, source = iota((128, 256), 0), iota((128, 256), 1)
+    pick = one_where(source == (row // 32) * 64 + (row % 32) * 2 + half)
+    low, even = lane_masks(8)
+    parts = []
+    for p in range(2):
+        rows = dot(pick, planes[p]).astype(BF16)
+        left = dot(wl_ref[...], rows, 0, 1).astype(BF16).astype(F32)
+        parts += swap_lane_groups([left[k * 8 : (k + 1) * 8] for k in range(4)], low, even)
+    block = jnp.concatenate(parts, 0).astype(BF16)
+    out_ref[:, 0:64] = jnp.broadcast_to(block[None], (32, 64, 128))
+
+    first = iota((32, 16, 128), 1) // 8 == half
+    kept = pair_ref[:, half].astype(F32)
+    came = got_ref[128:384].reshape(32, 8, 128).astype(F32)
+    kept = jnp.concatenate([kept, kept], 1)
+    came = jnp.concatenate([came, came], 1)
+    out_ref[:, 64:80] = jnp.where(first, kept, came).astype(BF16)
+
+    own, theirs = slot_ref[...].astype(F32), got_ref[384:400].astype(F32)
+    one = jnp.where(mine, own, theirs)
+    two = jnp.where(mine, theirs, own)
+    kv = jnp.concatenate([one[:8], two[:8]], 0).astype(BF16)
+    out_ref[:, 80:96] = jnp.broadcast_to(kv[None], (32, 16, 128))
+
+    place = jnp.concatenate([one[8:], two[8:]], 0)
+    widened = dot(wr_ref[...], one_where(iota((32, 128), 1) == iota((32, 128), 0) + 32)).astype(BF16)
+    both = jnp.concatenate(planes, 0)
+    for g in range(4):
+        row, source = iota((128, 512), 0) + g * 128, iota((128, 512), 1)
+        wanted = ((row // 8) % 2) * 256 + ((row // 2) % 4) * 64 + (row // 16) * 2 + row % 2
+        moved = dot(one_where(source == wanted), both).astype(BF16)
+        right = dot(moved, widened).reshape(8, 16, 128) + place[None]
+        out_ref[g * 8 : (g + 1) * 8, 96:112] = right.astype(BF16)
+
+
+def right_kernel(got_ref, out_ref):
+    rows = got_ref[:, 96:112].reshape(512, 128)
+    row, source = iota((128, 512), 0), iota((128, 512), 1)
+    start = (row // 4) * 16 + (row % 4) * 2
+    at, lane = iota((128, 128), 0), iota((128, 128), 1)
+    total = jnp.zeros((128, 128), F32)
+    for plane in range(2):
+        for column in range(2):
+            picked = dot(one_where(source == start + plane * 8 + column), rows).astype(BF16)
+            shift = (plane * 2 + column) * 32
+            keep = (lane >= shift) & (lane < shift + 32)
+            total = total + dot(picked, one_where((at + shift == lane + 32) & keep))
+    out_ref[...] = jnp.broadcast_to(total.astype(BF16)[None], out_ref.shape)
+
+
+def outer_kernel(got_ref, right_in, weight_ref, out_ref, left, right, joined, weight, update):
+    row = iota((256, 256), 0)
+    wanted = ((row // 4) % 4) * 64 + ((row // 16) % 2) * 32 + (row % 4) * 8 + row // 32
+    turn = one_where(iota((256, 256), 1) == wanted)
+    for g in range(8):
+        part = dot(turn, got_ref[g * 4 : (g + 1) * 4, 0:64].reshape(256, 128)).astype(BF16)
+        for q in range(8):
+            for p in range(2):
+                at = p * 128 + g * 16
+                left[at : at + 16, q * 128 : (q + 1) * 128] = part[q * 32 + p * 16 : q * 32 + p * 16 + 16]
+    low, even = lane_masks(128)
+    for t in range(4):
+        a, b = right_in[2 * t].astype(F32), right_in[2 * t + 1].astype(F32)
+        right[0:128, t * 128 : (t + 1) * 128] = jnp.where(low, a, pltpu.roll(b, 64, 1)).astype(BF16)
+        right[128:256, t * 128 : (t + 1) * 128] = jnp.where(low, pltpu.roll(a, 64, 1), b).astype(BF16)
+    for q in range(8):
+        for k in range(4):
+            at = (k * 8 + q) * 32
+            weight[q * 128 + k * 32 : q * 128 + k * 32 + 32] = weight_ref[at : at + 32]
+
+    low, even = lane_masks(32)
+    scale = 1.0 / 256.0
+    for q in range(8):
+        product = dot(left[:, q * 128 : (q + 1) * 128], right[...], 0, 0) * scale
+        for t in range(4):
+            tile = product[:, t * 128 : (t + 1) * 128]
+            blocks = swap_lane_groups([tile[k * 32 : (k + 1) * 32] for k in range(4)], low, even)
+            for j in range(4):
+                at = (t * 4 + j) * 32
+                joined[at : at + 32, q * 128 : (q + 1) * 128] = blocks[j].astype(BF16)
+    for j in range(0, 16, 4):
+        rows = dot(joined[j * 32 : (j + 4) * 32], weight[...])
+        for k in range(4):
+            update[:, j + k, :] = rows[k * 32 : (k + 1) * 32]
+    out_ref[...] = update[...].astype(BF16)
+
+
+def attend_kernel(
+    update_ref, got_ref, bias_ref, gain_ref, wq_ref, wk_ref, wv_ref, wg_ref, wo_ref, out_ref, q_s, k_s, v_s, mid_s, gate_s
 ):
-    turn = one_where(
-        iota((256, 256), 1) == (iota((256, 256), 0) % 16) * 16 + iota((256, 256), 0) // 16
-    )
-    for g in range(8):
-        part = dot(turn, left_in[g * 4 : (g + 1) * 4].reshape(256, 128)).astype(BF16)
-        for q in range(16):
-            left[g * 16 : (g + 1) * 16, q * 128 : (q + 1) * 128] = part[q * 16 : (q + 1) * 16]
-    row = iota((256, 256), 0)
-    turn = one_where(
-        iota((256, 256), 1) == ((row % 64) // 4) * 16 + (row // 64) * 4 + row % 4
-    )
-    for g in range(2):
-        part = dot(turn, right_in[g * 16 : (g + 1) * 16].reshape(256, 128)).astype(BF16)
-        for q in range(4):
-            right[g * 64 : (g + 1) * 64, q * 128 : (q + 1) * 128] = part[q * 64 : (q + 1) * 64]
-
-    lane = iota((128, 128), 1)
-    low, even = lane < 64, (lane // 32) % 2 == 0
-    scale = 1.0 / 256.0
-    for e in range(4):
-        products = [
-            dot(left[:, (4 * e + k) * 128 : (4 * e + k + 1) * 128], right[...], 0, 0) * scale
-            for k in range(4)
-        ]
-        for jq in range(4):
-            v0, v1, v2, v3 = [p[:, jq * 128 : (jq + 1) * 128] for p in products]
-            t0 = jnp.where(low, v0, pltpu.roll(v2, 64, 1))
-            t2 = jnp.where(low, pltpu.roll(v0, 64, 1), v2)
-            t1 = jnp.where(low, v1, pltpu.roll(v3, 64, 1))
-            t3 = jnp.where(low, pltpu.roll(v1, 64, 1), v3)
-            a = [
-                jnp.where(even, t0, pltpu.roll(t1, 32, 1)),
-                jnp.where(even, pltpu.roll(t0, 96, 1), t1),
-                jnp.where(even, t2, pltpu.roll(t3, 32, 1)),
-                jnp.where(even, pltpu.roll(t2, 96, 1), t3),
-            ]
-            for j in range(4):
-                block = a[j].astype(BF16)
-                at = (jq * 4 + j) * 64
-                joined[at : at + 64, e * 128 : (e + 1) * 128] = block[:64]
-                joined[at : at + 64, (4 + e) * 128 : (5 + e) * 128] = block[64:]
-    for j in range(16):
-        update[:, j, :] = dot(joined[j * 64 : (j + 1) * 64], weight_ref[...])
-    own = pl.multiple_of(half_ref[0] * 8, 8)
-    update[:, pl.ds(own, 8), :] += pair_ref[...].astype(F32) + bias_ref[...].reshape(1, 1, 128)
-    out_ref[:, 0:16, :] = update[...].astype(BF16)
-    out_ref[:, 16:32, :] = jnp.broadcast_to(slot_ref[...][None], (64, 16, 128))
-
-
-def attend_kernel(got_ref, gain_ref, wq_ref, wk_ref, wv_ref, wg_ref, wo_ref, out_ref, q_s, k_s, v_s, mid_s, gate_s):
-    both = got_ref[:, 0:16, :].astype(F32).reshape(32, 2, 16, 128)
-    pair_mid = (both[:, 0] + both[:, 1]).reshape(512, 128).astype(BF16).astype(F32)
+    row = iota((512, 512), 0)
+    wanted = ((row // 2) % 32) * 16 + (row // 64) * 2 + row % 2
+    turn = one_where(iota((512, 512), 1) == wanted)
+    pair_mid = dot(turn, update_ref[...].reshape(512, 128))
+    pair_mid = pair_mid + got_ref[:, 64:80].reshape(512, 128).astype(F32) + bias_ref[...]
+    pair_mid = pair_mid.astype(BF16).astype(F32)
     mid_s[...] = pair_mid
     normed = layer_normalize(pair_mid, gain_ref[...]).astype(BF16)
     q_s[...] = dot(normed, wq_ref[...]).astype(BF16)
@@ -177,9 +245,8 @@
 def node_kernel(
     count_ref, got_ref, index_ref, query_ref, nodes_ref, coords_ref, wo_ref, penalty_ref, step_ref, nodes_out, coords_out
 ):
-    table = got_ref[:, 16:32, :].reshape(64, 2, 8, 128)
-    kv_table = table[:, 0].reshape(512, 128)
-    place_table = table[:, 1].reshape(512, 128)
+    kv_table = got_ref[:, 80:96].reshape(512, 128)
+    place_table = got_ref[:, 96:112].reshape(512, 128)
     local, slots = index_ref.shape
     width, dim = nodes_ref.shape[1], nodes_ref.shape[1] // NODE_HEADS
     lane = iota((1, slots), 1)
@@ -261,27 +328,18 @@
     distance_penalty,
     coordinate_step,
 ):
-    left, right = call(
-        msa_kernel,
-        (shape((32, 64, 128)), shape((32, 16, 128))),
+    half = lax.axis_index("zh").reshape(1).astype(jnp.int32)
+    by_parity = pair.reshape(32, 2, 8, 128)
+    swap, normed, slot, node_query = call(
+        first_kernel,
+        (shape((400, 128)), shape((256, 64)), shape((16, 128)), shape((64, 8), F32)),
         (
+            half,
             homolog_activations,
             alignment_token_ids,
             symbol_lookup_matrix,
             homolog_rescale_vector.reshape(1, -1),
-            first_operand_projection,
-            second_operand_projection,
-        ),
-    )
-    right = lax.all_to_all(right, PLANE, split_axis=0, concat_axis=0, tiled=True)
-    left, right = lax.optimization_barrier((left, right))
-    across = [(a * 8 + r, r * 8 + a) for a in range(8) for r in range(8)]
-    right = lax.ppermute(right, ("x", "core", "row"), across)
-    left = lax.all_to_all(left, PLANE, split_axis=0, concat_axis=0, tiled=True)
-    slot, node_query = call(
-        node_project_kernel,
-        (shape((16, 128)), shape((64, 8), F32)),
-        (
+            by_parity,
             nodes,
             coords,
             node_norm_gain.reshape(1, -1),
@@ -289,33 +347,46 @@
             node_key_weight,
             node_value_weight,
         ),
-    )
-    partial_rows = call(
+        scalars=1,
+    )
+    swapped = lax.ppermute(swap, "zh", [(0, 1), (1, 0)])
+    spread = call(
+        spread_kernel,
+        shape((32, 112, 128)),
+        (
+            half,
+            normed,
+            slot,
+            by_parity,
+            swapped,
+            first_operand_projection,
+            second_operand_projection,
+        ),
+        scalars=1,
+    )
+    got = lax.all_to_all(spread, PLANE, split_axis=0, concat_axis=0, tiled=True)
+    right = call(right_kernel, shape((8, 128, 128)), (got,))
+    right = lax.all_to_all(right, "row", split_axis=0, concat_axis=0, tiled=True)
+    update = call(
         outer_kernel,
-        shape((64, 32, 128)),
-        (
-            lax.axis_index("zh").reshape(1).astype(jnp.int32),
-            left,
-            right,
-            pair,
-            outer_output_weight,
-            outer_bias.reshape(1, -1),
-            slot,
-        ),
+        shape((32, 16, 128)),
+        (got, right, outer_output_weight),
         scratch=(
-            pltpu.VMEM((128, 2048), BF16),
-            pltpu.VMEM((128, 512), BF16),
-            pltpu.VMEM((1024, 1024), BF16),
-            pltpu.VMEM((64, 16, 128), F32),
-        ),
-        scalars=1,
-    )
-    got = lax.all_to_all(partial_rows, GROUP, split_axis=0, concat_axis=0, tiled=True)
+            pltpu.VMEM((256, 1024), BF16),
+            pltpu.VMEM((256, 512), BF16),
+            pltpu.VMEM((512, 1024), BF16),
+            pltpu.VMEM((1024, 128), BF16),
+            pltpu.VMEM((32, 16, 128), F32),
+        ),
+    )
+    update = lax.all_to_all(update, PLANE, split_axis=0, concat_axis=0, tiled=True)
     row = call(
         attend_kernel,
         shape((64, 8, 128)),
         (
+            update,
             got,
+            outer_bias.reshape(1, -1),
             pair_norm_gain.reshape(1, -1),
             pair_query_weight,
             pair_key_weight,

time: 132 us -> 132 us (level)
  blocking collectives: 80.8 us -> 63.8 us
  starting transfers between devices: 9.67 us -> 26.6 us
  local copies, waits for them, and re-layouts: 6.51 us -> 8.23 us
  waiting for transfers between devices: 22.8 us -> 21.3 us
    all_to_all x2 -> x3, blocking collectives: 80.8 us -> 63.8 us  [the longest x1 25.5 us: on_device(): got = lax.all_to_all(spread, PLANE, split_axis=0, concat_axis=0, tiled=True)]
    ppermute x1, starting transfers between devices: 0.67 us -> 14.7 us  [on_device(): swapped = lax.ppermute(swap, 'zh', [(0, 1), (1, 0)])]
    all_to_all x1 -> x0, waiting for transfers between devices: 9.32 us -> none  [on_device(): left = lax.all_to_all(left, PLANE, split_axis=0, concat_axis=0, tiled=True)]
    all_to_all x1, starting transfers between devices: 4.81 us -> 11.9 us  [on_device(): lax.all_to_all(row, GROUP, split_axis=0, concat_axis=0, tiled=True)]
    ppermute x1, waiting for transfers between devices: 0.01 us -> 4.58 us  [on_device(): swapped = lax.ppermute(swap, 'zh', [(0, 1), (1, 0)])]
    all_to_all x1 -> x0, starting transfers between devices: 4.19 us -> none  [on_device(): left = lax.all_to_all(left, PLANE, split_axis=0, concat_axis=0, tiled=True)]
    all_to_all x1, waiting for transfers between devices: 13.5 us -> 16.7 us  [on_device(): lax.all_to_all(row, GROUP, split_axis=0, concat_axis=0, tiled=True)]
    unnamed x52 -> x60, local copies, waits for them, and re-layouts: 6.33 us -> 8.04 us
  transfers between devices with their start and end apart: 3 -> 2, of which waited for: 2 -> 2; matrix products, arithmetic and copies ran while one was open for 0% -> 0% of each run, Pallas kernels for 2% -> 2%
where the time goes in v2:
time: 132 us
  blocking collectives  63.8 us (48%)
  starting transfers between devices  26.6 us (20%)
  waiting for transfers between devices  21.3 us (16%)
  Pallas kernels  10.8 us (8%)
  local copies, waits for them, and re-layouts  8.23 us (6%)
    all_to_all x1, blocking collectives, on_device(): got = lax.all_to_all(spread, PLANE, split_axis=0, concat_axis=0, tiled=True)  25.5 us
    all_to_all x1, blocking collectives, on_device(): lax.all_to_all(right, 'row', split_axis=0, concat_axis=0, tiled=True)  21.4 us
    all_to_all x1, blocking collectives, on_device(): lax.all_to_all(update, PLANE, split_axis=0, concat_axis=0, tiled=True)  17 us
    all_to_all x1, waiting for transfers between devices, on_device(): lax.all_to_all(row, GROUP, split_axis=0, concat_axis=0, tiled=True)  16.7 us
    ppermute x1, starting transfers between devices, on_device(): swapped = lax.ppermute(swap, 'zh', [(0, 1), (1, 0)])  14.7 us
    all_to_all x1, starting transfers between devices, on_device(): lax.all_to_all(row, GROUP, split_axis=0, concat_axis=0, tiled=True)  11.9 us
    pallas_call x6, Pallas kernels, call(): pl.pallas_call(body, out_shape=out_shape, in_specs=[pl.BlockSpec(memory_s...  10.8 us
    unnamed x60, local copies, waits for them, and re-layouts  8.04 us
  transfers between devices with their start and end apart: 2, of which 2 were waited for; matrix products, arithmetic and copies ran while one was open for 0% of the time, Pallas kernels for 2%

profile of v2, /device:TPU:33, one launch (start us, length us, event | category | flops | bytes accessed | tf_op | source)
XLA Modules:
  0.0 131.6 jit_solution(842775564927756155)
XLA Ops:
  0.7 0.8 copy.29.emb_ref
  1.5 0.6 copy-done.20
  2.2 0.0 copy-done.21
  2.2 0.9 copy-done
  3.1 0.8 copy-done.3
  3.9 0.7 copy-done.13
  4.6 0.7 copy-done.15
  5.3 0.7 copy-done.18
  6.0 0.6 shard_map.265
  6.6 14.7 %collective-permute-start = (bf16[400,128]{1,0:T(8,128)(2,1)S(1)}, bf16[400,128]{1,0:T(8,128)(2,1)S(1)}, u32[]{:S(2)}, u32[]{:S(2)}) collective-permute-start(bf16[400,128]{1,0:T(8,128)(2,1)S(1)} %get-tuple-element.11), channel_id=1, source_target_pairs={{0,1},{1,0},{2,3},{3,2},{4,5},{5,4},{6,7},{7,6},{8,9},{9,8},{10,11... | collective-permute-start | bytes 307208 | tf_op jit(solution)/shard_map/ppermute | solution.py:352
  21.3 0.1 copy.30.wl_ref
  21.4 0.1 copy.31.wr_ref
  21.5 4.6 %collective-permute-done.got_ref = bf16[400,128]{1,0:T(8,128)(2,1)S(1)} collective-permute-done((bf16[400,128]{1,0:T(8,128)(2,1)S(1)}, bf16[400,128]{1,0:T(8,128)(2,1)S(1)}, u32[]{:S(2)}, u32[]{:S(2)}) %collective-permute-start) | collective-permute-done | bytes 102432 | tf_op jit(solution)/shard_map/ppermute | solution.py:352
  26.1 1.1 shard_map.266
  27.2 25.5 %all_to_all.20.got_ref = bf16[32,112,128]{2,1,0:T(8,128)(2,1)S(1)} all-to-all(bf16[32,112,128]{2,1,0:T(8,128)(2,1)S(1)} %shard_map.266), channel_id=1, replica_groups=mesh['x'=4,'core'=2,'row'=8,'y'=4,'zh'=2] {'x','core','y'}, dimensions={0} | all-to-all | bytes 1835008 | tf_op jit(solution)/shard_map/all_to_all | solution.py:367
  52.7 0.5 shard_map.267
  53.2 21.4 %all_to_all.21.right_in = bf16[8,128,128]{2,1,0:T(8,128)(2,1)S(1)} all-to-all(bf16[8,128,128]{2,1,0:T(8,128)(2,1)S(1)} %shard_map.267), channel_id=1, replica_groups=mesh['x'=4,'core'=2,'row'=8,'y'=4,'zh'=2] {'row'}, dimensions={0} | all-to-all | bytes 524288 | tf_op jit(solution)/shard_map/all_to_all | solution.py:369
  74.6 1.8 %shard_map.268 = bf16[32,16,128]{2,1,0:T(8,128)(2,1)S(1)} custom-call(bf16[32,112,128]{2,1,0:T(8,128)(2,1)S(1)} %all_to_all.20.got_ref, bf16[8,128,128]{2,1,0:T(8,128)(2,1)S(1)} %all_to_all.21.right_in, bf16[1024,128]{1,0:T(8,128)(2,1)S(1)} %copy-done.2), custom_call_target="tpu_custom_call" | custom-call | tf_op jit(solution)/shard_map/pallas_call | solution.py:288
  76.5 17.0 %all_to_all.22.update_ref = bf16[32,16,128]{2,1,0:T(8,128)(2,1)S(1)} all-to-all(bf16[32,16,128]{2,1,0:T(8,128)(2,1)S(1)} %shard_map.268), channel_id=1, replica_groups=mesh['x'=4,'core'=2,'row'=8,'y'=4,'zh'=2] {'x','core','y'}, dimensions={0} | all-to-all | bytes 262144 | tf_op jit(solution)/shard_map/all_to_all | solution.py:382
  93.5 0.6 copy-done.22
  94.1 0.0 copy-done.23
  94.1 4.3 %shard_map.269 = bf16[64,8,128]{2,1,0:T(8,128)(2,1)} custom-call(bf16[32,16,128]{2,1,0:T(8,128)(2,1)S(1)} %all_to_all.22.update_ref, bf16[32,112,128]{2,1,0:T(8,128)(2,1)S(1)} %all_to_all.20.got_ref, f32[1,128]{1,0:T(1,128)S(1)} %bitcast.12, f32[1,128]{1,0:T(1,128)S(1)} %bitcast.13, bf16[128,128]{1,0:T(8,128)(2,1)S(1)} %copy-done.4, ...), custom_call_target="tpu_custom_call" | custom-call | tf_op jit(solution)/shard_map/pallas_call | solution.py:288
  98.5 11.9 %all-to-all-start.3 = ((bf16[64,8,128]{2,1,0:T(8,128)(2,1)}), bf16[64,8,128]{2,1,0:T(8,128)(2,1)S(1)}, u32[]{:S(2)}, u32[]{:S(2)}) async-start(bf16[64,8,128]{2,1,0:T(8,128)(2,1)} %shard_map.269), calls=%async_computation.3 | async-start | bytes 262144 | tf_op jit(solution)/shard_map/all_to_all | solution.py:405
  110.4 0.6 copy-done.26
  111.0 0.1 copy.32.penalty_ref
  111.1 0.1 copy.33.step_ref
  111.2 0.5 copy-done.17
  111.7 0.1 copy-done.14
  111.8 0.0 copy-done.16
  111.8 2.4 %shard_map.270 = (bf16[8,64]{1,0:T(8,128)(2,1)}, f32[3,8]{1,0:T(4,128)}) custom-call(s32[8]{0:T(128)S(1)} %copy-done.19, bf16[32,112,128]{2,1,0:T(8,128)(2,1)S(1)} %all_to_all.20.got_ref, s32[8,64]{1,0:T(8,128)S(1)} %copy-done.17, f32[64,8]{1,0:T(8,128)S(1)} %get-tuple-element.12.query_ref, bf16[8,64]{1,0:T(8,128)(2,1)S(1)} %copy-done.14, ...), custom_call_target="tpu_custom_call" | custom-call | tf_op jit(solution)/shard_map/pallas_call | solution.py:288
  114.2 16.7 %all-to-all-done.3 = bf16[64,8,128]{2,1,0:T(8,128)(2,1)S(1)} async-done(((bf16[64,8,128]{2,1,0:T(8,128)(2,1)}), bf16[64,8,128]{2,1,0:T(8,128)(2,1)S(1)}, u32[]{:S(2)}, u32[]{:S(2)}) %all-to-all-start.3) | async-done | bytes 131104 | tf_op jit(solution)/shard_map/all_to_all | solution.py:405
  130.9 0.7 copy.35
  (43 shorter events, 0.1 us)
Async XLA Ops:
  0.6 0.9 copy-start.12
  0.6 0.9 copy-start.10
  0.7 0.9 copy-start.11
  1.5 0.7 copy-start.20
  1.5 0.7 copy-start.21
  2.2 0.9 copy-start
  3.1 0.8 copy-start.3
  3.9 0.7 copy-start.13
  4.6 0.7 copy-start.15
  5.3 0.7 copy-start.18
  6.0 15.3 %copy-start.24 = (bf16[64,32]{0,1:T(8,128)(2,1)S(1)}, bf16[64,32]{0,1:T(8,128)(2,1)}, u32[]{:S(2)}) copy-start(bf16[64,32]{0,1:T(8,128)(2,1)} %param.30) | copy-start | bytes 12292
  6.0 20.1 %copy-start.1 = (bf16[64,8,128]{2,1,0:T(8,128)(2,1)S(1)}, bf16[64,8,128]{2,1,0:T(8,128)(2,1)}, u32[]{:S(2)}) copy-start(bf16[64,8,128]{2,1,0:T(8,128)(2,1)} %param.34) | copy-start | bytes 393220
  6.6 14.8 %copy-start.25 = (bf16[64,32]{0,1:T(8,128)(2,1)S(1)}, bf16[64,32]{0,1:T(8,128)(2,1)}, u32[]{:S(2)}) copy-start(bf16[64,32]{0,1:T(8,128)(2,1)} %param.31) | copy-start | bytes 12292
  6.6 19.5 %collective-permute-start = (bf16[400,128]{1,0:T(8,128)(2,1)S(1)}, bf16[400,128]{1,0:T(8,128)(2,1)S(1)}, u32[]{:S(2)}, u32[]{:S(2)}) collective-permute-start(bf16[400,128]{1,0:T(8,128)(2,1)S(1)} %get-tuple-element.11), channel_id=1, source_target_pairs={{0,1},{1,0},{2,3},{3,2},{4,5},{5,4},{6,7},{7,6},{8,9},{9,8},{10,11... | collective-permute-start | bytes 307208 | tf_op jit(solution)/shard_map/ppermute | solution.py:352
  53.2 21.4 %copy-start.2 = (bf16[1024,128]{1,0:T(8,128)(2,1)S(1)}, bf16[1024,128]{1,0:T(8,128)(2,1)}, u32[]{:S(2)}) copy-start(bf16[1024,128]{1,0:T(8,128)(2,1)} %weight_ref.1) | copy-start | bytes 786436
  76.5 17.0 %copy-start.4 = (bf16[128,128]{1,0:T(8,128)(2,1)S(1)}, bf16[128,128]{1,0:T(8,128)(2,1)}, u32[]{:S(2)}) copy-start(bf16[128,128]{1,0:T(8,128)(2,1)} %wq_ref.3) | copy-start | bytes 98308
  76.5 17.0 %copy-start.5 = (bf16[128,128]{1,0:T(8,128)(2,1)S(1)}, bf16[128,128]{1,0:T(8,128)(2,1)}, u32[]{:S(2)}) copy-start(bf16[128,128]{1,0:T(8,128)(2,1)} %wk_ref.3) | copy-start | bytes 98308
  76.5 17.0 %copy-start.6 = (bf16[128,128]{1,0:T(8,128)(2,1)S(1)}, bf16[128,128]{1,0:T(8,128)(2,1)}, u32[]{:S(2)}) copy-start(bf16[128,128]{1,0:T(8,128)(2,1)} %wv_ref.3) | copy-start | bytes 98308
  76.5 17.0 %copy-start.7 = (bf16[128,128]{1,0:T(8,128)(2,1)S(1)}, bf16[128,128]{1,0:T(8,128)(2,1)}, u32[]{:S(2)}) copy-start(bf16[128,128]{1,0:T(8,128)(2,1)} %wg_ref.1) | copy-start | bytes 98308
  76.5 17.0 %copy-start.8 = (bf16[128,128]{1,0:T(8,128)(2,1)S(1)}, bf16[128,128]{1,0:T(8,128)(2,1)}, u32[]{:S(2)}) copy-start(bf16[128,128]{1,0:T(8,128)(2,1)} %wo_ref.2) | copy-start | bytes 98308
  93.5 0.7 copy-start.22
  93.5 0.7 copy-start.23
  98.5 12.7 %copy-start.27 = (f32[4]{0:T(128)S(1)}, f32[4]{0:T(128)}, u32[]{:S(2)}) copy-start(f32[4]{0:T(128)} %param.51) | copy-start | bytes 52
  98.5 12.8 %copy-start.9 = (bf16[64,64]{1,0:T(8,128)(2,1)S(1)}, bf16[64,64]{1,0:T(8,128)(2,1)}, u32[]{:S(2)}) copy-start(bf16[64,64]{1,0:T(8,128)(2,1)} %wo_ref.3) | copy-start | bytes 24580
  98.5 12.8 %copy-start.19 = (s32[8]{0:T(128)S(1)}, s32[8]{0:T(128)}, u32[]{:S(2)}) copy-start(s32[8]{0:T(128)} %count_ref.1) | copy-start | bytes 100
  98.5 32.4 %all-to-all-start.3 = ((bf16[64,8,128]{2,1,0:T(8,128)(2,1)}), bf16[64,8,128]{2,1,0:T(8,128)(2,1)S(1)}, u32[]{:S(2)}, u32[]{:S(2)}) async-start(bf16[64,8,128]{2,1,0:T(8,128)(2,1)} %shard_map.269), calls=%async_computation.3 | async-start | bytes 262144 | tf_op jit(solution)/shard_map/all_to_all | solution.py:405
  110.4 0.7 copy-start.26
  111.0 0.7 copy-start.17
  111.1 0.7 copy-start.14
  111.1 0.7 copy-start.16

commit v3 on v1

--- a/solution.py
+++ b/solution.py
@@ -14,6 +14,7 @@
 PLANE = ("x", "core", "y")
 GROUP = ("x", "core", "y", "zh")
 VMEM_LIMIT = 48 * 1024 * 1024
+FETCH_LIMIT = 56 * 1024 * 1024
 
 
 def dot(a, b, ca=1, cb=0):
@@ -35,19 +36,43 @@
     return centred * lax.rsqrt(variance + 1e-05) * gain
 
 
-def msa_kernel(
-    act_ref, tok_ref, emb_ref, gain_ref, wl_ref, wr_ref, left_ref, right_ref
+def swap_lane_groups(v, low, even):
+    t0 = jnp.where(low, v[0], pltpu.roll(v[2], 64, 1))
+    t2 = jnp.where(low, pltpu.roll(v[0], 64, 1), v[2])
+    t1 = jnp.where(low, v[1], pltpu.roll(v[3], 64, 1))
+    t3 = jnp.where(low, pltpu.roll(v[1], 64, 1), v[3])
+    return (
+        jnp.where(even, t0, pltpu.roll(t1, 32, 1)),
+        jnp.where(even, pltpu.roll(t0, 96, 1), t1),
+        jnp.where(even, t2, pltpu.roll(t3, 32, 1)),
+        jnp.where(even, pltpu.roll(t2, 96, 1), t3),
+    )
+
+
+def lane_masks(rows):
+    lane = iota((rows, 128), 1)
+    return lane < 64, (lane // 32) % 2 == 0
+
+
+def first_kernel(
+    act_ref,
+    tok_ref,
+    emb_ref,
+    gain_ref,
+    wl_ref,
+    wr_ref,
+    out_ref,
 ):
     seqs, length, _ = act_ref.shape
-    kinds = emb_ref.shape[0]
+    kinds = emb_ref.shape[1]
     emb = emb_ref[...]
     rows = []
     for s in range(seqs):
         picked = one_where(iota((kinds, length), 0) == tok_ref[s : s + 1, :])
-        rows.append(act_ref[s].astype(F32) + dot(picked, emb, 0, 0))
+        rows.append(act_ref[s].astype(F32) + dot(picked, emb, 0, 1))
     normed = layer_normalize(jnp.concatenate(rows, 0), gain_ref[...]).astype(BF16)
 
-    left = dot(wl_ref[...], normed, 0, 1).astype(BF16).astype(F32)
+    left = dot(wl_ref[...], normed, 1, 1).astype(BF16).astype(F32)
     low = iota((16, 128), 1) < 64
     parts = []
     for p in range(2):
@@ -56,28 +81,23 @@
         parts.append(jnp.where(low, a0, pltpu.roll(a1, 64, 1)))
         parts.append(jnp.where(low, pltpu.roll(a0, 64, 1), a1))
     block = jnp.concatenate(parts, 0).astype(BF16)
-    left_ref[...] = jnp.broadcast_to(block[None], left_ref.shape)
-
-    out_row, source = iota((256, 256), 0), iota((256, 256), 1)
-    wanted = (out_row % 4) * 64 + ((out_row % 64) // 4) * 4 + out_row // 64
-    moved = dot(one_where(source == wanted), normed).astype(BF16)
-    right = jnp.zeros((64, 128), F32)
-    for j in range(4):
-        place = one_where(iota((32, 128), 1) == iota((32, 128), 0) + 32 * j)
-        widened = dot(wr_ref[...], place).astype(BF16)
-        right = right + dot(moved[j * 64 : (j + 1) * 64], widened)
-    right = right.astype(BF16).reshape(4, 16, 128)
-    for a in range(8):
-        right_ref[a * 4 : (a + 1) * 4] = right
-
-
-def node_project_kernel(nodes_ref, coords_ref, gain_ref, wq_ref, wk_ref, wv_ref, slot_ref, query_ref):
-    normed = layer_normalize(nodes_ref[...].astype(F32), gain_ref[...]).astype(BF16)
+    out_ref[:, 0:64] = jnp.broadcast_to(block[None], (32, 64, 128))
+
+    widened = dot(wr_ref[...], one_where(iota((32, 128), 1) == iota((32, 128), 0)), 0, 0).astype(BF16)
+    for g in range(2):
+        row, source = iota((256, 256), 0) + g * 256, iota((256, 256), 1)
+        wanted = ((row % 8) // 2) * 64 + (row // 16) * 2 + row % 2
+        moved = dot(one_where((source == wanted) & (row % 16 < 8)), normed).astype(BF16)
+        right = dot(moved, widened).astype(BF16)
+        out_ref[g * 16 : (g + 1) * 16, 64:80] = right.reshape(16, 16, 128)
+
+
+def node_project_kernel(nodes_ref, coords_ref, node_gain_ref, wq_ref, wk_ref, wv_ref, slot_ref, query_ref):
+    row, lane = iota((64, 128), 0), iota((64, 128), 1)
+    normed = layer_normalize(nodes_ref[...].astype(F32), node_gain_ref[...]).astype(BF16)
     query_ref[...] = dot(wq_ref[...], normed, 0, 1).astype(BF16).astype(F32)
-    width = wk_ref.shape[1]
-    row, lane = iota((width, 128), 0), iota((width, 128), 1)
     kv = dot(normed, dot(wk_ref[...], one_where(lane == row)).astype(BF16))
-    kv = kv + dot(normed, dot(wv_ref[...], one_where(lane == row + width)).astype(BF16))
+    kv = kv + dot(normed, dot(wv_ref[...], one_where(lane == row + 64)).astype(BF16))
     rest = coords_ref[...]
     placed = jnp.zeros((8, 128), F32)
     for part in range(3):
@@ -88,61 +108,72 @@
     slot_ref[...] = jnp.concatenate([kv, placed], 0).astype(BF16)
 
 
+def right_kernel(got_ref, out_ref):
+    rows = got_ref[:, 64:80].reshape(512, 128)
+    row, source = iota((64, 512), 0), iota((64, 512), 1)
+    start = (row // 4) * 16 + (row % 4) * 2
+    at, lane = iota((128, 128), 0), iota((128, 128), 1)
+    total = jnp.zeros((64, 128), F32)
+    for hi in range(2):
+        for column in range(2):
+            picked = dot(one_where(source == start + hi * 256 + column), rows).astype(BF16)
+            shift = (hi * 2 + column) * 32
+            total = total + dot(picked, one_where((lane == at + shift) & (at < 32)))
+    out_ref[...] = jnp.broadcast_to(total.astype(BF16)[None], out_ref.shape)
+
+
 def outer_kernel(
-    half_ref, left_in, right_in, pair_ref, weight_ref, bias_ref, slot_ref, out_ref, left, right, joined, update
+    got_ref, right_in, pair_ref, weight_ref, slot_ref, out_ref, left, right, joined, update
 ):
     turn = one_where(
         iota((256, 256), 1) == (iota((256, 256), 0) % 16) * 16 + iota((256, 256), 0) // 16
     )
     for g in range(8):
-        part = dot(turn, left_in[g * 4 : (g + 1) * 4].reshape(256, 128)).astype(BF16)
+        part = dot(turn, got_ref[g * 4 : (g + 1) * 4, 0:64].reshape(256, 128)).astype(BF16)
         for q in range(16):
             left[g * 16 : (g + 1) * 16, q * 128 : (q + 1) * 128] = part[q * 16 : (q + 1) * 16]
-    row = iota((256, 256), 0)
-    turn = one_where(
-        iota((256, 256), 1) == ((row % 64) // 4) * 16 + (row // 64) * 4 + row % 4
-    )
-    for g in range(2):
-        part = dot(turn, right_in[g * 16 : (g + 1) * 16].reshape(256, 128)).astype(BF16)
-        for q in range(4):
-            right[g * 64 : (g + 1) * 64, q * 128 : (q + 1) * 128] = part[q * 64 : (q + 1) * 64]
-
-    lane = iota((128, 128), 1)
-    low, even = lane < 64, (lane // 32) % 2 == 0
+    low, even = lane_masks(64)
+    for t in range(4):
+        a, b = right_in[2 * t].astype(F32), right_in[2 * t + 1].astype(F32)
+        right[0:64, t * 128 : (t + 1) * 128] = jnp.where(low, a, pltpu.roll(b, 64, 1)).astype(BF16)
+        right[64:128, t * 128 : (t + 1) * 128] = jnp.where(low, pltpu.roll(a, 64, 1), b).astype(BF16)
+
+    low, even = lane_masks(128)
     scale = 1.0 / 256.0
     for e in range(4):
         products = [
             dot(left[:, (4 * e + k) * 128 : (4 * e + k + 1) * 128], right[...], 0, 0) * scale
             for k in range(4)
         ]
-        for jq in range(4):
-            v0, v1, v2, v3 = [p[:, jq * 128 : (jq + 1) * 128] for p in products]
-            t0 = jnp.where(low, v0, pltpu.roll(v2, 64, 1))
-            t2 = jnp.where(low, pltpu.roll(v0, 64, 1), v2)
-            t1 = jnp.where(low, v1, pltpu.roll(v3, 64, 1))
-            t3 = jnp.where(low, pltpu.roll(v1, 64, 1), v3)
-            a = [
-                jnp.where(even, t0, pltpu.roll(t1, 32, 1)),
-                jnp.where(even, pltpu.roll(t0, 96, 1), t1),
-                jnp.where(even, t2, pltpu.roll(t3, 32, 1)),
-                jnp.where(even, pltpu.roll(t2, 96, 1), t3),
-            ]
+        for t in range(4):
+            blocks = swap_lane_groups([p[:, t * 128 : (t + 1) * 128] for p in products], low, even)
             for j in range(4):
-                block = a[j].astype(BF16)
-                at = (jq * 4 + j) * 64
+                block = blocks[j].astype(BF16)
+                at = (t * 4 + j) * 64
                 joined[at : at + 64, e * 128 : (e + 1) * 128] = block[:64]
                 joined[at : at + 64, (4 + e) * 128 : (5 + e) * 128] = block[64:]
-    for j in range(16):
-        update[:, j, :] = dot(joined[j * 64 : (j + 1) * 64], weight_ref[...])
-    own = pl.multiple_of(half_ref[0] * 8, 8)
-    update[:, pl.ds(own, 8), :] += pair_ref[...].astype(F32) + bias_ref[...].reshape(1, 1, 128)
-    out_ref[:, 0:16, :] = update[...].astype(BF16)
-    out_ref[:, 16:32, :] = jnp.broadcast_to(slot_ref[...][None], (64, 16, 128))
-
-
-def attend_kernel(got_ref, gain_ref, wq_ref, wk_ref, wv_ref, wg_ref, wo_ref, out_ref, q_s, k_s, v_s, mid_s, gate_s):
-    both = got_ref[:, 0:16, :].astype(F32).reshape(32, 2, 16, 128)
-    pair_mid = (both[:, 0] + both[:, 1]).reshape(512, 128).astype(BF16).astype(F32)
+    for j in range(0, 16, 4):
+        rows = dot(joined[j * 64 : (j + 4) * 64], weight_ref[...])
+        for k in range(4):
+            update[:, j + k, :] = rows[k * 64 : (k + 1) * 64]
+    out_ref[:, 0:16] = update[...].astype(BF16)
+    slot = slot_ref[...].astype(F32)
+    kv = jnp.broadcast_to(slot[None, 0:8], (64, 8, 128))
+    out_ref[:, 16:32] = jnp.concatenate([pair_ref[...].astype(F32), kv], 1).astype(BF16)
+    out_ref[:, 32:40] = jnp.broadcast_to(slot[None, 8:16], (64, 8, 128)).astype(BF16)
+
+
+def attend_kernel(
+    got_ref, bias_ref, gain_ref, wq_ref, wk_ref, wv_ref, wg_ref, wo_ref, out_ref, q_s, k_s, v_s, mid_s, gate_s
+):
+    row = iota((512, 512), 0)
+    wanted = ((row // 2) % 32) * 16 + (row // 64) * 2 + row % 2
+    turn = one_where(iota((512, 512), 1) == wanted)
+    shares = got_ref[:, 0:16].reshape(32, 2, 16, 128)
+    pair_mid = dot(turn, shares[:, 0].reshape(512, 128)) + dot(turn, shares[:, 1].reshape(512, 128))
+    pair = got_ref[:, 16:32].reshape(64, 2, 8, 128)[:, 0].reshape(512, 128)
+    pair_mid = pair_mid + pair.astype(F32) + bias_ref[...]
+    pair_mid = pair_mid.astype(BF16).astype(F32)
     mid_s[...] = pair_mid
     normed = layer_normalize(pair_mid, gain_ref[...]).astype(BF16)
     q_s[...] = dot(normed, wq_ref[...]).astype(BF16)
@@ -177,9 +208,8 @@
 def node_kernel(
     count_ref, got_ref, index_ref, query_ref, nodes_ref, coords_ref, wo_ref, penalty_ref, step_ref, nodes_out, coords_out
 ):
-    table = got_ref[:, 16:32, :].reshape(64, 2, 8, 128)
-    kv_table = table[:, 0].reshape(512, 128)
-    place_table = table[:, 1].reshape(512, 128)
+    kv_table = got_ref[:, 16:32].reshape(64, 2, 8, 128)[:, 1].reshape(512, 128)
+    place_table = got_ref[:, 32:40].reshape(512, 128)
     local, slots = index_ref.shape
     width, dim = nodes_ref.shape[1], nodes_ref.shape[1] // NODE_HEADS
     lane = iota((1, slots), 1)
@@ -215,17 +245,32 @@
     coords_out[...] = coords_ref[...] + moved
 
 
-def call(body, out_shape, args, scratch=(), scalars=0, cost=None):
-    spaces = [pltpu.SMEM] * scalars + [pltpu.VMEM] * (len(args) - scalars)
-    out_specs = jax.tree.map(lambda _: pl.BlockSpec(memory_space=pltpu.VMEM), out_shape)
+def with_fetch(body, count):
+    def kernel(*refs):
+        sources, held, sems = refs[:count], refs[-count - 1 : -1], refs[-1]
+        copies = [pltpu.make_async_copy(sources[i], held[i], sems.at[i]) for i in range(count)]
+        for copy in copies:
+            copy.start()
+        for copy in copies:
+            copy.wait()
+        body(*held, *refs[count : -count - 1])
+
+    return kernel
+
+
+def call(body, out_shape, args, scratch=(), fetch=False):
+    scratch = list(scratch)
+    if fetch:
+        body = with_fetch(body, len(args))
+        scratch += [pltpu.VMEM(a.shape, a.dtype) for a in args] + [pltpu.SemaphoreType.DMA((len(args),))]
+    space = pltpu.HBM if fetch else pltpu.VMEM
     return pl.pallas_call(
         body,
         out_shape=out_shape,
-        in_specs=[pl.BlockSpec(memory_space=s) for s in spaces],
-        out_specs=out_specs,
-        scratch_shapes=list(scratch),
-        compiler_params=pltpu.CompilerParams(vmem_limit_bytes=VMEM_LIMIT),
-        cost_estimate=cost,
+        in_specs=[pl.BlockSpec(memory_space=pltpu.SMEM if a.ndim == 1 else space) for a in args],
+        out_specs=jax.tree.map(lambda _: pl.BlockSpec(memory_space=pltpu.VMEM), out_shape),
+        scratch_shapes=scratch,
+        compiler_params=pltpu.CompilerParams(vmem_limit_bytes=FETCH_LIMIT if fetch else VMEM_LIMIT),
     )(*args)
 
 
@@ -261,23 +306,20 @@
     distance_penalty,
     coordinate_step,
 ):
-    left, right = call(
-        msa_kernel,
-        (shape((32, 64, 128)), shape((32, 16, 128))),
+    spread = call(
+        first_kernel,
+        shape((32, 80, 128)),
         (
             homolog_activations,
             alignment_token_ids,
-            symbol_lookup_matrix,
+            symbol_lookup_matrix.T,
             homolog_rescale_vector.reshape(1, -1),
-            first_operand_projection,
-            second_operand_projection,
-        ),
-    )
-    right = lax.all_to_all(right, PLANE, split_axis=0, concat_axis=0, tiled=True)
-    left, right = lax.optimization_barrier((left, right))
-    across = [(a * 8 + r, r * 8 + a) for a in range(8) for r in range(8)]
-    right = lax.ppermute(right, ("x", "core", "row"), across)
-    left = lax.all_to_all(left, PLANE, split_axis=0, concat_axis=0, tiled=True)
+            first_operand_projection.T,
+            second_operand_projection.T,
+        ),
+        fetch=True,
+    )
+    got = lax.all_to_all(spread, PLANE, split_axis=0, concat_axis=0, tiled=True)
     slot, node_query = call(
         node_project_kernel,
         (shape((16, 128)), shape((64, 8), F32)),
@@ -290,32 +332,26 @@
             node_value_weight,
         ),
     )
-    partial_rows = call(
+    right = call(right_kernel, shape((8, 64, 128)), (got,))
+    right = lax.all_to_all(right, "row", split_axis=0, concat_axis=0, tiled=True)
+    shares = call(
         outer_kernel,
-        shape((64, 32, 128)),
-        (
-            lax.axis_index("zh").reshape(1).astype(jnp.int32),
-            left,
-            right,
-            pair,
-            outer_output_weight,
-            outer_bias.reshape(1, -1),
-            slot,
-        ),
+        shape((64, 40, 128)),
+        (got, right, pair, outer_output_weight, slot),
         scratch=(
             pltpu.VMEM((128, 2048), BF16),
             pltpu.VMEM((128, 512), BF16),
             pltpu.VMEM((1024, 1024), BF16),
             pltpu.VMEM((64, 16, 128), F32),
         ),
-        scalars=1,
-    )
-    got = lax.all_to_all(partial_rows, GROUP, split_axis=0, concat_axis=0, tiled=True)
+    )
+    got = lax.all_to_all(shares, GROUP, split_axis=0, concat_axis=0, tiled=True)
     row = call(
         attend_kernel,
         shape((64, 8, 128)),
         (
             got,
+            outer_bias.reshape(1, -1),
             pair_norm_gain.reshape(1, -1),
             pair_query_weight,
             pair_key_weight,
@@ -346,7 +382,6 @@
             distance_penalty.reshape(-1, 1),
             coordinate_step.reshape(-1, 1),
         ),
-        scalars=1,
     )
     return (pair_out, nodes_out, coords_out)
 

time: 132 us -> 134 us (1.015)
  starting transfers between devices: 9.67 us -> 17.1 us
  blocking collectives: 80.8 us -> 76.8 us
  local copies, waits for them, and re-layouts: 6.51 us -> 3.46 us
  Pallas kernels: 11.1 us -> 13.7 us
  waiting for transfers between devices: 22.8 us -> 21.2 us
    all_to_all x1, starting transfers between devices: 4.19 us -> 12.2 us  [on_device(): lax.all_to_all(right, 'row', split_axis=0, concat_axis=0, tiled=True)]
    all_to_all x2, blocking collectives: 80.8 us -> 76.8 us  [the longest x1 56.8 us: on_device(): got = lax.all_to_all(shares, GROUP, split_axis=0, concat_axis=0, tiled=True)]
    unnamed x52 -> x41, local copies, waits for them, and re-layouts: 6.33 us -> 3.28 us
    pallas_call x5 -> x6, Pallas kernels: 11.1 us -> 13.7 us  [call(): pl.pallas_call(body, out_shape=out_shape, in_specs=[pl.BlockSpec(memory_s...]
    all_to_all x1, waiting for transfers between devices: 9.32 us -> 7.68 us  [on_device(): lax.all_to_all(right, 'row', split_axis=0, concat_axis=0, tiled=True)]
  transfers between devices with their start and end apart: 3 -> 2, of which waited for: 2 -> 2; matrix products, arithmetic and copies ran while one was open for 0% -> 0% of each run, Pallas kernels for 2% -> 2%
where the time goes in v3:
time: 134 us; the launch traced here: 133 us
  blocking collectives  76.8 us (57%)
  waiting for transfers between devices  21.2 us (16%)
  starting transfers between devices  17.1 us (13%)
  Pallas kernels  13.7 us (10%)
  local copies, waits for them, and re-layouts  3.46 us (3%)
    all_to_all x1, blocking collectives, on_device(): got = lax.all_to_all(shares, GROUP, split_axis=0, concat_axis=0, tiled=True)  56.8 us
    all_to_all x1, blocking collectives, on_device(): got = lax.all_to_all(spread, PLANE, split_axis=0, concat_axis=0, tiled=True)  20 us
    pallas_call x6, Pallas kernels, call(): pl.pallas_call(body, out_shape=out_shape, in_specs=[pl.BlockSpec(memory_s...  13.7 us
    all_to_all x1, waiting for transfers between devices, on_device(): lax.all_to_all(row, GROUP, split_axis=0, concat_axis=0, tiled=True)  13.5 us
    all_to_all x1, starting transfers between devices, on_device(): lax.all_to_all(right, 'row', split_axis=0, concat_axis=0, tiled=True)  12.2 us
    all_to_all x1, waiting for transfers between devices, on_device(): lax.all_to_all(right, 'row', split_axis=0, concat_axis=0, tiled=True)  7.68 us
    all_to_all x1, starting transfers between devices, on_device(): lax.all_to_all(row, GROUP, split_axis=0, concat_axis=0, tiled=True)  4.87 us
    unnamed x41, local copies, waits for them, and re-layouts  3.28 us
  transfers between devices with their start and end apart: 2, of which 2 were waited for; matrix products, arithmetic and copies ran while one was open for 0% of the time, Pallas kernels for 2%

profile of v3, /device:TPU:33, one launch (start us, length us, event | category | flops | bytes accessed | tf_op | source)
XLA Modules:
  0.0 132.9 jit_solution(12706199738859881601)
XLA Ops:
  0.6 2.6 %shard_map.265 = bf16[32,80,128]{2,1,0:T(8,128)(2,1)} custom-call(bf16[4,64,64]{2,1,0:T(8,128)(2,1)} %refs_0_.1, s32[4,64]{1,0:T(4,128)} %refs_1_.1, bf16[64,80]{1,0:T(8,128)(2,1)} %bitcast.12, f32[1,64]{1,0:T(1,128)} %bitcast.15, bf16[32,64]{1,0:T(8,128)(2,1)} %bitcast.13, bf16[32,64]{1,0:T(8,128)(2,1)} %bitcast.14), custom_call_target="tpu_custom_call" | custom-call | tf_op jit(solution)/shard_map/pallas_call | solution.py:267
  3.3 20.0 %all_to_all.20.got_ref = bf16[32,80,128]{2,1,0:T(8,128)(2,1)S(1)} all-to-all(bf16[32,80,128]{2,1,0:T(8,128)(2,1)} %shard_map.265), channel_id=1, replica_groups=mesh['x'=4,'core'=2,'row'=8,'y'=4,'zh'=2] {'x','core','y'}, dimensions={0} | all-to-all | bytes 1310720 | tf_op jit(solution)/shard_map/all_to_all | solution.py:322
  23.3 0.0 copy-start.12
  23.3 0.0 copy-start.1
  23.3 1.1 shard_map.266
  24.5 12.2 %all-to-all-start.1 = ((bf16[8,64,128]{2,1,0:T(8,128)(2,1)}), bf16[8,64,128]{2,1,0:T(8,128)(2,1)S(1)}, u32[]{:S(2)}, u32[]{:S(2)}) async-start(bf16[8,64,128]{2,1,0:T(8,128)(2,1)} %shard_map.266), calls=%async_computation.1 | async-start | bytes 262144 | tf_op jit(solution)/shard_map/all_to_all | solution.py:336
  36.7 0.6 copy-done.14
  37.3 0.4 shard_map.267
  37.7 7.7 %all-to-all-done.1.right_in = bf16[8,64,128]{2,1,0:T(8,128)(2,1)S(1)} async-done(((bf16[8,64,128]{2,1,0:T(8,128)(2,1)}), bf16[8,64,128]{2,1,0:T(8,128)(2,1)S(1)}, u32[]{:S(2)}, u32[]{:S(2)}) %all-to-all-start.1) | async-done | bytes 131104 | tf_op jit(solution)/shard_map/all_to_all | solution.py:336
  45.4 0.0 copy-done.1
  45.4 2.7 %shard_map.268 = bf16[64,40,128]{2,1,0:T(8,128)(2,1)S(1)} custom-call(bf16[32,80,128]{2,1,0:T(8,128)(2,1)S(1)} %all_to_all.20.got_ref, bf16[8,64,128]{2,1,0:T(8,128)(2,1)S(1)} %all-to-all-done.1.right_in, bf16[64,8,128]{2,1,0:T(8,128)(2,1)S(1)} %copy-done.1, bf16[1024,128]{1,0:T(8,128)(2,1)S(1)} %copy-done, bf16[16,128]{1,0:T(8,128)(2,1)S(1)} %get-tuple-element.7.slot_ref), custom_call_target="tpu_custom_call" | custom-call | tf_op jit(solution)/shard_map/pallas_call | solution.py:267
  48.1 0.0 copy-start.2
  48.1 0.0 copy-start.3
  48.2 0.0 copy-start.4
  48.2 0.0 copy-start.5
  48.2 0.0 copy-start.6
  48.2 56.8 %all_to_all.21.got_ref = bf16[64,40,128]{2,1,0:T(8,128)(2,1)S(1)} all-to-all(bf16[64,40,128]{2,1,0:T(8,128)(2,1)S(1)} %shard_map.268), channel_id=1, replica_groups=mesh['x'=4,'core'=2,'row'=8,'y'=4,'zh'=2] {'x','core','y','zh'}, dimensions={0} | all-to-all | bytes 1310720 | tf_op jit(solution)/shard_map/all_to_all | solution.py:348
  105.0 0.0 copy-done.2
  105.0 0.6 copy-done.15
  105.6 0.0 copy-done.16
  105.6 4.4 %shard_map.269 = bf16[64,8,128]{2,1,0:T(8,128)(2,1)} custom-call(bf16[64,40,128]{2,1,0:T(8,128)(2,1)S(1)} %all_to_all.21.got_ref, f32[1,128]{1,0:T(1,128)S(1)} %bitcast.10, f32[1,128]{1,0:T(1,128)S(1)} %bitcast.11, bf16[128,128]{1,0:T(8,128)(2,1)S(1)} %copy-done.2, bf16[128,128]{1,0:T(8,128)(2,1)S(1)} %copy-done.3, bf16[128,128]{1,0:T(8,128)(2,1)S(1)} %copy-done.4, ...), custom_call_target="tpu_custom_call" | custom-call | tf_op jit(solution)/shard_map/pallas_call | solution.py:267
  110.0 4.9 %all-to-all-start.3 = ((bf16[64,8,128]{2,1,0:T(8,128)(2,1)}), bf16[64,8,128]{2,1,0:T(8,128)(2,1)S(1)}, u32[]{:S(2)}, u32[]{:S(2)}) async-start(bf16[64,8,128]{2,1,0:T(8,128)(2,1)} %shard_map.269), calls=%async_computation.3 | async-start | bytes 262144 | tf_op jit(solution)/shard_map/all_to_all | solution.py:370
  114.9 0.0 copy-start.18
  114.9 0.6 copy-done.18
  115.6 0.1 copy.29.penalty_ref
  115.7 0.1 copy.30.step_ref
  115.7 0.0 copy-done.7
  115.8 0.5 copy-done.13
  116.2 0.2 copy-done.17
  116.4 2.4 %shard_map.270 = (bf16[8,64]{1,0:T(8,128)(2,1)}, f32[3,8]{1,0:T(4,128)}) custom-call(s32[8]{0:T(128)S(1)} %copy-done.17, bf16[64,40,128]{2,1,0:T(8,128)(2,1)S(1)} %all_to_all.21.got_ref, s32[8,64]{1,0:T(8,128)S(1)} %copy-done.13, f32[64,8]{1,0:T(8,128)S(1)} %get-tuple-element.8.query_ref, bf16[8,64]{1,0:T(8,128)(2,1)S(1)} %copy-done.11, ...), custom_call_target="tpu_custom_call" | custom-call | tf_op jit(solution)/shard_map/pallas_call | solution.py:267
  118.8 13.5 %all-to-all-done.3 = bf16[64,8,128]{2,1,0:T(8,128)(2,1)S(1)} async-done(((bf16[64,8,128]{2,1,0:T(8,128)(2,1)}), bf16[64,8,128]{2,1,0:T(8,128)(2,1)S(1)}, u32[]{:S(2)}, u32[]{:S(2)}) %all-to-all-start.3) | async-done | bytes 131104 | tf_op jit(solution)/shard_map/all_to_all | solution.py:370
  132.2 0.7 copy.32
  (23 shorter events, 0.0 us)
Async XLA Ops:
  23.3 13.4 %copy-start.8 = (bf16[64,64]{1,0:T(8,128)(2,1)S(1)}, bf16[64,64]{1,0:T(8,128)(2,1)}, u32[]{:S(2)}) copy-start(bf16[64,64]{1,0:T(8,128)(2,1)} %wq_ref.2) | copy-start | bytes 24580
  23.3 13.4 %copy-start.9 = (bf16[64,64]{1,0:T(8,128)(2,1)S(1)}, bf16[64,64]{1,0:T(8,128)(2,1)}, u32[]{:S(2)}) copy-start(bf16[64,64]{1,0:T(8,128)(2,1)} %wk_ref.2) | copy-start | bytes 24580
  23.3 13.4 %copy-start.10 = (bf16[64,64]{1,0:T(8,128)(2,1)S(1)}, bf16[64,64]{1,0:T(8,128)(2,1)}, u32[]{:S(2)}) copy-start(bf16[64,64]{1,0:T(8,128)(2,1)} %wv_ref.2) | copy-start | bytes 24580
  23.3 13.4 %copy-start.11 = (bf16[8,64]{1,0:T(8,128)(2,1)S(1)}, bf16[8,64]{1,0:T(8,128)(2,1)}, u32[]{:S(2)}) copy-start(bf16[8,64]{1,0:T(8,128)(2,1)} %nodes_ref.3) | copy-start | bytes 3076
  23.3 13.4 %copy-start.12 = (f32[3,8]{1,0:T(4,128)S(1)}, f32[3,8]{1,0:T(4,128)}, u32[]{:S(2)}) copy-start(f32[3,8]{1,0:T(4,128)} %coords_ref.3) | copy-start | bytes 292
  23.3 22.1 %copy-start.1 = (bf16[64,8,128]{2,1,0:T(8,128)(2,1)S(1)}, bf16[64,8,128]{2,1,0:T(8,128)(2,1)}, u32[]{:S(2)}) copy-start(bf16[64,8,128]{2,1,0:T(8,128)(2,1)} %pair_ref.1) | copy-start | bytes 393220
  24.5 21.0 %copy-start = (bf16[1024,128]{1,0:T(8,128)(2,1)S(1)}, bf16[1024,128]{1,0:T(8,128)(2,1)}, u32[]{:S(2)}) copy-start(bf16[1024,128]{1,0:T(8,128)(2,1)} %weight_ref.1) | copy-start | bytes 786436
  24.5 21.0 %all-to-all-start.1 = ((bf16[8,64,128]{2,1,0:T(8,128)(2,1)}), bf16[8,64,128]{2,1,0:T(8,128)(2,1)S(1)}, u32[]{:S(2)}, u32[]{:S(2)}) async-start(bf16[8,64,128]{2,1,0:T(8,128)(2,1)} %shard_map.266), calls=%async_computation.1 | async-start | bytes 262144 | tf_op jit(solution)/shard_map/all_to_all | solution.py:336
  36.7 0.7 copy-start.14
  48.1 56.8 %copy-start.2 = (bf16[128,128]{1,0:T(8,128)(2,1)S(1)}, bf16[128,128]{1,0:T(8,128)(2,1)}, u32[]{:S(2)}) copy-start(bf16[128,128]{1,0:T(8,128)(2,1)} %wq_ref.3) | copy-start | bytes 98308
  48.1 56.8 %copy-start.3 = (bf16[128,128]{1,0:T(8,128)(2,1)S(1)}, bf16[128,128]{1,0:T(8,128)(2,1)}, u32[]{:S(2)}) copy-start(bf16[128,128]{1,0:T(8,128)(2,1)} %wk_ref.3) | copy-start | bytes 98308
  48.2 56.8 %copy-start.4 = (bf16[128,128]{1,0:T(8,128)(2,1)S(1)}, bf16[128,128]{1,0:T(8,128)(2,1)}, u32[]{:S(2)}) copy-start(bf16[128,128]{1,0:T(8,128)(2,1)} %wv_ref.3) | copy-start | bytes 98308
  48.2 56.8 %copy-start.5 = (bf16[128,128]{1,0:T(8,128)(2,1)S(1)}, bf16[128,128]{1,0:T(8,128)(2,1)}, u32[]{:S(2)}) copy-start(bf16[128,128]{1,0:T(8,128)(2,1)} %wg_ref.1) | copy-start | bytes 98308
  48.2 56.8 %copy-start.6 = (bf16[128,128]{1,0:T(8,128)(2,1)S(1)}, bf16[128,128]{1,0:T(8,128)(2,1)}, u32[]{:S(2)}) copy-start(bf16[128,128]{1,0:T(8,128)(2,1)} %wo_ref.2) | copy-start | bytes 98308
  105.0 0.7 copy-start.15
  105.0 0.7 copy-start.16
  110.0 5.6 %copy-start.19 = (f32[4]{0:T(128)S(1)}, f32[4]{0:T(128)}, u32[]{:S(2)}) copy-start(f32[4]{0:T(128)} %param.51) | copy-start | bytes 52
  110.0 5.7 %copy-start.7 = (bf16[64,64]{1,0:T(8,128)(2,1)S(1)}, bf16[64,64]{1,0:T(8,128)(2,1)}, u32[]{:S(2)}) copy-start(bf16[64,64]{1,0:T(8,128)(2,1)} %wo_ref.3) | copy-start | bytes 24580
  110.0 22.2 %all-to-all-start.3 = ((bf16[64,8,128]{2,1,0:T(8,128)(2,1)}), bf16[64,8,128]{2,1,0:T(8,128)(2,1)S(1)}, u32[]{:S(2)}, u32[]{:S(2)}) async-start(bf16[64,8,128]{2,1,0:T(8,128)(2,1)} %shard_map.269), calls=%async_computation.3 | async-start | bytes 262144 | tf_op jit(solution)/shard_map/all_to_all | solution.py:370
  114.9 0.7 copy-start.18
  115.6 0.7 copy-start.13
  115.7 0.7 copy-start.17

commit v4 on v2

v4 whole, which is shorter than its diff:
```python
import math

import jax
import jax.numpy as jnp
from jax import lax
from jax.experimental import pallas as pl
from jax.experimental.pallas import tpu as pltpu
from jax.sharding import Mesh, PartitionSpec as P

F32 = jnp.float32
BF16 = jnp.bfloat16
PAIR_HEADS = 4
NODE_HEADS = 4
PLANE = ("x", "core", "y")
GROUP = ("x", "core", "y", "zh")
VMEM_LIMIT = 48 * 1024 * 1024
FETCH_LIMIT = 56 * 1024 * 1024


def dot(a, b, ca=1, cb=0):
    return lax.dot_general(a, b, (((ca,), (cb,)), ((), ())), preferred_element_type=F32)


def iota(shape, dim):
    return lax.broadcasted_iota(jnp.int32, shape, dim)


def one_where(mask):
    return jnp.where(mask, 1.0, 0.0).astype(BF16)


def layer_normalize(values_in, gain):
    average = jnp.mean(values_in, -1, keepdims=True)
    centred = values_in - average
    variance = jnp.mean(centred * centred, -1, keepdims=True)
    return centred * lax.rsqrt(variance + 1e-05) * gain


def swap_lane_groups(v, low, even):
    t0 = jnp.where(low, v[0], pltpu.roll(v[2], 64, 1))
    t2 = jnp.where(low, pltpu.roll(v[0], 64, 1), v[2])
    t1 = jnp.where(low, v[1], pltpu.roll(v[3], 64, 1))
    t3 = jnp.where(low, pltpu.roll(v[1], 64, 1), v[3])
    return (
        jnp.where(even, t0, pltpu.roll(t1, 32, 1)),
        jnp.where(even, pltpu.roll(t0, 96, 1), t1),
        jnp.where(even, t2, pltpu.roll(t3, 32, 1)),
        jnp.where(even, pltpu.roll(t2, 96, 1), t3),
    )


def lane_masks(rows):
    lane = iota((rows, 128), 1)
    return lane < 64, (lane // 32) % 2 == 0


def first_kernel(
    act_ref,
    tok_ref,
    emb_ref,
    gain_ref,
    nodes_ref,
    coords_ref,
    node_gain_ref,
    wq_ref,
    wk_ref,
    wv_ref,
    swap_ref,
    query_ref,
):
    seqs, length, _ = act_ref.shape
    kinds = emb_ref.shape[1]
    emb = emb_ref[...]
    rows = []
    for s in range(seqs):
        picked = one_where(iota((kinds, length), 0) == tok_ref[s : s + 1, :])
        rows.append(act_ref[s].astype(F32) + dot(picked, emb, 0, 1))
    normed = layer_normalize(jnp.concatenate(rows, 0), gain_ref[...]).astype(BF16)
    row, lane = iota((64, 128), 0), iota((64, 128), 1)
    packed = dot(normed[:128], one_where(lane == row)) + dot(normed[128:], one_where(lane == row + 64))
    swap_ref[0:128] = packed.astype(BF16)

    normed = layer_normalize(nodes_ref[...].astype(F32), node_gain_ref[...]).astype(BF16)
    query_ref[...] = dot(wq_ref[...], normed, 0, 1).astype(BF16).astype(F32)
    kv = dot(normed, dot(wk_ref[...], one_where(lane == row)).astype(BF16))
    kv = kv + dot(normed, dot(wv_ref[...], one_where(lane == row + 64)).astype(BF16))
    rest = coords_ref[...]
    placed = jnp.zeros((8, 128), F32)
    for part in range(3):
        piece = rest.astype(BF16)
        rest = rest - piece.astype(F32)
        spot = one_where(iota((3, 128), 1) == iota((3, 128), 0) * 3 + part)
        placed = placed + dot(piece, spot, 0, 0)
    swap_ref[128:144] = jnp.concatenate([kv, placed], 0).astype(BF16)


def spread_kernel(half_ref, own_ref, got_ref, wl_ref, wr_ref, out_ref):
    mine = half_ref[0] == 0
    own, came = own_ref[...].astype(F32), got_ref[...].astype(F32)
    one = jnp.where(mine, own, came)
    two = jnp.where(mine, came, own)
    row, lane = iota((128, 64), 0), iota((128, 64), 1)
    planes = []
    for block in (one, two):
        packed = block[:128].astype(BF16)
        parts = [dot(packed, one_where(row == lane)), dot(packed, one_where(row == lane + 64))]
        planes.append(jnp.concatenate(parts, 0).astype(BF16))

    row, source = iota((128, 256), 0), iota((128, 256), 1)
    low, even = lane_masks(8)
    for core in range(2):
        pick = one_where(source == (row // 32) * 64 + (row % 32) * 2 + core)
        parts = []
        for p in range(2):
            rows = dot(pick, planes[p]).astype(BF16)
            left = dot(wl_ref[...], rows, 1, 1).astype(BF16).astype(F32)
            parts += swap_lane_groups([left[k * 8 : (k + 1) * 8] for k in range(4)], low, even)
        block = jnp.concatenate(parts, 0).astype(BF16)
        for to in range(32):
            if (to // 4) % 2 == core:
                out_ref[to, 0:64] = block

    kv = jnp.concatenate([one[128:136], two[128:136]], 0).astype(BF16)
    out_ref[:, 64:80] = jnp.broadcast_to(kv[None], (32, 16, 128))
    place = jnp.concatenate([one[136:144], two[136:144]], 0)
    widened = dot(wr_ref[...], one_where(iota((32, 128), 1) == iota((32, 128), 0) + 32), 0, 0).astype(BF16)
    both = jnp.concatenate(planes, 0)
    for g in range(4):
        row, source = iota((128, 512), 0) + g * 128, iota((128, 512), 1)
        wanted = ((row // 8) % 2) * 256 + ((row // 2) % 4) * 64 + (row // 16) * 2 + row % 2
        moved = dot(one_where(source == wanted), both).astype(BF16)
        right = dot(moved, widened).reshape(8, 16, 128) + place[None]
        out_ref[g * 8 : (g + 1) * 8, 80:96] = right.astype(BF16)


def right_kernel(got_ref, out_ref):
    rows = got_ref[:, 80:96].reshape(512, 128)
    row, source = iota((128, 512), 0), iota((128, 512), 1)
    start = (row // 4) * 16 + (row % 4) * 2
    at, lane = iota((128, 128), 0), iota((128, 128), 1)
    total = jnp.zeros((128, 128), F32)
    for plane in range(2):
        for column in range(2):
            picked = dot(one_where(source == start + plane * 8 + column), rows).astype(BF16)
            shift = (plane * 2 + column) * 32
            keep = (lane >= shift) & (lane < shift + 32)
            total = total + dot(picked, one_where((at + shift == lane + 32) & keep))
    out_ref[...] = jnp.broadcast_to(total.astype(BF16)[None], out_ref.shape)


def outer_kernel(
    half_ref, got_ref, right_in, other_in, pair_ref, came_ref, weight_ref, out_ref, left, right, joined, weight, update
):
    row = iota((256, 256), 0)
    wanted = ((row // 4) % 4) * 64 + ((row // 16) % 2) * 32 + (row % 4) * 8 + row // 32
    turn = one_where(iota((256, 256), 1) == wanted)
    for g in range(8):
        part = dot(turn, got_ref[g * 4 : (g + 1) * 4, 0:64].reshape(256, 128)).astype(BF16)
        for q in range(8):
            for p in range(2):
                at = p * 128 + g * 16
                left[at : at + 16, q * 128 : (q + 1) * 128] = part[q * 32 + p * 16 : q * 32 + p * 16 + 16]
    low, even = lane_masks(128)
    for t in range(8):
        source = right_in if t < 4 else other_in
        a, b = source[2 * (t % 4)].astype(F32), source[2 * (t % 4) + 1].astype(F32)
        right[0:128, t * 128 : (t + 1) * 128] = jnp.where(low, a, pltpu.roll(b, 64, 1)).astype(BF16)
        right[128:256, t * 128 : (t + 1) * 128] = jnp.where(low, pltpu.roll(a, 64, 1), b).astype(BF16)
    for q in range(8):
        for k in range(4):
            at = (k * 8 + q) * 32
            weight[q * 128 + k * 32 : q * 128 + k * 32 + 32] = weight_ref[at : at + 32]

    low, even = lane_masks(32)
    scale = 1.0 / 256.0
    for q in range(8):
        product = dot(left[:, q * 128 : (q + 1) * 128], right[...], 0, 0) * scale
        for t in range(8):
            tile = product[:, t * 128 : (t + 1) * 128]
            blocks = swap_lane_groups([tile[k * 32 : (k + 1) * 32] for k in range(4)], low, even)
            for j in range(4):
                at = (t * 4 + j) * 32
                joined[at : at + 32, q * 128 : (q + 1) * 128] = blocks[j].astype(BF16)
    for j in range(0, 32, 8):
        rows = dot(joined[j * 32 : (j + 8) * 32], weight[...])
        for k in range(8):
            update[:, j + k, :] = rows[k * 32 : (k + 1) * 32]
    out_ref[:, 0:32] = update[...].astype(BF16)

    first = iota((64, 16, 128), 1) // 8 == half_ref[0]
    kept, came = pair_ref[...].astype(F32), came_ref[...].astype(F32)
    pairs = jnp.where(first, jnp.concatenate([kept, kept], 1), jnp.concatenate([came, came], 1))
    out_ref[:, 32:64] = pairs.reshape(32, 32, 128).astype(BF16)


def attend_kernel(
    half_ref, got_ref, bias_ref, gain_ref, wq_ref, wk_ref, wv_ref, wg_ref, wo_ref, out_ref, q_s, k_s, v_s, mid_s, gate_s, done_s
):
    mine = half_ref[0] == 0
    factor = 32 ** (-0.5) * math.log2(math.e)
    head_of = iota((512, 128), 1) // 32
    zero, one = jnp.zeros((512, 128), BF16), jnp.ones((512, 128), BF16)
    row, source = iota((512, 512), 0), iota((512, 512), 1)
    for p in range(2):
        other = (row // 8) % 2 if p == 0 else 1 - (row // 8) % 2
        wanted = ((row // 16) % 4) * 128 + ((row // 2) % 4) * 32 + other * 16 + (row // 64) * 2 + row % 2
        update = got_ref[:, 0:32].reshape(4, 2, 4, 32, 128)[:, p].reshape(512, 128)
        pair = got_ref[:, 32:64].reshape(32, 2, 16, 128)[:, p].reshape(512, 128)
        pair_mid = dot(one_where(source == wanted), update) + pair.astype(F32) + bias_ref[...]
        pair_mid = pair_mid.astype(BF16).astype(F32)
        normed = layer_normalize(pair_mid, gain_ref[...])
        split = pair_mid.reshape(32, 2, 8, 128)
        mid_s[...] = jnp.where(mine, split[:, 0], split[:, 1]).reshape(256, 128)
        split = normed.reshape(32, 2, 8, 128)
        asking = jnp.where(mine, split[:, 0], split[:, 1]).reshape(256, 128).astype(BF16)
        normed = normed.astype(BF16)
        q_s[...] = dot(asking, wq_ref[...]).astype(BF16)
        gate_s[...] = dot(asking, wg_ref[...])
        k_s[...] = dot(normed, wk_ref[...]).astype(BF16)
        v_s[...] = dot(normed, wv_ref[...]).astype(BF16)
        keys, values = k_s[...], v_s[...]
        head_keys = [jnp.where(head_of == h, keys, zero) for h in range(PAIR_HEADS)]
        head_values = [
            jnp.concatenate(
                [jnp.where(head_of == h, values, zero), jnp.where(head_of == h, one, zero)], 1
            )
            for h in range(PAIR_HEADS)
        ]
        for c in range(2):
            at = slice(c * 128, (c + 1) * 128)
            queries = q_s[at, :]
            total = jnp.zeros((128, 256), F32)
            for h in range(PAIR_HEADS):
                scores = dot(queries, head_keys[h], 1, 1)
                top = jnp.max(scores, -1, keepdims=True)
                weights = jnp.exp2((scores - top) * factor).astype(BF16)
                total = total + dot(weights, head_values[h])
            attended = total[:, :128] / total[:, 128:] * jax.nn.sigmoid(gate_s[at, :])
            result = mid_s[at, :] + dot(attended.astype(BF16), wo_ref[...])
            done_s[c * 16 : (c + 1) * 16, p * 8 : (p + 1) * 8] = result.reshape(16, 8, 128)
    out_ref[...] = done_s[...].astype(BF16)


def node_kernel(
    count_ref, got_ref, index_ref, query_ref, nodes_ref, coords_ref, wo_ref, penalty_ref, step_ref, nodes_out, coords_out
):
    kv_table = got_ref[:, 64:80].reshape(512, 128)
    place_table = got_ref[:, 80:96].reshape(512, 128)
    local, slots = index_ref.shape
    width, dim = nodes_ref.shape[1], nodes_ref.shape[1] // NODE_HEADS
    lane = iota((1, slots), 1)
    spot = iota((1, local), 1)
    mixed = jnp.zeros((width, local), F32)
    moved = jnp.zeros((3, local), F32)
    for i in range(local):
        picked = one_where(iota((512, slots), 0) == index_ref[i : i + 1, :])
        near = dot(kv_table, picked, 0, 0)
        where = dot(place_table, picked, 0, 0)
        position = [
            where[3 * c : 3 * c + 1] + where[3 * c + 1 : 3 * c + 2] + where[3 * c + 2 : 3 * c + 3]
            for c in range(3)
        ]
        offsets = jnp.concatenate(position, 0) - coords_ref[:, i : i + 1]
        dist2 = jnp.sum(offsets * offsets, 0, keepdims=True)
        products = near[:width] * query_ref[:, i : i + 1]
        logits = jnp.sum(products.reshape(NODE_HEADS, dim, slots), 1) * dim ** (-0.5)
        logits = logits - penalty_ref[...] * dist2
        valid = lane < count_ref[i]
        logits = jnp.where(valid, logits, -1e30)
        powers = jnp.exp(logits - jnp.max(logits, -1, keepdims=True))
        weight = powers / jnp.sum(powers, -1, keepdims=True)
        weight = jnp.where(valid, weight, 0.0)
        low = weight.astype(BF16).astype(F32)
        spread = jnp.broadcast_to(low[:, None, :], (NODE_HEADS, dim, slots)).reshape(width, slots)
        column = jnp.sum(near[width:] * spread, -1, keepdims=True)
        mixed = mixed + jnp.where(spot == i, column, 0.0)
        pull = jnp.sum(weight * step_ref[...], 0, keepdims=True)
        moved = moved + jnp.where(spot == i, jnp.sum(offsets * pull, -1, keepdims=True), 0.0)
    out = nodes_ref[...].astype(F32) + dot(mixed.astype(BF16), wo_ref[...], 0, 0)
    nodes_out[...] = out.astype(BF16)
    coords_out[...] = coords_ref[...] + moved


def with_fetch(body, count):
    def kernel(*refs):
        sources, held, sems = refs[:count], refs[-count - 1 : -1], refs[-1]
        copies = [pltpu.make_async_copy(sources[i], held[i], sems.at[i]) for i in range(count)]
        for copy in copies:
            copy.start()
        for copy in copies:
            copy.wait()
        body(*held, *refs[count : -count - 1])

    return kernel


def call(body, out_shape, args, scratch=(), fetch=False):
    scratch = list(scratch)
    if fetch:
        body = with_fetch(body, len(args))
        scratch += [pltpu.VMEM(a.shape, a.dtype) for a in args] + [pltpu.SemaphoreType.DMA((len(args),))]
    space = pltpu.HBM if fetch else pltpu.VMEM
    return pl.pallas_call(
        body,
        out_shape=out_shape,
        in_specs=[pl.BlockSpec(memory_space=pltpu.SMEM if a.ndim == 1 else space) for a in args],
        out_specs=jax.tree.map(lambda _: pl.BlockSpec(memory_space=pltpu.VMEM), out_shape),
        scratch_shapes=scratch,
        compiler_params=pltpu.CompilerParams(vmem_limit_bytes=FETCH_LIMIT if fetch else VMEM_LIMIT),
    )(*args)


def shape(dims, kind=BF16):
    return jax.ShapeDtypeStruct(dims, kind)


def on_device(
    homolog_activations,
    alignment_token_ids,
    symbol_lookup_matrix,
    homolog_rescale_vector,
    first_operand_projection,
    second_operand_projection,
    outer_output_weight,
    outer_bias,
    pair,
    pair_norm_gain,
    pair_query_weight,
    pair_key_weight,
    pair_value_weight,
    pair_gate_weight,
    pair_output_weight,
    nodes,
    coords,
    neighbour_index,
    neighbour_count,
    node_norm_gain,
    node_query_weight,
    node_key_weight,
    node_value_weight,
    node_output_weight,
    distance_penalty,
    coordinate_step,
):
    half = lax.axis_index("zh").reshape(1).astype(jnp.int32)
    swap, node_query = call(
        first_kernel,
        (shape((144, 128)), shape((64, 8), F32)),
        (
            homolog_activations,
            alignment_token_ids,
            symbol_lookup_matrix.T,
            homolog_rescale_vector.reshape(1, -1),
            nodes,
            coords,
            node_norm_gain.reshape(1, -1),
            node_query_weight,
            node_key_weight,
            node_value_weight,
        ),
        fetch=True,
    )
    swapped = lax.ppermute(swap, "zh", [(0, 1), (1, 0)])
    given, _ = lax.optimization_barrier((pair, swap))
    slots = jnp.stack([jnp.where(half[0] == 1, given, 0), jnp.where(half[0] == 0, given, 0)])
    came = lax.psum_scatter(slots, "zh", scatter_dimension=0, tiled=False)
    spread = call(
        spread_kernel,
        shape((32, 96, 128)),
        (half, swap, swapped, first_operand_projection.T, second_operand_projection.T),
    )
    got = lax.all_to_all(spread, PLANE, split_axis=0, concat_axis=0, tiled=True)
    right = call(right_kernel, shape((8, 128, 128)), (got,))
    right = lax.all_to_all(right, "row", split_axis=0, concat_axis=0, tiled=True)
    other = lax.ppermute(right, "core", [(0, 1), (1, 0)])
    rows = call(
        outer_kernel,
        shape((32, 64, 128)),
        (half, got, right, other, pair, came, outer_output_weight),
        scratch=(
            pltpu.VMEM((256, 1024), BF16),
            pltpu.VMEM((256, 1024), BF16),
            pltpu.VMEM((1024, 1024), BF16),
            pltpu.VMEM((1024, 128), BF16),
            pltpu.VMEM((32, 32, 128), F32),
        ),
    )
    rows = lax.all_to_all(rows, PLANE, split_axis=0, concat_axis=0, tiled=True)
    done = call(
        attend_kernel,
        shape((32, 16, 128)),
        (
            half,
            rows,
            outer_bias.reshape(1, -1),
            pair_norm_gain.reshape(1, -1),
            pair_query_weight,
            pair_key_weight,
            pair_value_weight,
            pair_gate_weight,
            pair_output_weight,
        ),
        scratch=(
            pltpu.VMEM((256, 128), BF16),
            pltpu.VMEM((512, 128), BF16),
            pltpu.VMEM((512, 128), BF16),
            pltpu.VMEM((256, 128), F32),
            pltpu.VMEM((256, 128), F32),
            pltpu.VMEM((32, 16, 128), F32),
        ),
    )
    done = lax.all_to_all(done, PLANE, split_axis=0, concat_axis=0, tiled=True)
    pair_out = done.reshape(pair.shape)
    nodes_out, coords_out = call(
        node_kernel,
        (shape(nodes.shape), shape(coords.shape, F32)),
        (
            neighbour_count,
            got,
            neighbour_index,
            node_query,
            nodes,
            coords,
            node_output_weight,
            distance_penalty.reshape(-1, 1),
            coordinate_step.reshape(-1, 1),
        ),
    )
    return (pair_out, nodes_out, coords_out)


def solution(mesh):
    fine = Mesh(mesh.devices.reshape(4, 2, 8, 4, 2), ("x", "core", "row", "y", "zh"))
    placed = (
        P(GROUP, "row", None),
        P(GROUP, "row"),
        P(),
        P(),
        P(),
        P(),
        P(),
        P(),
        P("row", GROUP, None),
        P(),
        P(),
        P(),
        P(),
        P(),
        P(),
        P(GROUP, None),
        P(None, GROUP),
        P(GROUP, None),
        P(GROUP),
        P(),
        P(),
        P(),
        P(),
        P(),
        P(),
        P(),
    )
    return jax.shard_map(
        on_device,
        mesh=fine,
        in_specs=placed,
        out_specs=(
            P("row", GROUP, None),
            P(GROUP, None),
            P(None, GROUP),
        ),
        check_vma=False,
    )
```

time: 132 us -> 153 us (1.16)
  the two profiles are of different devices: /device:TPU:33 before, /device:TPU:1 now
where the time goes in v4:
time: 153 us; the launch traced here: 152 us
  blocking collectives  40.4 us (26%)
  starting transfers between devices  37.8 us (25%)
  waiting for transfers between devices  36.7 us (24%)
  Pallas kernels  17.8 us (12%)
  between operations  14.2 us (9%)
  local copies, waits for them, and re-layouts  4.46 us (3%)
    all_to_all x1, blocking collectives, on_device(): got = lax.all_to_all(spread, PLANE, split_axis=0, concat_axis=0, tiled=True)  22 us
    reduce_scatter x1, waiting for transfers between devices, on_device(): came = lax.psum_scatter(slots, 'zh', scatter_dimension=0, tiled=False)  20.2 us
    all_to_all x1, blocking collectives, on_device(): rows = lax.all_to_all(rows, PLANE, split_axis=0, concat_axis=0, tiled=True)  18.4 us
    pallas_call x6, Pallas kernels, call(): pl.pallas_call(body, out_shape=out_shape, in_specs=[pl.BlockSpec(memory_s...  17.8 us
    ppermute x1, starting transfers between devices, on_device(): swapped = lax.ppermute(swap, 'zh', [(0, 1), (1, 0)])  16.3 us
    all_to_all x1, waiting for transfers between devices, on_device(): lax.all_to_all(right, 'row', split_axis=0, concat_axis=0, tiled=True)  10.9 us
    all_to_all x1, starting transfers between devices, on_device(): lax.all_to_all(right, 'row', split_axis=0, concat_axis=0, tiled=True)  9.15 us
    ppermute x1, starting transfers between devices, on_device(): other = lax.ppermute(right, 'core', [(0, 1), (1, 0)])  7.73 us
  transfers between devices with their start and end apart: 5, of which 4 were waited for; matrix products, arithmetic and copies ran while one was open for 1% of the time, Pallas kernels for 2%

profile of v4, /device:TPU:1, one launch (start us, length us, event | category | flops | bytes accessed | tf_op | source)
XLA Modules:
  0.0 152.1 jit_solution(10702182488210534625)
XLA Ops:
  7.2 2.2 %shard_map.265 = (bf16[144,128]{1,0:T(8,128)(2,1)}, f32[64,8]{1,0:T(8,128)}) custom-call(bf16[4,64,64]{2,1,0:T(8,128)(2,1)} %refs_0_.1, s32[4,64]{1,0:T(4,128)} %refs_1_.1, bf16[64,80]{1,0:T(8,128)(2,1)} %bitcast.22, f32[1,64]{1,0:T(1,128)} %bitcast.23, bf16[8,64]{1,0:T(8,128)(2,1)} %nodes_ref.1, f32[3,8]{1,0:T(4,128)} %coords_ref.1, f32[1,64]{1,0:T(1,128)} %bitcast.24, ...), custom_call_target="tpu_custom_call" | custom-call | tf_op jit(solution)/shard_map/pallas_call | solution.py:303
  9.4 0.0 copy-start.11
  9.4 16.3 %collective-permute-start = (bf16[144,128]{1,0:T(8,128)(2,1)}, bf16[144,128]{1,0:T(8,128)(2,1)S(1)}, u32[]{:S(2)}, u32[]{:S(2)}) collective-permute-start(bf16[144,128]{1,0:T(8,128)(2,1)} %get-tuple-element.8.own_ref), channel_id=1, source_target_pairs={{0,1},{1,0},{2,3},{3,2},{4,5},{5,4},{6,7},{7,6},{8,9},{9,8},{10,11... | collective-permute-start | bytes 110600 | tf_op jit(solution)/shard_map/ppermute | solution.py:363
  25.7 1.7 %collective-permute-done.got_ref = bf16[144,128]{1,0:T(8,128)(2,1)S(1)} collective-permute-done((bf16[144,128]{1,0:T(8,128)(2,1)}, bf16[144,128]{1,0:T(8,128)(2,1)S(1)}, u32[]{:S(2)}, u32[]{:S(2)}) %collective-permute-start) | collective-permute-done | bytes 36896 | tf_op jit(solution)/shard_map/ppermute | solution.py:363
  27.4 0.8 copy-done.3
  28.1 1.2 shard_map.266
  29.3 22.0 %all_to_all.20.got_ref = bf16[32,96,128]{2,1,0:T(8,128)(2,1)S(1)} all-to-all(bf16[32,96,128]{2,1,0:T(8,128)(2,1)S(1)} %shard_map.266), channel_id=1, replica_groups=mesh['x'=4,'core'=2,'row'=8,'y'=4,'zh'=2] {'x','core','y'}, dimensions={0} | all-to-all | bytes 1572864 | tf_op jit(solution)/shard_map/all_to_all | solution.py:372
  51.3 1.2 shard_map.267
  52.5 9.2 %all-to-all-start.1 = ((bf16[8,128,128]{2,1,0:T(8,128)(2,1)}), bf16[8,128,128]{2,1,0:T(8,128)(2,1)S(1)}, u32[]{:S(2)}, u32[]{:S(2)}) async-start(bf16[8,128,128]{2,1,0:T(8,128)(2,1)} %shard_map.267), calls=%async_computation.1 | async-start | bytes 524288 | tf_op jit(solution)/shard_map/all_to_all | solution.py:374
  61.7 0.0 reduce-scatter.2.cloned.1.call-start
  61.8 0.7 pad_maximum_fusion
  62.5 0.0 reduce-scatter.2.cloned.1.call-update
  62.5 10.9 %all-to-all-done.1.right_in = bf16[8,128,128]{2,1,0:T(8,128)(2,1)S(1)} async-done(((bf16[8,128,128]{2,1,0:T(8,128)(2,1)}), bf16[8,128,128]{2,1,0:T(8,128)(2,1)S(1)}, u32[]{:S(2)}, u32[]{:S(2)}) %all-to-all-start.1) | async-done | bytes 262176 | tf_op jit(solution)/shard_map/all_to_all | solution.py:374
  73.5 7.7 %collective-permute-start.1 = (bf16[8,128,128]{2,1,0:T(8,128)(2,1)S(1)}, bf16[8,128,128]{2,1,0:T(8,128)(2,1)S(1)}, u32[]{:S(2)}, u32[]{:S(2)}) collective-permute-start(bf16[8,128,128]{2,1,0:T(8,128)(2,1)S(1)} %all-to-all-done.1.right_in), channel_id=1, source_target_pairs={{0,64},{64,0},{1,65},{65,1},{2,66},{66,2},{3,67},{67,3},{4,68},{68... | collective-permute-start | bytes 786440 | tf_op jit(solution)/shard_map/ppermute | solution.py:375
  81.2 20.2 %reduce-scatter.2.cloned.1.call-done = bf16[1,64,8,128]{3,2,1,0:T(8,128)(2,1)} async-done(((bf16[2,64,8,128]{3,2,1,0:T(8,128)(2,1)}), bf16[1,64,8,128]{3,2,1,0:T(8,128)(2,1)}) %reduce-scatter.2.cloned.1.call-update) | async-done | bytes 131088 | tf_op jit(solution)/shard_map/reduce_scatter | solution.py:366
  101.5 0.9 copy-done.2
  102.4 5.8 %shard_map.268 = bf16[32,64,128]{2,1,0:T(8,128)(2,1)S(1)} custom-call(s32[1]{0:T(128)} %bitcast.half_ref, bf16[32,96,128]{2,1,0:T(8,128)(2,1)S(1)} %all_to_all.20.got_ref, bf16[8,128,128]{2,1,0:T(8,128)(2,1)S(1)} %all-to-all-done.1.right_in, bf16[8,128,128]{2,1,0:T(8,128)(2,1)S(1)} %collective-permute-done.1.other_in, bf16[64,8,128]{2,1,0:T(8,128)(2,1)S(1)} %copy-done, ...), custom_call_target="tpu_custom_call" | custom-call | tf_op jit(solution)/shard_map/pallas_call | solution.py:303
  108.2 0.0 copy-start.6
  108.2 18.4 %all_to_all.21.got_ref = bf16[32,64,128]{2,1,0:T(8,128)(2,1)S(1)} all-to-all(bf16[32,64,128]{2,1,0:T(8,128)(2,1)S(1)} %shard_map.268), channel_id=1, replica_groups=mesh['x'=4,'core'=2,'row'=8,'y'=4,'zh'=2] {'x','core','y'}, dimensions={0} | all-to-all | bytes 1048576 | tf_op jit(solution)/shard_map/all_to_all | solution.py:388
  126.7 0.6 copy-done.16
  127.3 0.0 copy-done.17
  127.3 5.0 %shard_map.269 = bf16[32,16,128]{2,1,0:T(8,128)(2,1)} custom-call(s32[1]{0:T(128)} %bitcast.half_ref, bf16[32,64,128]{2,1,0:T(8,128)(2,1)S(1)} %all_to_all.21.got_ref, f32[1,128]{1,0:T(1,128)S(1)} %bitcast.19, f32[1,128]{1,0:T(1,128)S(1)} %bitcast.20, bf16[128,128]{1,0:T(8,128)(2,1)S(1)} %copy-done.4, bf16[128,128]{1,0:T(8,128)(2,1)S(1)} %copy-done.5, ...), custom_call_target="tpu_custom_call" | custom-call | tf_op jit(solution)/shard_map/pallas_call | solution.py:303
  132.3 4.7 %all-to-all-start.3 = ((bf16[32,16,128]{2,1,0:T(8,128)(2,1)}), bf16[32,16,128]{2,1,0:T(8,128)(2,1)S(1)}, u32[]{:S(2)}, u32[]{:S(2)}) async-start(bf16[32,16,128]{2,1,0:T(8,128)(2,1)} %shard_map.269), calls=%async_computation.4 | async-start | bytes 262144 | tf_op jit(solution)/shard_map/all_to_all | solution.py:412
  137.0 0.6 copy-done.19
  137.6 0.1 copy.29.penalty_ref
  137.7 0.1 copy.30.step_ref
  137.8 0.5 copy-done.15
  138.3 0.1 copy-done.13
  138.4 0.0 copy-done.14
  138.4 2.4 %shard_map.270 = (bf16[8,64]{1,0:T(8,128)(2,1)}, f32[3,8]{1,0:T(4,128)}) custom-call(s32[8]{0:T(128)S(1)} %copy-done.18, bf16[32,96,128]{2,1,0:T(8,128)(2,1)S(1)} %all_to_all.20.got_ref, s32[8,64]{1,0:T(8,128)S(1)} %copy-done.15, f32[64,8]{1,0:T(8,128)S(1)} %copy-done.9, bf16[8,64]{1,0:T(8,128)(2,1)S(1)} %copy-done.13, f32[3,8]{1,0:T(4,128)S(1)} %copy-done.14, ...), custom_call_target="tpu_custom_call" | custom-call | tf_op jit(solution)/shard_map/pallas_call | solution.py:303
  140.8 3.8 %all-to-all-done.3 = bf16[32,16,128]{2,1,0:T(8,128)(2,1)S(1)} async-done(((bf16[32,16,128]{2,1,0:T(8,128)(2,1)}), bf16[32,16,128]{2,1,0:T(8,128)(2,1)S(1)}, u32[]{:S(2)}, u32[]{:S(2)}) %all-to-all-start.3) | async-done | bytes 131104 | tf_op jit(solution)/shard_map/all_to_all | solution.py:412
  144.6 0.7 copy.32
  (34 shorter events, 0.1 us)
Async XLA Ops:
  7.2 20.2 %copy-start.12 = (bf16[64,32]{0,1:T(8,128)(2,1)S(1)}, bf16[64,32]{0,1:T(8,128)(2,1)}, u32[]{:S(2)}) copy-start(bf16[64,32]{0,1:T(8,128)(2,1)} %param.31) | copy-start | bytes 12292
  9.4 18.0 %copy-start.11 = (bf16[64,32]{0,1:T(8,128)(2,1)S(1)}, bf16[64,32]{0,1:T(8,128)(2,1)}, u32[]{:S(2)}) copy-start(bf16[64,32]{0,1:T(8,128)(2,1)} %param.30) | copy-start | bytes 12292
  9.4 18.0 %collective-permute-start = (bf16[144,128]{1,0:T(8,128)(2,1)}, bf16[144,128]{1,0:T(8,128)(2,1)S(1)}, u32[]{:S(2)}, u32[]{:S(2)}) collective-permute-start(bf16[144,128]{1,0:T(8,128)(2,1)} %get-tuple-element.8.own_ref), channel_id=1, source_target_pairs={{0,1},{1,0},{2,3},{3,2},{4,5},{5,4},{6,7},{7,6},{8,9},{9,8},{10,11... | collective-permute-start | bytes 110600 | tf_op jit(solution)/shard_map/ppermute | solution.py:363
  27.4 0.8 copy-start.3
  52.5 9.2 %copy-start = (bf16[64,8,128]{2,1,0:T(8,128)(2,1)S(1)}, bf16[64,8,128]{2,1,0:T(8,128)(2,1)}, u32[]{:S(2)}) copy-start(bf16[64,8,128]{2,1,0:T(8,128)(2,1)} %pair_ref.1) | copy-start | bytes 393220
  52.5 21.0 %all-to-all-start.1 = ((bf16[8,128,128]{2,1,0:T(8,128)(2,1)}), bf16[8,128,128]{2,1,0:T(8,128)(2,1)S(1)}, u32[]{:S(2)}, u32[]{:S(2)}) async-start(bf16[8,128,128]{2,1,0:T(8,128)(2,1)} %shard_map.267), calls=%async_computation.1 | async-start | bytes 524288 | tf_op jit(solution)/shard_map/all_to_all | solution.py:374
  61.7 39.8 %reduce-scatter.2.cloned.1.call-start = ((), (), s32[]{:S(2)}) async-start(), calls=%async_computation.5 | async-start | bytes 393216 | tf_op jit(solution)/shard_map/reduce_scatter | solution.py:366
  62.5 38.9 %copy-start.1 = (bf16[1024,128]{1,0:T(8,128)(2,1)S(1)}, bf16[1024,128]{1,0:T(8,128)(2,1)}, u32[]{:S(2)}) copy-start(bf16[1024,128]{1,0:T(8,128)(2,1)} %weight_ref.1) | copy-start | bytes 786436
  73.5 28.0 %collective-permute-start.1 = (bf16[8,128,128]{2,1,0:T(8,128)(2,1)S(1)}, bf16[8,128,128]{2,1,0:T(8,128)(2,1)S(1)}, u32[]{:S(2)}, u32[]{:S(2)}) collective-permute-start(bf16[8,128,128]{2,1,0:T(8,128)(2,1)S(1)} %all-to-all-done.1.right_in), channel_id=1, source_target_pairs={{0,64},{64,0},{1,65},{65,1},{2,66},{66,2},{3,67},{67,3},{4,68},{68... | collective-permute-start | bytes 786440 | tf_op jit(solution)/shard_map/ppermute | solution.py:375
  101.5 0.9 copy-start.2
  108.2 18.5 %copy-start.4 = (bf16[128,128]{1,0:T(8,128)(2,1)S(1)}, bf16[128,128]{1,0:T(8,128)(2,1)}, u32[]{:S(2)}) copy-start(bf16[128,128]{1,0:T(8,128)(2,1)} %wq_ref.1) | copy-start | bytes 98308
  108.2 18.5 %copy-start.5 = (bf16[128,128]{1,0:T(8,128)(2,1)S(1)}, bf16[128,128]{1,0:T(8,128)(2,1)}, u32[]{:S(2)}) copy-start(bf16[128,128]{1,0:T(8,128)(2,1)} %wk_ref.1) | copy-start | bytes 98308
  108.2 18.5 %copy-start.6 = (bf16[128,128]{1,0:T(8,128)(2,1)S(1)}, bf16[128,128]{1,0:T(8,128)(2,1)}, u32[]{:S(2)}) copy-start(bf16[128,128]{1,0:T(8,128)(2,1)} %wv_ref.1) | copy-start | bytes 98308
  108.2 18.5 %copy-start.7 = (bf16[128,128]{1,0:T(8,128)(2,1)S(1)}, bf16[128,128]{1,0:T(8,128)(2,1)}, u32[]{:S(2)}) copy-start(bf16[128,128]{1,0:T(8,128)(2,1)} %wg_ref.1) | copy-start | bytes 98308
  108.2 18.4 %copy-start.8 = (bf16[128,128]{1,0:T(8,128)(2,1)S(1)}, bf16[128,128]{1,0:T(8,128)(2,1)}, u32[]{:S(2)}) copy-start(bf16[128,128]{1,0:T(8,128)(2,1)} %wo_ref.2) | copy-start | bytes 98308
  126.6 0.7 copy-start.16
  126.6 0.7 copy-start.17
  132.3 5.4 %copy-start.20 = (f32[4]{0:T(128)S(1)}, f32[4]{0:T(128)}, u32[]{:S(2)}) copy-start(f32[4]{0:T(128)} %param.51) | copy-start | bytes 52
  132.3 5.5 %copy-start.9 = (f32[64,8]{1,0:T(8,128)S(1)}, f32[64,8]{1,0:T(8,128)}, u32[]{:S(2)}) copy-start(f32[64,8]{1,0:T(8,128)} %get-tuple-element.10.query_ref) | copy-start | bytes 6148
  132.3 5.5 %copy-start.10 = (bf16[64,64]{1,0:T(8,128)(2,1)S(1)}, bf16[64,64]{1,0:T(8,128)(2,1)}, u32[]{:S(2)}) copy-start(bf16[64,64]{1,0:T(8,128)(2,1)} %wo_ref.3) | copy-start | bytes 24580
  132.3 5.5 %copy-start.18 = (s32[8]{0:T(128)S(1)}, s32[8]{0:T(128)}, u32[]{:S(2)}) copy-start(s32[8]{0:T(128)} %count_ref.1) | copy-start | bytes 100
  132.3 12.3 %all-to-all-start.3 = ((bf16[32,16,128]{2,1,0:T(8,128)(2,1)}), bf16[32,16,128]{2,1,0:T(8,128)(2,1)S(1)}, u32[]{:S(2)}, u32[]{:S(2)}) async-start(bf16[32,16,128]{2,1,0:T(8,128)(2,1)} %shard_map.269), calls=%async_computation.4 | async-start | bytes 262144 | tf_op jit(solution)/shard_map/all_to_all | solution.py:412
  137.0 0.7 copy-start.19
  137.6 0.7 copy-start.15
  137.7 0.7 copy-start.13
  137.7 0.7 copy-start.14
Sparse Core Ops, SparseCore 0:
  65.3 36.1 reduce-scatter.1

commit v5 on v4

--- a/solution.py
+++ b/solution.py
@@ -14,7 +14,6 @@
 PLANE = ("x", "core", "y")
 GROUP = ("x", "core", "y", "zh")
 VMEM_LIMIT = 48 * 1024 * 1024
-FETCH_LIMIT = 56 * 1024 * 1024
 
 
 def dot(a, b, ca=1, cb=0):
@@ -65,9 +64,15 @@
     wq_ref,
     wk_ref,
     wv_ref,
+    bias_ref,
+    pair_gain_ref,
+    pair_ref,
     swap_ref,
     query_ref,
+    consts_ref,
 ):
+    swap_ref[144:656] = pair_ref[...]
+    consts_ref[...] = jnp.where(iota((8, 128), 0) == 0, bias_ref[...], pair_gain_ref[...])
     seqs, length, _ = act_ref.shape
     kinds = emb_ref.shape[1]
     emb = emb_ref[...]
@@ -96,7 +101,7 @@
 
 def spread_kernel(half_ref, own_ref, got_ref, wl_ref, wr_ref, out_ref):
     mine = half_ref[0] == 0
-    own, came = own_ref[...].astype(F32), got_ref[...].astype(F32)
+    own, came = own_ref[0:144].astype(F32), got_ref[0:144].astype(F32)
     one = jnp.where(mine, own, came)
     two = jnp.where(mine, came, own)
     row, lane = iota((128, 64), 0), iota((128, 64), 1)
@@ -188,13 +193,13 @@
     out_ref[:, 0:32] = update[...].astype(BF16)
 
     first = iota((64, 16, 128), 1) // 8 == half_ref[0]
-    kept, came = pair_ref[...].astype(F32), came_ref[...].astype(F32)
+    kept, came = pair_ref[...].astype(F32), came_ref[144:656].reshape(64, 8, 128).astype(F32)
     pairs = jnp.where(first, jnp.concatenate([kept, kept], 1), jnp.concatenate([came, came], 1))
     out_ref[:, 32:64] = pairs.reshape(32, 32, 128).astype(BF16)
 
 
 def attend_kernel(
-    half_ref, got_ref, bias_ref, gain_ref, wq_ref, wk_ref, wv_ref, wg_ref, wo_ref, out_ref, q_s, k_s, v_s, mid_s, gate_s, done_s
+    half_ref, got_ref, consts_ref, wq_ref, wk_ref, wv_ref, wg_ref, wo_ref, out_ref, q_s, k_s, v_s, mid_s, gate_s, done_s
 ):
     mine = half_ref[0] == 0
     factor = 32 ** (-0.5) * math.log2(math.e)
@@ -206,9 +211,9 @@
         wanted = ((row // 16) % 4) * 128 + ((row // 2) % 4) * 32 + other * 16 + (row // 64) * 2 + row % 2
         update = got_ref[:, 0:32].reshape(4, 2, 4, 32, 128)[:, p].reshape(512, 128)
         pair = got_ref[:, 32:64].reshape(32, 2, 16, 128)[:, p].reshape(512, 128)
-        pair_mid = dot(one_where(source == wanted), update) + pair.astype(F32) + bias_ref[...]
+        pair_mid = dot(one_where(source == wanted), update) + pair.astype(F32) + consts_ref[0:1]
         pair_mid = pair_mid.astype(BF16).astype(F32)
-        normed = layer_normalize(pair_mid, gain_ref[...])
+        normed = layer_normalize(pair_mid, consts_ref[1:2])
         split = pair_mid.reshape(32, 2, 8, 128)
         mid_s[...] = jnp.where(mine, split[:, 0], split[:, 1]).reshape(256, 128)
         split = normed.reshape(32, 2, 8, 128)
@@ -299,6 +304,7 @@
     if fetch:
         body = with_fetch(body, len(args))
         scratch += [pltpu.VMEM(a.shape, a.dtype) for a in args] + [pltpu.SemaphoreType.DMA((len(args),))]
+        args = [pltpu.with_memory_space_constraint(a, pltpu.HBM) for a in args]
     space = pltpu.HBM if fetch else pltpu.VMEM
     return pl.pallas_call(
         body,
@@ -306,7 +312,7 @@
         in_specs=[pl.BlockSpec(memory_space=pltpu.SMEM if a.ndim == 1 else space) for a in args],
         out_specs=jax.tree.map(lambda _: pl.BlockSpec(memory_space=pltpu.VMEM), out_shape),
         scratch_shapes=scratch,
-        compiler_params=pltpu.CompilerParams(vmem_limit_bytes=FETCH_LIMIT if fetch else VMEM_LIMIT),
+        compiler_params=pltpu.CompilerParams(vmem_limit_bytes=VMEM_LIMIT),
     )(*args)
 
 
@@ -343,9 +349,9 @@
     coordinate_step,
 ):
     half = lax.axis_index("zh").reshape(1).astype(jnp.int32)
-    swap, node_query = call(
+    swap, node_query, consts = call(
         first_kernel,
-        (shape((144, 128)), shape((64, 8), F32)),
+        (shape((656, 128)), shape((64, 8), F32), shape((8, 128), F32)),
         (
             homolog_activations,
             alignment_token_ids,
@@ -357,13 +363,13 @@
             node_query_weight,
             node_key_weight,
             node_value_weight,
+            outer_bias.reshape(1, -1),
+            pair_norm_gain.reshape(1, -1),
+            pair.reshape(512, 128),
         ),
         fetch=True,
     )
     swapped = lax.ppermute(swap, "zh", [(0, 1), (1, 0)])
-    given, _ = lax.optimization_barrier((pair, swap))
-    slots = jnp.stack([jnp.where(half[0] == 1, given, 0), jnp.where(half[0] == 0, given, 0)])
-    came = lax.psum_scatter(slots, "zh", scatter_dimension=0, tiled=False)
     spread = call(
         spread_kernel,
         shape((32, 96, 128)),
@@ -376,7 +382,7 @@
     rows = call(
         outer_kernel,
         shape((32, 64, 128)),
-        (half, got, right, other, pair, came, outer_output_weight),
+        (half, got, right, other, pair, swapped, outer_output_weight),
         scratch=(
             pltpu.VMEM((256, 1024), BF16),
             pltpu.VMEM((256, 1024), BF16),
@@ -392,8 +398,7 @@
         (
             half,
             rows,
-            outer_bias.reshape(1, -1),
-            pair_norm_gain.reshape(1, -1),
+            consts,
             pair_query_weight,
             pair_key_weight,
             pair_value_weight,

time: 153 us -> 124 us (0.81)
  waiting for transfers between devices: 36.7 us -> 9.18 us
  blocking collectives: 40.4 us -> 66 us
  between operations: 14.2 us -> 0.8 us
  starting transfers between devices: 37.8 us -> 28.7 us
  local copies, waits for them, and re-layouts: 4.46 us -> 2.16 us
    all_to_all x0 -> x1, blocking collectives: none -> 29 us  [on_device(): lax.all_to_all(right, 'row', split_axis=0, concat_axis=0, tiled=True)]
    reduce_scatter x1 -> x0, waiting for transfers between devices: 20.2 us -> none  [on_device(): came = lax.psum_scatter(slots, 'zh', scatter_dimension=0, tiled=False)]
    all_to_all x1 -> x0, waiting for transfers between devices: 10.9 us -> none  [on_device(): lax.all_to_all(right, 'row', split_axis=0, concat_axis=0, tiled=True)]
    all_to_all x1 -> x0, starting transfers between devices: 9.15 us -> none  [on_device(): lax.all_to_all(right, 'row', split_axis=0, concat_axis=0, tiled=True)]
    all_to_all x1, blocking collectives: 18.4 us -> 15.3 us  [on_device(): rows = lax.all_to_all(rows, PLANE, split_axis=0, concat_axis=0, tiled=True)]
    ppermute x1, waiting for transfers between devices: 1.67 us -> 4.21 us  [on_device(): swapped = lax.ppermute(swap, 'zh', [(0, 1), (1, 0)])]
    unnamed x43 -> x33, local copies, waits for them, and re-layouts: 4.27 us -> 1.97 us
  transfers between devices with their start and end apart: 5 -> 3, of which waited for: 4 -> 3; matrix products, arithmetic and copies ran while one was open for 1% -> 0% of each run, Pallas kernels for 2% -> 2%
where the time goes in v5:
time: 124 us; the launch traced here: 123 us
  blocking collectives  66 us (53%)
  starting transfers between devices  28.7 us (23%)
  Pallas kernels  16.7 us (13%)
  waiting for transfers between devices  9.18 us (7%)
  local copies, waits for them, and re-layouts  2.16 us (2%)
    all_to_all x1, blocking collectives, on_device(): lax.all_to_all(right, 'row', split_axis=0, concat_axis=0, tiled=True)  29 us
    all_to_all x1, blocking collectives, on_device(): got = lax.all_to_all(spread, PLANE, split_axis=0, concat_axis=0, tiled=True)  21.7 us
    pallas_call x6, Pallas kernels, call(): pl.pallas_call(body, out_shape=out_shape, in_specs=[pl.BlockSpec(memory_s...  16.7 us
    ppermute x1, starting transfers between devices, on_device(): swapped = lax.ppermute(swap, 'zh', [(0, 1), (1, 0)])  16.3 us
    all_to_all x1, blocking collectives, on_device(): rows = lax.all_to_all(rows, PLANE, split_axis=0, concat_axis=0, tiled=True)  15.3 us
    ppermute x1, starting transfers between devices, on_device(): other = lax.ppermute(right, 'core', [(0, 1), (1, 0)])  7.73 us
    all_to_all x1, starting transfers between devices, on_device(): done = lax.all_to_all(done, PLANE, split_axis=0, concat_axis=0, tiled=True)  4.65 us
    ppermute x1, waiting for transfers between devices, on_device(): swapped = lax.ppermute(swap, 'zh', [(0, 1), (1, 0)])  4.21 us
  transfers between devices with their start and end apart: 3, of which 3 were waited for; matrix products, arithmetic and copies ran while one was open for 0% of the time, Pallas kernels for 2%

profile of v5, /device:TPU:1, one launch (start us, length us, event | category | flops | bytes accessed | tf_op | source)
XLA Modules:
  0.0 123.5 jit_solution(8877998146102901420)
XLA Ops:
  0.6 1.8 %shard_map.265 = (bf16[656,128]{1,0:T(8,128)(2,1)S(1)}, f32[64,8]{1,0:T(8,128)S(1)}, f32[8,128]{1,0:T(8,128)S(1)}) custom-call(bf16[4,64,64]{2,1,0:T(8,128)(2,1)} %refs_0_.1, s32[4,64]{1,0:T(4,128)} %refs_1_.1, bf16[64,80]{1,0:T(8,128)(2,1)} %bitcast.16, f32[1,64]{1,0:T(1,128)} %bitcast.17, bf16[8,64]{1,0:T(8,128)(2,1)} %nodes_ref.1, f32[3,8]{1,0:T(4,128)} %coords_ref.1, ...), custom_call_target="tpu_custom_call" | custom-call | tf_op jit(solution)/shard_map/pallas_call | solution.py:309
  2.5 0.0 copy-start.8
  2.5 16.3 %collective-permute-start = (bf16[656,128]{1,0:T(8,128)(2,1)S(1)}, bf16[656,128]{1,0:T(8,128)(2,1)S(1)}, u32[]{:S(2)}, u32[]{:S(2)}) collective-permute-start(bf16[656,128]{1,0:T(8,128)(2,1)S(1)} %get-tuple-element.8.own_ref), channel_id=1, source_target_pairs={{0,1},{1,0},{2,3},{3,2},{4,5},{5,4},{6,7},{7,6},{8,9},{9,8},{10,11... | collective-permute-start | bytes 503816 | tf_op jit(solution)/shard_map/ppermute | solution.py:372
  18.8 4.2 %collective-permute-done.got_ref.came_ref = bf16[656,128]{1,0:T(8,128)(2,1)S(1)} collective-permute-done((bf16[656,128]{1,0:T(8,128)(2,1)S(1)}, bf16[656,128]{1,0:T(8,128)(2,1)S(1)}, u32[]{:S(2)}, u32[]{:S(2)}) %collective-permute-start) | collective-permute-done | bytes 167968 | tf_op jit(solution)/shard_map/ppermute | solution.py:372
  23.0 1.2 shard_map.266
  24.2 21.7 %all_to_all.20.got_ref = bf16[32,96,128]{2,1,0:T(8,128)(2,1)S(1)} all-to-all(bf16[32,96,128]{2,1,0:T(8,128)(2,1)S(1)} %shard_map.266), channel_id=1, replica_groups=mesh['x'=4,'core'=2,'row'=8,'y'=4,'zh'=2] {'x','core','y'}, dimensions={0} | all-to-all | bytes 1572864 | tf_op jit(solution)/shard_map/all_to_all | solution.py:378
  45.9 0.5 shard_map.267
  46.5 0.0 copy-start
  46.5 0.0 copy-start.1
  46.5 29.0 %all_to_all.21.right_in = bf16[8,128,128]{2,1,0:T(8,128)(2,1)S(1)} all-to-all(bf16[8,128,128]{2,1,0:T(8,128)(2,1)S(1)} %shard_map.267), channel_id=1, replica_groups=mesh['x'=4,'core'=2,'row'=8,'y'=4,'zh'=2] {'row'}, dimensions={0} | all-to-all | bytes 524288 | tf_op jit(solution)/shard_map/all_to_all | solution.py:380
  75.5 7.7 %collective-permute-start.1 = (bf16[8,128,128]{2,1,0:T(8,128)(2,1)S(1)}, bf16[8,128,128]{2,1,0:T(8,128)(2,1)S(1)}, u32[]{:S(2)}, u32[]{:S(2)}) collective-permute-start(bf16[8,128,128]{2,1,0:T(8,128)(2,1)S(1)} %all_to_all.21.right_in), channel_id=1, source_target_pairs={{0,64},{64,0},{1,65},{65,1},{2,66},{66,2},{3,67},{67,3},{4,68},{68... | collective-permute-start | bytes 786440 | tf_op jit(solution)/shard_map/ppermute | solution.py:381
  83.2 1.1 collective-permute-done.1.other_in
  84.3 5.8 %shard_map.268 = bf16[32,64,128]{2,1,0:T(8,128)(2,1)S(1)} custom-call(s32[1]{0:T(128)} %bitcast.half_ref, bf16[32,96,128]{2,1,0:T(8,128)(2,1)S(1)} %all_to_all.20.got_ref, bf16[8,128,128]{2,1,0:T(8,128)(2,1)S(1)} %all_to_all.21.right_in, bf16[8,128,128]{2,1,0:T(8,128)(2,1)S(1)} %collective-permute-done.1.other_in, bf16[64,8,128]{2,1,0:T(8,128)(2,1)S(1)} %copy-done, ...), custom_call_target="tpu_custom_call" | custom-call | tf_op jit(solution)/shard_map/pallas_call | solution.py:309
  90.1 0.0 copy-start.2
  90.2 0.0 copy-start.3
  90.2 0.0 copy-start.4
  90.2 0.0 copy-start.5
  90.2 0.0 copy-start.6
  90.2 15.3 %all_to_all.22.got_ref = bf16[32,64,128]{2,1,0:T(8,128)(2,1)S(1)} all-to-all(bf16[32,64,128]{2,1,0:T(8,128)(2,1)S(1)} %shard_map.268), channel_id=1, replica_groups=mesh['x'=4,'core'=2,'row'=8,'y'=4,'zh'=2] {'x','core','y'}, dimensions={0} | all-to-all | bytes 1048576 | tf_op jit(solution)/shard_map/all_to_all | solution.py:394
  105.5 0.0 copy-done.3
  105.5 5.0 %shard_map.269 = bf16[32,16,128]{2,1,0:T(8,128)(2,1)} custom-call(s32[1]{0:T(128)} %bitcast.half_ref, bf16[32,64,128]{2,1,0:T(8,128)(2,1)S(1)} %all_to_all.22.got_ref, f32[8,128]{1,0:T(8,128)S(1)} %get-tuple-element.9.consts_ref, bf16[128,128]{1,0:T(8,128)(2,1)S(1)} %copy-done.2, bf16[128,128]{1,0:T(8,128)(2,1)S(1)} %copy-done.3, ...), custom_call_target="tpu_custom_call" | custom-call | tf_op jit(solution)/shard_map/pallas_call | solution.py:309
  110.5 4.7 %all-to-all-start.3 = ((bf16[32,16,128]{2,1,0:T(8,128)(2,1)}), bf16[32,16,128]{2,1,0:T(8,128)(2,1)S(1)}, u32[]{:S(2)}, u32[]{:S(2)}) async-start(bf16[32,16,128]{2,1,0:T(8,128)(2,1)} %shard_map.269), calls=%async_computation.3 | async-start | bytes 262144 | tf_op jit(solution)/shard_map/all_to_all | solution.py:417
  115.2 0.0 copy-start.14
  115.2 0.6 copy-done.14
  115.8 0.1 copy.29.penalty_ref
  115.9 0.1 copy.30.step_ref
  116.0 0.5 copy-done.12
  116.5 0.1 copy-done.10
  116.6 0.0 copy-done.11
  116.6 2.4 %shard_map.270 = (bf16[8,64]{1,0:T(8,128)(2,1)}, f32[3,8]{1,0:T(4,128)}) custom-call(s32[8]{0:T(128)S(1)} %copy-done.13, bf16[32,96,128]{2,1,0:T(8,128)(2,1)S(1)} %all_to_all.20.got_ref, s32[8,64]{1,0:T(8,128)S(1)} %copy-done.12, f32[64,8]{1,0:T(8,128)S(1)} %get-tuple-element.10.query_ref, bf16[8,64]{1,0:T(8,128)(2,1)S(1)} %copy-done.10, ...), custom_call_target="tpu_custom_call" | custom-call | tf_op jit(solution)/shard_map/pallas_call | solution.py:309
  119.0 3.8 %all-to-all-done.3 = bf16[32,16,128]{2,1,0:T(8,128)(2,1)S(1)} async-done(((bf16[32,16,128]{2,1,0:T(8,128)(2,1)}), bf16[32,16,128]{2,1,0:T(8,128)(2,1)S(1)}, u32[]{:S(2)}, u32[]{:S(2)}) %all-to-all-start.3) | async-done | bytes 131104 | tf_op jit(solution)/shard_map/all_to_all | solution.py:417
  122.8 0.7 copy.32
  (18 shorter events, 0.0 us)
Async XLA Ops:
  0.6 22.4 %copy-start.9 = (bf16[64,32]{0,1:T(8,128)(2,1)S(1)}, bf16[64,32]{0,1:T(8,128)(2,1)}, u32[]{:S(2)}) copy-start(bf16[64,32]{0,1:T(8,128)(2,1)} %param.31) | copy-start | bytes 12292
  2.5 20.5 %copy-start.8 = (bf16[64,32]{0,1:T(8,128)(2,1)S(1)}, bf16[64,32]{0,1:T(8,128)(2,1)}, u32[]{:S(2)}) copy-start(bf16[64,32]{0,1:T(8,128)(2,1)} %param.30) | copy-start | bytes 12292
  2.5 20.5 %collective-permute-start = (bf16[656,128]{1,0:T(8,128)(2,1)S(1)}, bf16[656,128]{1,0:T(8,128)(2,1)S(1)}, u32[]{:S(2)}, u32[]{:S(2)}) collective-permute-start(bf16[656,128]{1,0:T(8,128)(2,1)S(1)} %get-tuple-element.8.own_ref), channel_id=1, source_target_pairs={{0,1},{1,0},{2,3},{3,2},{4,5},{5,4},{6,7},{7,6},{8,9},{9,8},{10,11... | collective-permute-start | bytes 503816 | tf_op jit(solution)/shard_map/ppermute | solution.py:372
  46.5 37.9 %copy-start = (bf16[64,8,128]{2,1,0:T(8,128)(2,1)S(1)}, bf16[64,8,128]{2,1,0:T(8,128)(2,1)}, u32[]{:S(2)}) copy-start(bf16[64,8,128]{2,1,0:T(8,128)(2,1)} %pair_ref.1) | copy-start | bytes 393220
  46.5 37.9 %copy-start.1 = (bf16[1024,128]{1,0:T(8,128)(2,1)S(1)}, bf16[1024,128]{1,0:T(8,128)(2,1)}, u32[]{:S(2)}) copy-start(bf16[1024,128]{1,0:T(8,128)(2,1)} %weight_ref.1) | copy-start | bytes 786436
  75.5 8.9 %collective-permute-start.1 = (bf16[8,128,128]{2,1,0:T(8,128)(2,1)S(1)}, bf16[8,128,128]{2,1,0:T(8,128)(2,1)S(1)}, u32[]{:S(2)}, u32[]{:S(2)}) collective-permute-start(bf16[8,128,128]{2,1,0:T(8,128)(2,1)S(1)} %all_to_all.21.right_in), channel_id=1, source_target_pairs={{0,64},{64,0},{1,65},{65,1},{2,66},{66,2},{3,67},{67,3},{4,68},{68... | collective-permute-start | bytes 786440 | tf_op jit(solution)/shard_map/ppermute | solution.py:381
  90.1 15.3 %copy-start.2 = (bf16[128,128]{1,0:T(8,128)(2,1)S(1)}, bf16[128,128]{1,0:T(8,128)(2,1)}, u32[]{:S(2)}) copy-start(bf16[128,128]{1,0:T(8,128)(2,1)} %wq_ref.1) | copy-start | bytes 98308
  90.2 15.3 %copy-start.3 = (bf16[128,128]{1,0:T(8,128)(2,1)S(1)}, bf16[128,128]{1,0:T(8,128)(2,1)}, u32[]{:S(2)}) copy-start(bf16[128,128]{1,0:T(8,128)(2,1)} %wk_ref.1) | copy-start | bytes 98308
  90.2 15.3 %copy-start.4 = (bf16[128,128]{1,0:T(8,128)(2,1)S(1)}, bf16[128,128]{1,0:T(8,128)(2,1)}, u32[]{:S(2)}) copy-start(bf16[128,128]{1,0:T(8,128)(2,1)} %wv_ref.1) | copy-start | bytes 98308
  90.2 15.3 %copy-start.5 = (bf16[128,128]{1,0:T(8,128)(2,1)S(1)}, bf16[128,128]{1,0:T(8,128)(2,1)}, u32[]{:S(2)}) copy-start(bf16[128,128]{1,0:T(8,128)(2,1)} %wg_ref.1) | copy-start | bytes 98308
  90.2 15.3 %copy-start.6 = (bf16[128,128]{1,0:T(8,128)(2,1)S(1)}, bf16[128,128]{1,0:T(8,128)(2,1)}, u32[]{:S(2)}) copy-start(bf16[128,128]{1,0:T(8,128)(2,1)} %wo_ref.2) | copy-start | bytes 98308
  110.5 5.4 %copy-start.15 = (f32[4]{0:T(128)S(1)}, f32[4]{0:T(128)}, u32[]{:S(2)}) copy-start(f32[4]{0:T(128)} %param.51) | copy-start | bytes 52
  110.5 5.5 %copy-start.7 = (bf16[64,64]{1,0:T(8,128)(2,1)S(1)}, bf16[64,64]{1,0:T(8,128)(2,1)}, u32[]{:S(2)}) copy-start(bf16[64,64]{1,0:T(8,128)(2,1)} %wo_ref.3) | copy-start | bytes 24580
  110.5 5.5 %copy-start.13 = (s32[8]{0:T(128)S(1)}, s32[8]{0:T(128)}, u32[]{:S(2)}) copy-start(s32[8]{0:T(128)} %count_ref.1) | copy-start | bytes 100
  110.5 12.3 %all-to-all-start.3 = ((bf16[32,16,128]{2,1,0:T(8,128)(2,1)}), bf16[32,16,128]{2,1,0:T(8,128)(2,1)S(1)}, u32[]{:S(2)}, u32[]{:S(2)}) async-start(bf16[32,16,128]{2,1,0:T(8,128)(2,1)} %shard_map.269), calls=%async_computation.3 | async-start | bytes 262144 | tf_op jit(solution)/shard_map/all_to_all | solution.py:417
  115.2 0.7 copy-start.14
  115.8 0.7 copy-start.12
  115.9 0.7 copy-start.10
  115.9 0.7 copy-start.11

commit v6 on v5

--- a/solution.py
+++ b/solution.py
@@ -67,11 +67,16 @@
     bias_ref,
     pair_gain_ref,
     pair_ref,
+    wl_ref,
+    wr_ref,
     swap_ref,
     query_ref,
     consts_ref,
+    factor_ref,
 ):
     swap_ref[144:656] = pair_ref[...]
+    factor_ref[0:32] = wl_ref[...]
+    factor_ref[32:64] = wr_ref[...]
     consts_ref[...] = jnp.where(iota((8, 128), 0) == 0, bias_ref[...], pair_gain_ref[...])
     seqs, length, _ = act_ref.shape
     kinds = emb_ref.shape[1]
@@ -99,7 +104,7 @@
     swap_ref[128:144] = jnp.concatenate([kv, placed], 0).astype(BF16)
 
 
-def spread_kernel(half_ref, own_ref, got_ref, wl_ref, wr_ref, out_ref):
+def spread_kernel(half_ref, after_ref, own_ref, got_ref, factor_ref, out_ref):
     mine = half_ref[0] == 0
     own, came = own_ref[0:144].astype(F32), got_ref[0:144].astype(F32)
     one = jnp.where(mine, own, came)
@@ -111,14 +116,14 @@
         parts = [dot(packed, one_where(row == lane)), dot(packed, one_where(row == lane + 64))]
         planes.append(jnp.concatenate(parts, 0).astype(BF16))
 
-    row, source = iota((128, 256), 0), iota((128, 256), 1)
+    row, source = iota((128, 1), 0), iota((128, 256), 1)
     low, even = lane_masks(8)
     for core in range(2):
-        pick = one_where(source == (row // 32) * 64 + (row % 32) * 2 + core)
+        pick = one_where(source == ((row >> 5) << 6) + ((row & 31) << 1) + core)
         parts = []
         for p in range(2):
             rows = dot(pick, planes[p]).astype(BF16)
-            left = dot(wl_ref[...], rows, 1, 1).astype(BF16).astype(F32)
+            left = dot(factor_ref[0:32], rows, 1, 1).astype(BF16).astype(F32)
             parts += swap_lane_groups([left[k * 8 : (k + 1) * 8] for k in range(4)], low, even)
         block = jnp.concatenate(parts, 0).astype(BF16)
         for to in range(32):
@@ -128,11 +133,11 @@
     kv = jnp.concatenate([one[128:136], two[128:136]], 0).astype(BF16)
     out_ref[:, 64:80] = jnp.broadcast_to(kv[None], (32, 16, 128))
     place = jnp.concatenate([one[136:144], two[136:144]], 0)
-    widened = dot(wr_ref[...], one_where(iota((32, 128), 1) == iota((32, 128), 0) + 32), 0, 0).astype(BF16)
+    widened = dot(factor_ref[32:64], one_where(iota((32, 128), 1) == iota((32, 128), 0) + 32), 0, 0).astype(BF16)
     both = jnp.concatenate(planes, 0)
     for g in range(4):
-        row, source = iota((128, 512), 0) + g * 128, iota((128, 512), 1)
-        wanted = ((row // 8) % 2) * 256 + ((row // 2) % 4) * 64 + (row // 16) * 2 + row % 2
+        row, source = iota((128, 1), 0) + g * 128, iota((128, 512), 1)
+        wanted = (((row >> 3) & 1) << 8) + (((row >> 1) & 3) << 6) + ((row >> 4) << 1) + (row & 1)
         moved = dot(one_where(source == wanted), both).astype(BF16)
         right = dot(moved, widened).reshape(8, 16, 128) + place[None]
         out_ref[g * 8 : (g + 1) * 8, 80:96] = right.astype(BF16)
@@ -140,8 +145,8 @@
 
 def right_kernel(got_ref, out_ref):
     rows = got_ref[:, 80:96].reshape(512, 128)
-    row, source = iota((128, 512), 0), iota((128, 512), 1)
-    start = (row // 4) * 16 + (row % 4) * 2
+    row, source = iota((128, 1), 0), iota((128, 512), 1)
+    start = ((row >> 2) << 4) + ((row & 3) << 1)
     at, lane = iota((128, 128), 0), iota((128, 128), 1)
     total = jnp.zeros((128, 128), F32)
     for plane in range(2):
@@ -153,11 +158,24 @@
     out_ref[...] = jnp.broadcast_to(total.astype(BF16)[None], out_ref.shape)
 
 
+def weight_kernel(after_ref, weight_ref, out_ref, token_ref):
+    token_ref[...] = after_ref[...]
+    out_ref[...] = jnp.zeros_like(out_ref)
+    for q in range(8):
+        for k in range(4):
+            block = weight_ref[(k * 8 + q) * 32 : (k * 8 + q) * 32 + 32]
+            for j in range(4):
+                at = (q * 4 + k) * 128 + j * 32
+                out_ref[at : at + 32, j * 128 : (j + 1) * 128] = block
+
+
 def outer_kernel(
-    half_ref, got_ref, right_in, other_in, pair_ref, came_ref, weight_ref, out_ref, left, right, joined, weight, update
+    half_ref, got_ref, right_in, pair_ref, came_ref, weight_hbm, out_ref, left, right, joined, update, weight, sem
 ):
-    row = iota((256, 256), 0)
-    wanted = ((row // 4) % 4) * 64 + ((row // 16) % 2) * 32 + (row % 4) * 8 + row // 32
+    copy = pltpu.make_async_copy(weight_hbm, weight, sem)
+    copy.start()
+    row = iota((256, 1), 0)
+    wanted = (((row >> 2) & 3) << 6) + (((row >> 4) & 1) << 5) + ((row & 3) << 3) + (row >> 5)
     turn = one_where(iota((256, 256), 1) == wanted)
     for g in range(8):
         part = dot(turn, got_ref[g * 4 : (g + 1) * 4, 0:64].reshape(256, 128)).astype(BF16)
@@ -165,31 +183,24 @@
             for p in range(2):
                 at = p * 128 + g * 16
                 left[at : at + 16, q * 128 : (q + 1) * 128] = part[q * 32 + p * 16 : q * 32 + p * 16 + 16]
-    low, even = lane_masks(128)
+    low, _ = lane_masks(128)
     for t in range(8):
-        source = right_in if t < 4 else other_in
-        a, b = source[2 * (t % 4)].astype(F32), source[2 * (t % 4) + 1].astype(F32)
+        a, b = right_in[2 * t].astype(F32), right_in[2 * t + 1].astype(F32)
         right[0:128, t * 128 : (t + 1) * 128] = jnp.where(low, a, pltpu.roll(b, 64, 1)).astype(BF16)
         right[128:256, t * 128 : (t + 1) * 128] = jnp.where(low, pltpu.roll(a, 64, 1), b).astype(BF16)
     for q in range(8):
-        for k in range(4):
-            at = (k * 8 + q) * 32
-            weight[q * 128 + k * 32 : q * 128 + k * 32 + 32] = weight_ref[at : at + 32]
-
-    low, even = lane_masks(32)
-    scale = 1.0 / 256.0
-    for q in range(8):
-        product = dot(left[:, q * 128 : (q + 1) * 128], right[...], 0, 0) * scale
+        product = (dot(left[:, q * 128 : (q + 1) * 128], right[...], 0, 0) * (1.0 / 256.0)).astype(BF16)
         for t in range(8):
-            tile = product[:, t * 128 : (t + 1) * 128]
-            blocks = swap_lane_groups([tile[k * 32 : (k + 1) * 32] for k in range(4)], low, even)
-            for j in range(4):
-                at = (t * 4 + j) * 32
-                joined[at : at + 32, q * 128 : (q + 1) * 128] = blocks[j].astype(BF16)
-    for j in range(0, 32, 8):
-        rows = dot(joined[j * 32 : (j + 8) * 32], weight[...])
-        for k in range(8):
-            update[:, j + k, :] = rows[k * 32 : (k + 1) * 32]
+            for k in range(4):
+                at = (q * 4 + k) * 128
+                joined[t * 32 : (t + 1) * 32, at : at + 128] = product[
+                    k * 32 : (k + 1) * 32, t * 128 : (t + 1) * 128
+                ]
+    copy.wait()
+    rows = dot(joined[...], weight[...])
+    for t in range(8):
+        for j in range(4):
+            update[:, t * 4 + j, :] = rows[t * 32 : (t + 1) * 32, j * 128 : (j + 1) * 128]
     out_ref[:, 0:32] = update[...].astype(BF16)
 
     first = iota((64, 16, 128), 1) // 8 == half_ref[0]
@@ -205,13 +216,16 @@
     factor = 32 ** (-0.5) * math.log2(math.e)
     head_of = iota((512, 128), 1) // 32
     zero, one = jnp.zeros((512, 128), BF16), jnp.ones((512, 128), BF16)
-    row, source = iota((512, 512), 0), iota((512, 512), 1)
+    row, source = iota((512, 1), 0), iota((512, 512), 1)
+    wanted = (((row >> 4) & 3) << 7) + (((row >> 1) & 3) << 5) + (((row >> 3) & 1) << 4)
+    turn = one_where(source == wanted + ((row >> 6) << 1) + (row & 1))
+    shares = got_ref[:, 0:32].reshape(4, 2, 4, 32, 128)
+    updates = jnp.concatenate([shares[:, p].reshape(512, 128) for p in range(2)], 1)
+    updates = dot(turn, updates)
     for p in range(2):
-        other = (row // 8) % 2 if p == 0 else 1 - (row // 8) % 2
-        wanted = ((row // 16) % 4) * 128 + ((row // 2) % 4) * 32 + other * 16 + (row // 64) * 2 + row % 2
-        update = got_ref[:, 0:32].reshape(4, 2, 4, 32, 128)[:, p].reshape(512, 128)
+        update = updates[:, p * 128 : (p + 1) * 128]
         pair = got_ref[:, 32:64].reshape(32, 2, 16, 128)[:, p].reshape(512, 128)
-        pair_mid = dot(one_where(source == wanted), update) + pair.astype(F32) + consts_ref[0:1]
+        pair_mid = update + pair.astype(F32) + consts_ref[0:1]
         pair_mid = pair_mid.astype(BF16).astype(F32)
         normed = layer_normalize(pair_mid, consts_ref[1:2])
         split = pair_mid.reshape(32, 2, 8, 128)
@@ -299,17 +313,19 @@
     return kernel
 
 
-def call(body, out_shape, args, scratch=(), fetch=False):
-    scratch = list(scratch)
+def call(body, out_shape, args, scratch=(), fetch=False, hbm=0):
+    scratch, args = list(scratch), list(args)
     if fetch:
         body = with_fetch(body, len(args))
         scratch += [pltpu.VMEM(a.shape, a.dtype) for a in args] + [pltpu.SemaphoreType.DMA((len(args),))]
-        args = [pltpu.with_memory_space_constraint(a, pltpu.HBM) for a in args]
-    space = pltpu.HBM if fetch else pltpu.VMEM
+        hbm = len(args)
+    first = len(args) - hbm
+    args = args[:first] + [pltpu.with_memory_space_constraint(a, pltpu.HBM) for a in args[first:]]
+    spaces = [pltpu.SMEM if a.ndim == 1 else pltpu.VMEM for a in args[:first]] + [pltpu.HBM] * hbm
     return pl.pallas_call(
         body,
         out_shape=out_shape,
-        in_specs=[pl.BlockSpec(memory_space=pltpu.SMEM if a.ndim == 1 else space) for a in args],
+        in_specs=[pl.BlockSpec(memory_space=s) for s in spaces],
         out_specs=jax.tree.map(lambda _: pl.BlockSpec(memory_space=pltpu.VMEM), out_shape),
         scratch_shapes=scratch,
         compiler_params=pltpu.CompilerParams(vmem_limit_bytes=VMEM_LIMIT),
@@ -349,9 +365,9 @@
     coordinate_step,
 ):
     half = lax.axis_index("zh").reshape(1).astype(jnp.int32)
-    swap, node_query, consts = call(
+    swap, node_query, consts, factors = call(
         first_kernel,
-        (shape((656, 128)), shape((64, 8), F32), shape((8, 128), F32)),
+        (shape((656, 128)), shape((64, 8), F32), shape((8, 128), F32), shape((64, 64))),
         (
             homolog_activations,
             alignment_token_ids,
@@ -366,30 +382,37 @@
             outer_bias.reshape(1, -1),
             pair_norm_gain.reshape(1, -1),
             pair.reshape(512, 128),
+            first_operand_projection.T,
+            second_operand_projection.T,
         ),
         fetch=True,
     )
     swapped = lax.ppermute(swap, "zh", [(0, 1), (1, 0)])
+    weight, token = call(
+        weight_kernel, (shape((4096, 512)), shape((8, 128), F32)), (consts, outer_output_weight)
+    )
     spread = call(
         spread_kernel,
         shape((32, 96, 128)),
-        (half, swap, swapped, first_operand_projection.T, second_operand_projection.T),
+        (half, token, swap, swapped, factors),
     )
     got = lax.all_to_all(spread, PLANE, split_axis=0, concat_axis=0, tiled=True)
     right = call(right_kernel, shape((8, 128, 128)), (got,))
     right = lax.all_to_all(right, "row", split_axis=0, concat_axis=0, tiled=True)
-    other = lax.ppermute(right, "core", [(0, 1), (1, 0)])
+    right = lax.all_gather(right, "core", axis=0, tiled=True)
     rows = call(
         outer_kernel,
         shape((32, 64, 128)),
-        (half, got, right, other, pair, swapped, outer_output_weight),
+        (half, got, right, pair, swapped, weight),
         scratch=(
             pltpu.VMEM((256, 1024), BF16),
             pltpu.VMEM((256, 1024), BF16),
-            pltpu.VMEM((1024, 1024), BF16),
-            pltpu.VMEM((1024, 128), BF16),
+            pltpu.VMEM((256, 4096), BF16),
             pltpu.VMEM((32, 32, 128), F32),
+            pltpu.VMEM((4096, 512), BF16),
+            pltpu.SemaphoreType.DMA,
         ),
+        hbm=1,
     )
     rows = lax.all_to_all(rows, PLANE, split_axis=0, concat_axis=0, tiled=True)
     done = call(

time: 124 us -> 121 us (0.976)
  starting transfers between devices: 28.7 us -> 20.8 us
  blocking collectives: 66 us -> 73.5 us
  waiting for transfers between devices: 9.18 us -> 5.95 us
  local copies, waits for them, and re-layouts: 2.16 us -> 3.79 us
  Pallas kernels: 16.7 us -> 15.3 us
    all_gather x0 -> x1, blocking collectives: none -> 7.77 us  [on_device(): right = lax.all_gather(right, 'core', axis=0, tiled=True)]
    ppermute x1 -> x0, starting transfers between devices: 7.73 us -> none  [on_device(): other = lax.ppermute(right, 'core', [(0, 1), (1, 0)])]
    ppermute x1, waiting for transfers between devices: 4.21 us -> 0.9 us  [on_device(): swapped = lax.ppermute(swap, 'zh', [(0, 1), (1, 0)])]
    unnamed x33 -> x31, local copies, waits for them, and re-layouts: 1.97 us -> 3.6 us
    pallas_call x6 -> x7, Pallas kernels: 16.7 us -> 15.3 us  [call(): pl.pallas_call(body, out_shape=out_shape, in_specs=[pl.BlockSpec(memory_s...]
  transfers between devices with their start and end apart: 3 -> 2, of which waited for: 3 -> 2; matrix products, arithmetic and copies ran while one was open for 0% -> 0% of each run, Pallas kernels for 2% -> 2%
where the time goes in v6:
time: 121 us; the launch traced here: 120 us
  blocking collectives  73.5 us (61%)
  starting transfers between devices  20.8 us (17%)
  Pallas kernels  15.3 us (13%)
  waiting for transfers between devices  5.95 us (5%)
  local copies, waits for them, and re-layouts  3.79 us (3%)
    all_to_all x1, blocking collectives, on_device(): lax.all_to_all(right, 'row', split_axis=0, concat_axis=0, tiled=True)  28.9 us
    all_to_all x1, blocking collectives, on_device(): got = lax.all_to_all(spread, PLANE, split_axis=0, concat_axis=0, tiled=True)  21.7 us
    ppermute x1, starting transfers between devices, on_device(): swapped = lax.ppermute(swap, 'zh', [(0, 1), (1, 0)])  16.3 us
    pallas_call x7, Pallas kernels, call(): pl.pallas_call(body, out_shape=out_shape, in_specs=[pl.BlockSpec(memory_s...  15.3 us
    all_to_all x1, blocking collectives, on_device(): rows = lax.all_to_all(rows, PLANE, split_axis=0, concat_axis=0, tiled=True)  15.1 us
    all_gather x1, blocking collectives, on_device(): right = lax.all_gather(right, 'core', axis=0, tiled=True)  7.77 us
    all_to_all x1, waiting for transfers between devices, on_device(): done = lax.all_to_all(done, PLANE, split_axis=0, concat_axis=0, tiled=True)  5.06 us
    all_to_all x1, starting transfers between devices, on_device(): done = lax.all_to_all(done, PLANE, split_axis=0, concat_axis=0, tiled=True)  4.52 us
  transfers between devices with their start and end apart: 2, of which 2 were waited for; matrix products, arithmetic and copies ran while one was open for 0% of the time, Pallas kernels for 2%

profile of v6, /device:TPU:1, one launch (start us, length us, event | category | flops | bytes accessed | tf_op | source)
XLA Modules:
  0.0 120.1 jit_solution(14282803889458946937)
XLA Ops:
  0.6 0.0 copy-start.1
  0.6 1.9 %shard_map.265 = (bf16[656,128]{1,0:T(8,128)(2,1)S(1)}, f32[64,8]{1,0:T(8,128)S(1)}, f32[8,128]{1,0:T(8,128)S(1)}, bf16[64,64]{1,0:T(8,128)(2,1)S(1)}) custom-call(bf16[4,64,64]{2,1,0:T(8,128)(2,1)} %refs_0_.1, s32[4,64]{1,0:T(4,128)} %refs_1_.1, bf16[64,80]{1,0:T(8,128)(2,1)} %bitcast.14, f32[1,64]{1,0:T(1,128)} %bitcast.17, bf16[8,64]{1,0:T(8,128)(2,1)} %nodes_ref.1, ...), custom_call_target="tpu_custom_call" | custom-call | tf_op jit(solution)/shard_map/pallas_call | solution.py:325
  2.5 16.3 %collective-permute-start = (bf16[656,128]{1,0:T(8,128)(2,1)S(1)}, bf16[656,128]{1,0:T(8,128)(2,1)S(1)}, u32[]{:S(2)}, u32[]{:S(2)}) collective-permute-start(bf16[656,128]{1,0:T(8,128)(2,1)S(1)} %get-tuple-element.13.own_ref), channel_id=1, source_target_pairs={{0,1},{1,0},{2,3},{3,2},{4,5},{5,4},{6,7},{7,6},{8,9},{9,8},{10,11... | collective-permute-start | bytes 503816 | tf_op jit(solution)/shard_map/ppermute | solution.py:390
  18.8 0.0 copy-start.2
  18.8 0.9 copy-done.2
  19.8 0.4 shard_map.266
  20.2 0.0 copy-start
  20.2 1.9 %copy-done = bf16[4096,512]{1,0:T(8,128)(2,1)} copy-done((bf16[4096,512]{1,0:T(8,128)(2,1)}, bf16[4096,512]{1,0:T(8,128)(2,1)S(1)}, u32[]{:S(2)}) %copy-start) | copy-done | bytes 4194328
  22.1 0.9 collective-permute-done.got_ref.came_ref
  23.0 1.2 shard_map.267
  24.2 21.7 %all_to_all.20.got_ref = bf16[32,96,128]{2,1,0:T(8,128)(2,1)S(1)} all-to-all(bf16[32,96,128]{2,1,0:T(8,128)(2,1)S(1)} %shard_map.267), channel_id=1, replica_groups=mesh['x'=4,'core'=2,'row'=8,'y'=4,'zh'=2] {'x','core','y'}, dimensions={0} | all-to-all | bytes 1572864 | tf_op jit(solution)/shard_map/all_to_all | solution.py:399
  45.9 0.5 shard_map.268
  46.5 28.9 %all_to_all.21 = bf16[8,128,128]{2,1,0:T(8,128)(2,1)S(1)} all-to-all(bf16[8,128,128]{2,1,0:T(8,128)(2,1)S(1)} %shard_map.268), channel_id=1, replica_groups=mesh['x'=4,'core'=2,'row'=8,'y'=4,'zh'=2] {'row'}, dimensions={0} | all-to-all | bytes 524288 | tf_op jit(solution)/shard_map/all_to_all | solution.py:401
  75.3 0.0 copy-start.7
  75.4 7.8 %all_gather.3.right_in = bf16[16,128,128]{2,1,0:T(8,128)(2,1)S(1)} all-gather(bf16[8,128,128]{2,1,0:T(8,128)(2,1)S(1)} %all_to_all.21), channel_id=1, replica_groups=mesh['x'=4,'core'=2,'row'=8,'y'=4,'zh'=2] {'core'}, dimensions={0}, use_global_device_ids=true | all-gather | bytes 786432 | tf_op jit(solution)/shard_map/all_gather | solution.py:402
  83.1 0.0 copy-start.9
  83.1 0.0 copy-start.10
  83.2 0.0 copy-start.11
  83.2 0.0 copy-start.12
  83.2 4.3 %shard_map.269 = bf16[32,64,128]{2,1,0:T(8,128)(2,1)S(1)} custom-call(s32[1]{0:T(128)} %bitcast.half_ref, bf16[32,96,128]{2,1,0:T(8,128)(2,1)S(1)} %all_to_all.20.got_ref, bf16[16,128,128]{2,1,0:T(8,128)(2,1)S(1)} %all_gather.3.right_in, bf16[64,8,128]{2,1,0:T(8,128)(2,1)S(1)} %copy-done.1, bf16[656,128]{1,0:T(8,128)(2,1)S(1)} %collective-permute-done.got_ref.came_ref, ...), custom_call_target="tpu_custom_call" | custom-call | tf_op jit(solution)/shard_map/pallas_call | solution.py:325
  87.5 15.1 %all_to_all.22.got_ref = bf16[32,64,128]{2,1,0:T(8,128)(2,1)S(1)} all-to-all(bf16[32,64,128]{2,1,0:T(8,128)(2,1)S(1)} %shard_map.269), channel_id=1, replica_groups=mesh['x'=4,'core'=2,'row'=8,'y'=4,'zh'=2] {'x','core','y'}, dimensions={0} | all-to-all | bytes 1048576 | tf_op jit(solution)/shard_map/all_to_all | solution.py:417
  102.6 0.0 copy-done.6
  102.6 0.0 copy-done.7
  102.6 4.6 %shard_map.270 = bf16[32,16,128]{2,1,0:T(8,128)(2,1)} custom-call(s32[1]{0:T(128)} %bitcast.half_ref, bf16[32,64,128]{2,1,0:T(8,128)(2,1)S(1)} %all_to_all.22.got_ref, f32[8,128]{1,0:T(8,128)S(1)} %get-tuple-element.11.after_ref.consts_ref, bf16[128,128]{1,0:T(8,128)(2,1)S(1)} %copy-done.3, bf16[128,128]{1,0:T(8,128)(2,1)S(1)} %copy-done.4, ...), custom_call_target="tpu_custom_call" | custom-call | tf_op jit(solution)/shard_map/pallas_call | solution.py:325
  107.3 4.5 %all-to-all-start.3 = ((bf16[32,16,128]{2,1,0:T(8,128)(2,1)}), bf16[32,16,128]{2,1,0:T(8,128)(2,1)S(1)}, u32[]{:S(2)}, u32[]{:S(2)}) async-start(bf16[32,16,128]{2,1,0:T(8,128)(2,1)} %shard_map.270), calls=%async_computation.3 | async-start | bytes 262144 | tf_op jit(solution)/shard_map/all_to_all | solution.py:440
  111.8 0.1 copy.31.penalty_ref
  111.9 0.0 copy-done.14
  111.9 0.1 copy.32.step_ref
  112.0 0.0 copy-done.8
  112.0 2.4 %shard_map.271 = (bf16[8,64]{1,0:T(8,128)(2,1)}, f32[3,8]{1,0:T(4,128)}) custom-call(s32[8]{0:T(128)S(1)} %copy-done.12, bf16[32,96,128]{2,1,0:T(8,128)(2,1)S(1)} %all_to_all.20.got_ref, s32[8,64]{1,0:T(8,128)S(1)} %copy-done.11, f32[64,8]{1,0:T(8,128)S(1)} %get-tuple-element.16.query_ref, bf16[8,64]{1,0:T(8,128)(2,1)S(1)} %copy-done.9, ...), custom_call_target="tpu_custom_call" | custom-call | tf_op jit(solution)/shard_map/pallas_call | solution.py:325
  114.4 5.1 %all-to-all-done.3 = bf16[32,16,128]{2,1,0:T(8,128)(2,1)S(1)} async-done(((bf16[32,16,128]{2,1,0:T(8,128)(2,1)}), bf16[32,16,128]{2,1,0:T(8,128)(2,1)S(1)}, u32[]{:S(2)}, u32[]{:S(2)}) %all-to-all-start.3) | async-done | bytes 131104 | tf_op jit(solution)/shard_map/all_to_all | solution.py:440
  119.5 0.7 copy.34
  (16 shorter events, 0.0 us)
Async XLA Ops:
  0.6 82.5 %copy-start.1 = (bf16[64,8,128]{2,1,0:T(8,128)(2,1)S(1)}, bf16[64,8,128]{2,1,0:T(8,128)(2,1)}, u32[]{:S(2)}) copy-start(bf16[64,8,128]{2,1,0:T(8,128)(2,1)} %pair_ref.1) | copy-start | bytes 393220
  2.5 20.5 %collective-permute-start = (bf16[656,128]{1,0:T(8,128)(2,1)S(1)}, bf16[656,128]{1,0:T(8,128)(2,1)S(1)}, u32[]{:S(2)}, u32[]{:S(2)}) collective-permute-start(bf16[656,128]{1,0:T(8,128)(2,1)S(1)} %get-tuple-element.13.own_ref), channel_id=1, source_target_pairs={{0,1},{1,0},{2,3},{3,2},{4,5},{5,4},{6,7},{7,6},{8,9},{9,8},{10,11... | collective-permute-start | bytes 503816 | tf_op jit(solution)/shard_map/ppermute | solution.py:390
  18.8 1.0 copy-start.2
  20.2 1.9 %copy-start = (bf16[4096,512]{1,0:T(8,128)(2,1)}, bf16[4096,512]{1,0:T(8,128)(2,1)S(1)}, u32[]{:S(2)}) copy-start(bf16[4096,512]{1,0:T(8,128)(2,1)S(1)} %get-tuple-element.15.weight_hbm) | copy-start | bytes 12582916
  75.3 27.3 %copy-start.3 = (bf16[128,128]{1,0:T(8,128)(2,1)S(1)}, bf16[128,128]{1,0:T(8,128)(2,1)}, u32[]{:S(2)}) copy-start(bf16[128,128]{1,0:T(8,128)(2,1)} %wq_ref.1) | copy-start | bytes 98308
  75.3 27.3 %copy-start.4 = (bf16[128,128]{1,0:T(8,128)(2,1)S(1)}, bf16[128,128]{1,0:T(8,128)(2,1)}, u32[]{:S(2)}) copy-start(bf16[128,128]{1,0:T(8,128)(2,1)} %wk_ref.1) | copy-start | bytes 98308
  75.3 27.3 %copy-start.5 = (bf16[128,128]{1,0:T(8,128)(2,1)S(1)}, bf16[128,128]{1,0:T(8,128)(2,1)}, u32[]{:S(2)}) copy-start(bf16[128,128]{1,0:T(8,128)(2,1)} %wv_ref.1) | copy-start | bytes 98308
  75.3 27.3 %copy-start.6 = (bf16[128,128]{1,0:T(8,128)(2,1)S(1)}, bf16[128,128]{1,0:T(8,128)(2,1)}, u32[]{:S(2)}) copy-start(bf16[128,128]{1,0:T(8,128)(2,1)} %wg_ref.1) | copy-start | bytes 98308
  75.3 27.3 %copy-start.7 = (bf16[128,128]{1,0:T(8,128)(2,1)S(1)}, bf16[128,128]{1,0:T(8,128)(2,1)}, u32[]{:S(2)}) copy-start(bf16[128,128]{1,0:T(8,128)(2,1)} %wo_ref.2) | copy-start | bytes 98308
  83.1 28.7 %copy-start.13 = (f32[4]{0:T(128)S(1)}, f32[4]{0:T(128)}, u32[]{:S(2)}) copy-start(f32[4]{0:T(128)} %param.50) | copy-start | bytes 52
  83.1 28.8 %copy-start.14 = (f32[4]{0:T(128)S(1)}, f32[4]{0:T(128)}, u32[]{:S(2)}) copy-start(f32[4]{0:T(128)} %param.51) | copy-start | bytes 52
  83.1 28.9 %copy-start.8 = (bf16[64,64]{1,0:T(8,128)(2,1)S(1)}, bf16[64,64]{1,0:T(8,128)(2,1)}, u32[]{:S(2)}) copy-start(bf16[64,64]{1,0:T(8,128)(2,1)} %wo_ref.3) | copy-start | bytes 24580
  83.1 28.9 %copy-start.9 = (bf16[8,64]{1,0:T(8,128)(2,1)S(1)}, bf16[8,64]{1,0:T(8,128)(2,1)}, u32[]{:S(2)}) copy-start(bf16[8,64]{1,0:T(8,128)(2,1)} %nodes_ref.1) | copy-start | bytes 3076
  83.1 28.9 %copy-start.10 = (f32[3,8]{1,0:T(4,128)S(1)}, f32[3,8]{1,0:T(4,128)}, u32[]{:S(2)}) copy-start(f32[3,8]{1,0:T(4,128)} %coords_ref.1) | copy-start | bytes 292
  83.2 28.9 %copy-start.11 = (s32[8,64]{1,0:T(8,128)S(1)}, s32[8,64]{1,0:T(8,128)}, u32[]{:S(2)}) copy-start(s32[8,64]{1,0:T(8,128)} %index_ref.1) | copy-start | bytes 6148
  83.2 28.8 %copy-start.12 = (s32[8]{0:T(128)S(1)}, s32[8]{0:T(128)}, u32[]{:S(2)}) copy-start(s32[8]{0:T(128)} %count_ref.1) | copy-start | bytes 100
  107.3 12.2 %all-to-all-start.3 = ((bf16[32,16,128]{2,1,0:T(8,128)(2,1)}), bf16[32,16,128]{2,1,0:T(8,128)(2,1)S(1)}, u32[]{:S(2)}, u32[]{:S(2)}) async-start(bf16[32,16,128]{2,1,0:T(8,128)(2,1)} %shard_map.270), calls=%async_computation.3 | async-start | bytes 262144 | tf_op jit(solution)/shard_map/all_to_all | solution.py:440

commit v7 on v6

--- a/solution.py
+++ b/solution.py
@@ -13,7 +13,7 @@
 NODE_HEADS = 4
 PLANE = ("x", "core", "y")
 GROUP = ("x", "core", "y", "zh")
-VMEM_LIMIT = 48 * 1024 * 1024
+VMEM_LIMIT = 24 * 1024 * 1024
 
 
 def dot(a, b, ca=1, cb=0):
@@ -104,7 +104,7 @@
     swap_ref[128:144] = jnp.concatenate([kv, placed], 0).astype(BF16)
 
 
-def spread_kernel(half_ref, after_ref, own_ref, got_ref, factor_ref, out_ref):
+def spread_kernel(half_ref, own_ref, got_ref, factor_ref, out_ref):
     mine = half_ref[0] == 0
     own, came = own_ref[0:144].astype(F32), got_ref[0:144].astype(F32)
     one = jnp.where(mine, own, came)
@@ -143,7 +143,8 @@
         out_ref[g * 8 : (g + 1) * 8, 80:96] = right.astype(BF16)
 
 
-def right_kernel(got_ref, out_ref):
+def right_kernel(got_ref, out_ref, token_ref):
+    token_ref[...] = jnp.zeros_like(token_ref)
     rows = got_ref[:, 80:96].reshape(512, 128)
     row, source = iota((128, 1), 0), iota((128, 512), 1)
     start = ((row >> 2) << 4) + ((row & 3) << 1)
@@ -158,55 +159,55 @@
     out_ref[...] = jnp.broadcast_to(total.astype(BF16)[None], out_ref.shape)
 
 
-def weight_kernel(after_ref, weight_ref, out_ref, token_ref):
-    token_ref[...] = after_ref[...]
-    out_ref[...] = jnp.zeros_like(out_ref)
+def left_kernel(after_ref, got_ref, out_ref, left):
+    row = iota((256, 1), 0)
+    wanted = (((row >> 2) & 3) << 6) + (((row >> 4) & 1) << 5) + ((row & 3) << 3) + (row >> 5)
+    turn = one_where(iota((256, 256), 1) == wanted)
+    for g in range(8):
+        part = dot(turn, got_ref[g * 4 : (g + 1) * 4, 0:64].reshape(256, 128))
+        for q in range(8):
+            for p in range(2):
+                at = p * 128 + g * 16
+                left[at : at + 16, q * 128 : (q + 1) * 128] = part[q * 32 + p * 16 : q * 32 + p * 16 + 16]
+    for q in range(8):
+        out_ref[q * 128 : (q + 1) * 128] = left[:, q * 128 : (q + 1) * 128].T.astype(BF16)
+
+
+def outer_kernel(
+    place_ref, own_ref, other_ref, right_in, pair_ref, came_ref, weight_ref, out_ref, right, joined, update, weight
+):
+    weight[...] = jnp.zeros_like(weight)
     for q in range(8):
         for k in range(4):
             block = weight_ref[(k * 8 + q) * 32 : (k * 8 + q) * 32 + 32]
             for j in range(4):
                 at = (q * 4 + k) * 128 + j * 32
-                out_ref[at : at + 32, j * 128 : (j + 1) * 128] = block
-
-
-def outer_kernel(
-    half_ref, got_ref, right_in, pair_ref, came_ref, weight_hbm, out_ref, left, right, joined, update, weight, sem
-):
-    copy = pltpu.make_async_copy(weight_hbm, weight, sem)
-    copy.start()
-    row = iota((256, 1), 0)
-    wanted = (((row >> 2) & 3) << 6) + (((row >> 4) & 1) << 5) + ((row & 3) << 3) + (row >> 5)
-    turn = one_where(iota((256, 256), 1) == wanted)
-    for g in range(8):
-        part = dot(turn, got_ref[g * 4 : (g + 1) * 4, 0:64].reshape(256, 128)).astype(BF16)
-        for q in range(8):
-            for p in range(2):
-                at = p * 128 + g * 16
-                left[at : at + 16, q * 128 : (q + 1) * 128] = part[q * 32 + p * 16 : q * 32 + p * 16 + 16]
+                weight[at : at + 32, j * 128 : (j + 1) * 128] = block
     low, _ = lane_masks(128)
-    for t in range(8):
+    for t in range(4):
         a, b = right_in[2 * t].astype(F32), right_in[2 * t + 1].astype(F32)
         right[0:128, t * 128 : (t + 1) * 128] = jnp.where(low, a, pltpu.roll(b, 64, 1)).astype(BF16)
         right[128:256, t * 128 : (t + 1) * 128] = jnp.where(low, pltpu.roll(a, 64, 1), b).astype(BF16)
-    for q in range(8):
-        product = (dot(left[:, q * 128 : (q + 1) * 128], right[...], 0, 0) * (1.0 / 256.0)).astype(BF16)
-        for t in range(8):
-            for k in range(4):
-                at = (q * 4 + k) * 128
-                joined[t * 32 : (t + 1) * 32, at : at + 128] = product[
-                    k * 32 : (k + 1) * 32, t * 128 : (t + 1) * 128
-                ]
-    copy.wait()
+    for n, left in enumerate((own_ref, other_ref)):
+        for q in range(8):
+            product = (dot(left[q * 128 : (q + 1) * 128], right[...]) * (1.0 / 256.0)).astype(BF16)
+            for t in range(4):
+                for k in range(4):
+                    at, to = (q * 4 + k) * 128, (n * 4 + t) * 32
+                    joined[to : to + 32, at : at + 128] = product[
+                        k * 32 : (k + 1) * 32, t * 128 : (t + 1) * 128
+                    ]
+    first = iota((64, 16, 128), 1) // 8 == place_ref[0]
+    kept, came = pair_ref[...].astype(F32), came_ref[144:656].reshape(64, 8, 128).astype(F32)
+    pairs = jnp.where(first, jnp.concatenate([kept, kept], 1), jnp.concatenate([came, came], 1))
+    out_ref[:, 32:64] = pairs.reshape(32, 32, 128).astype(BF16)
     rows = dot(joined[...], weight[...])
     for t in range(8):
         for j in range(4):
             update[:, t * 4 + j, :] = rows[t * 32 : (t + 1) * 32, j * 128 : (j + 1) * 128]
-    out_ref[:, 0:32] = update[...].astype(BF16)
-
-    first = iota((64, 16, 128), 1) // 8 == half_ref[0]
-    kept, came = pair_ref[...].astype(F32), came_ref[144:656].reshape(64, 8, 128).astype(F32)
-    pairs = jnp.where(first, jnp.concatenate([kept, kept], 1), jnp.concatenate([came, came], 1))
-    out_ref[:, 32:64] = pairs.reshape(32, 32, 128).astype(BF16)
+    core = place_ref[1]
+    out_ref[:, pl.ds(pl.multiple_of(core * 16, 16), 16)] = update[:, 0:16].astype(BF16)
+    out_ref[:, pl.ds(pl.multiple_of((1 - core) * 16, 16), 16)] = update[:, 16:32].astype(BF16)
 
 
 def attend_kernel(
@@ -217,9 +218,8 @@
     head_of = iota((512, 128), 1) // 32
     zero, one = jnp.zeros((512, 128), BF16), jnp.ones((512, 128), BF16)
     row, source = iota((512, 1), 0), iota((512, 512), 1)
-    wanted = (((row >> 4) & 3) << 7) + (((row >> 1) & 3) << 5) + (((row >> 3) & 1) << 4)
-    turn = one_where(source == wanted + ((row >> 6) << 1) + (row & 1))
-    shares = got_ref[:, 0:32].reshape(4, 2, 4, 32, 128)
+    turn = one_where(source == (((row >> 1) & 31) << 4) + ((row >> 6) << 1) + (row & 1))
+    shares = got_ref[:, 0:32].reshape(32, 2, 16, 128)
     updates = jnp.concatenate([shares[:, p].reshape(512, 128) for p in range(2)], 1)
     updates = dot(turn, updates)
     for p in range(2):
@@ -245,18 +245,16 @@
             )
             for h in range(PAIR_HEADS)
         ]
-        for c in range(2):
-            at = slice(c * 128, (c + 1) * 128)
-            queries = q_s[at, :]
-            total = jnp.zeros((128, 256), F32)
-            for h in range(PAIR_HEADS):
-                scores = dot(queries, head_keys[h], 1, 1)
-                top = jnp.max(scores, -1, keepdims=True)
-                weights = jnp.exp2((scores - top) * factor).astype(BF16)
-                total = total + dot(weights, head_values[h])
-            attended = total[:, :128] / total[:, 128:] * jax.nn.sigmoid(gate_s[at, :])
-            result = mid_s[at, :] + dot(attended.astype(BF16), wo_ref[...])
-            done_s[c * 16 : (c + 1) * 16, p * 8 : (p + 1) * 8] = result.reshape(16, 8, 128)
+        queries = q_s[...]
+        total = jnp.zeros((256, 256), F32)
+        for h in range(PAIR_HEADS):
+            scores = dot(queries, head_keys[h], 1, 1)
+            top = jnp.max(scores, -1, keepdims=True)
+            weights = jnp.exp2((scores - top) * factor).astype(BF16)
+            total = total + dot(weights, head_values[h])
+        attended = total[:, :128] / total[:, 128:] * jax.nn.sigmoid(gate_s[...])
+        result = mid_s[...] + dot(attended.astype(BF16), wo_ref[...])
+        done_s[:, p * 8 : (p + 1) * 8] = result.reshape(32, 8, 128)
     out_ref[...] = done_s[...].astype(BF16)
 
 
@@ -388,31 +386,29 @@
         fetch=True,
     )
     swapped = lax.ppermute(swap, "zh", [(0, 1), (1, 0)])
-    weight, token = call(
-        weight_kernel, (shape((4096, 512)), shape((8, 128), F32)), (consts, outer_output_weight)
-    )
     spread = call(
         spread_kernel,
         shape((32, 96, 128)),
-        (half, token, swap, swapped, factors),
+        (half, swap, swapped, factors),
     )
     got = lax.all_to_all(spread, PLANE, split_axis=0, concat_axis=0, tiled=True)
-    right = call(right_kernel, shape((8, 128, 128)), (got,))
+    right, token = call(right_kernel, (shape((8, 128, 128)), shape((8, 128), F32)), (got,))
     right = lax.all_to_all(right, "row", split_axis=0, concat_axis=0, tiled=True)
-    right = lax.all_gather(right, "core", axis=0, tiled=True)
+    left = call(
+        left_kernel, shape((1024, 256)), (token, got), scratch=(pltpu.VMEM((256, 1024), F32),)
+    )
+    other = lax.ppermute(left, "core", [(0, 1), (1, 0)])
+    place = jnp.stack([lax.axis_index("zh"), lax.axis_index("core")]).astype(jnp.int32)
     rows = call(
         outer_kernel,
         shape((32, 64, 128)),
-        (half, got, right, pair, swapped, weight),
+        (place, left, other, right, pair, swapped, outer_output_weight),
         scratch=(
-            pltpu.VMEM((256, 1024), BF16),
-            pltpu.VMEM((256, 1024), BF16),
+            pltpu.VMEM((256, 512), BF16),
             pltpu.VMEM((256, 4096), BF16),
             pltpu.VMEM((32, 32, 128), F32),
             pltpu.VMEM((4096, 512), BF16),
-            pltpu.SemaphoreType.DMA,
-        ),
-        hbm=1,
+        ),
     )
     rows = lax.all_to_all(rows, PLANE, split_axis=0, concat_axis=0, tiled=True)
     done = call(

time: 121 us -> 118 us (0.975)
  blocking collectives: 73.5 us -> 42.4 us
  starting transfers between devices: 20.8 us -> 41.4 us
  waiting for transfers between devices: 5.95 us -> 15.9 us
  local copies, waits for them, and re-layouts: 3.79 us -> 2.14 us
    all_to_all x1 -> x0, blocking collectives: 28.9 us -> none  [on_device(): lax.all_to_all(right, 'row', split_axis=0, concat_axis=0, tiled=True)]
    all_to_all x0 -> x1, starting transfers between devices: none -> 17.2 us  [on_device(): lax.all_to_all(right, 'row', split_axis=0, concat_axis=0, tiled=True)]
    all_gather x1 -> x0, blocking collectives: 7.77 us -> none  [on_device(): right = lax.all_gather(right, 'core', axis=0, tiled=True)]
    all_to_all x0 -> x1, waiting for transfers between devices: none -> 6.44 us  [on_device(): lax.all_to_all(right, 'row', split_axis=0, concat_axis=0, tiled=True)]
    all_to_all x1, blocking collectives: 15.1 us -> 20.7 us  [on_device(): rows = lax.all_to_all(rows, PLANE, split_axis=0, concat_axis=0, tiled=True)]
    ppermute x1, waiting for transfers between devices: 0.9 us -> 4.21 us  [on_device(): swapped = lax.ppermute(swap, 'zh', [(0, 1), (1, 0)])]
    ppermute x0 -> x1, starting transfers between devices: none -> 3.27 us  [on_device(): other = lax.ppermute(left, 'core', [(0, 1), (1, 0)])]
    unnamed x31 -> x29, local copies, waits for them, and re-layouts: 3.6 us -> 1.96 us
  transfers between devices with their start and end apart: 2 -> 4, of which waited for: 2 -> 4; matrix products, arithmetic and copies ran while one was open for 0% -> 0% of each run, Pallas kernels for 2% -> 3%
where the time goes in v7:
time: 118 us; the launch traced here: 117 us
  blocking collectives  42.4 us (36%)
  starting transfers between devices  41.4 us (35%)
  waiting for transfers between devices  15.9 us (13%)
  Pallas kernels  14.2 us (12%)
  local copies, waits for them, and re-layouts  2.14 us (2%)
    all_to_all x1, blocking collectives, on_device(): got = lax.all_to_all(spread, PLANE, split_axis=0, concat_axis=0, tiled=True)  21.7 us
    all_to_all x1, blocking collectives, on_device(): rows = lax.all_to_all(rows, PLANE, split_axis=0, concat_axis=0, tiled=True)  20.7 us
    all_to_all x1, starting transfers between devices, on_device(): lax.all_to_all(right, 'row', split_axis=0, concat_axis=0, tiled=True)  17.2 us
    ppermute x1, starting transfers between devices, on_device(): swapped = lax.ppermute(swap, 'zh', [(0, 1), (1, 0)])  16.3 us
    pallas_call x7, Pallas kernels, call(): pl.pallas_call(body, out_shape=out_shape, in_specs=[pl.BlockSpec(memory_s...  14.2 us
    all_to_all x1, waiting for transfers between devices, on_device(): lax.all_to_all(right, 'row', split_axis=0, concat_axis=0, tiled=True)  6.44 us
    all_to_all x1, starting transfers between devices, on_device(): done = lax.all_to_all(done, PLANE, split_axis=0, concat_axis=0, tiled=True)  4.65 us
    ppermute x1, waiting for transfers between devices, on_device(): swapped = lax.ppermute(swap, 'zh', [(0, 1), (1, 0)])  4.21 us
  transfers between devices with their start and end apart: 4, of which 4 were waited for; matrix products, arithmetic and copies ran while one was open for 0% of the time, Pallas kernels for 3%

profile of v7, /device:TPU:1, one launch (start us, length us, event | category | flops | bytes accessed | tf_op | source)
XLA Modules:
  0.0 117.0 jit_solution(10405476349681424922)
XLA Ops:
  0.6 1.9 %shard_map.265 = (bf16[656,128]{1,0:T(8,128)(2,1)S(1)}, f32[64,8]{1,0:T(8,128)S(1)}, f32[8,128]{1,0:T(8,128)S(1)}, bf16[64,64]{1,0:T(8,128)(2,1)S(1)}) custom-call(bf16[4,64,64]{2,1,0:T(8,128)(2,1)} %refs_0_.1, s32[4,64]{1,0:T(4,128)} %refs_1_.1, bf16[64,80]{1,0:T(8,128)(2,1)} %bitcast.15, f32[1,64]{1,0:T(1,128)} %bitcast.18, bf16[8,64]{1,0:T(8,128)(2,1)} %nodes_ref.1, ...), custom_call_target="tpu_custom_call" | custom-call | tf_op jit(solution)/shard_map/pallas_call | solution.py:323
  2.5 16.3 %collective-permute-start = (bf16[656,128]{1,0:T(8,128)(2,1)S(1)}, bf16[656,128]{1,0:T(8,128)(2,1)S(1)}, u32[]{:S(2)}, u32[]{:S(2)}) collective-permute-start(bf16[656,128]{1,0:T(8,128)(2,1)S(1)} %get-tuple-element.11.own_ref), channel_id=1, source_target_pairs={{0,1},{1,0},{2,3},{3,2},{4,5},{5,4},{6,7},{7,6},{8,9},{9,8},{10,11... | collective-permute-start | bytes 503816 | tf_op jit(solution)/shard_map/ppermute | solution.py:388
  18.8 4.2 %collective-permute-done.got_ref.came_ref = bf16[656,128]{1,0:T(8,128)(2,1)S(1)} collective-permute-done((bf16[656,128]{1,0:T(8,128)(2,1)S(1)}, bf16[656,128]{1,0:T(8,128)(2,1)S(1)}, u32[]{:S(2)}, u32[]{:S(2)}) %collective-permute-start) | collective-permute-done | bytes 167968 | tf_op jit(solution)/shard_map/ppermute | solution.py:388
  23.0 1.2 %shard_map.266 = bf16[32,96,128]{2,1,0:T(8,128)(2,1)S(1)} custom-call(s32[1]{0:T(128)} %bitcast.half_ref, bf16[656,128]{1,0:T(8,128)(2,1)S(1)} %get-tuple-element.11.own_ref, bf16[656,128]{1,0:T(8,128)(2,1)S(1)} %collective-permute-done.got_ref.came_ref, bf16[64,64]{1,0:T(8,128)(2,1)S(1)} %get-tuple-element.12.factor_ref), custom_call_target="tpu_custom_call" | custom-call | tf_op jit(solution)/shard_map/pallas_call | solution.py:323
  24.2 21.7 %all_to_all.20.got_ref = bf16[32,96,128]{2,1,0:T(8,128)(2,1)S(1)} all-to-all(bf16[32,96,128]{2,1,0:T(8,128)(2,1)S(1)} %shard_map.266), channel_id=1, replica_groups=mesh['x'=4,'core'=2,'row'=8,'y'=4,'zh'=2] {'x','core','y'}, dimensions={0} | all-to-all | bytes 1572864 | tf_op jit(solution)/shard_map/all_to_all | solution.py:394
  45.9 1.2 %shard_map.267 = (bf16[8,128,128]{2,1,0:T(8,128)(2,1)}, f32[8,128]{1,0:T(8,128)S(1)}) custom-call(bf16[32,96,128]{2,1,0:T(8,128)(2,1)S(1)} %all_to_all.20.got_ref), custom_call_target="tpu_custom_call" | custom-call | tf_op jit(solution)/shard_map/pallas_call | solution.py:323
  47.1 17.2 %all-to-all-start.1 = ((bf16[8,128,128]{2,1,0:T(8,128)(2,1)}), bf16[8,128,128]{2,1,0:T(8,128)(2,1)S(1)}, u32[]{:S(2)}, u32[]{:S(2)}) async-start(bf16[8,128,128]{2,1,0:T(8,128)(2,1)} %get-tuple-element.14), calls=%async_computation.1 | async-start | bytes 524288 | tf_op jit(solution)/shard_map/all_to_all | solution.py:396
  64.4 0.0 copy-start.1
  64.4 0.6 shard_map.268.own_ref
  65.0 3.3 %collective-permute-start.1 = (bf16[1024,256]{1,0:T(8,128)(2,1)S(1)}, bf16[1024,256]{1,0:T(8,128)(2,1)S(1)}, u32[]{:S(2)}, u32[]{:S(2)}) collective-permute-start(bf16[1024,256]{1,0:T(8,128)(2,1)S(1)} %shard_map.268.own_ref), channel_id=1, source_target_pairs={{0,64},{64,0},{1,65},{65,1},{2,66},{66,2},{3,67},{67,3},{4,68},{68... | collective-permute-start | bytes 1572872 | tf_op jit(solution)/shard_map/ppermute | solution.py:400
  68.2 0.1 pad_add_fusion.place_ref
  68.3 1.4 %collective-permute-done.1.other_ref = bf16[1024,256]{1,0:T(8,128)(2,1)S(1)} collective-permute-done((bf16[1024,256]{1,0:T(8,128)(2,1)S(1)}, bf16[1024,256]{1,0:T(8,128)(2,1)S(1)}, u32[]{:S(2)}, u32[]{:S(2)}) %collective-permute-start.1) | collective-permute-done | bytes 524320 | tf_op jit(solution)/shard_map/ppermute | solution.py:400
  69.8 6.4 %all-to-all-done.1.right_in = bf16[8,128,128]{2,1,0:T(8,128)(2,1)S(1)} async-done(((bf16[8,128,128]{2,1,0:T(8,128)(2,1)}), bf16[8,128,128]{2,1,0:T(8,128)(2,1)S(1)}, u32[]{:S(2)}, u32[]{:S(2)}) %all-to-all-start.1) | async-done | bytes 262176 | tf_op jit(solution)/shard_map/all_to_all | solution.py:396
  76.2 3.1 %shard_map.269 = bf16[32,64,128]{2,1,0:T(8,128)(2,1)S(1)} custom-call(s32[2]{0:T(128)S(1)} %pad_add_fusion.place_ref, bf16[1024,256]{1,0:T(8,128)(2,1)S(1)} %shard_map.268.own_ref, bf16[1024,256]{1,0:T(8,128)(2,1)S(1)} %collective-permute-done.1.other_ref, bf16[8,128,128]{2,1,0:T(8,128)(2,1)S(1)} %all-to-all-done.1.right_in, ...), custom_call_target="tpu_custom_call" | custom-call | tf_op jit(solution)/shard_map/pallas_call | solution.py:323
  79.3 0.0 copy-start.2
  79.3 0.0 copy-start.3
  79.3 0.0 copy-start.4
  79.3 0.0 copy-start.5
  79.4 0.0 copy-start.6
  79.4 20.7 %all_to_all.21.got_ref = bf16[32,64,128]{2,1,0:T(8,128)(2,1)S(1)} all-to-all(bf16[32,64,128]{2,1,0:T(8,128)(2,1)S(1)} %shard_map.269), channel_id=1, replica_groups=mesh['x'=4,'core'=2,'row'=8,'y'=4,'zh'=2] {'x','core','y'}, dimensions={0} | all-to-all | bytes 1048576 | tf_op jit(solution)/shard_map/all_to_all | solution.py:413
  100.1 3.9 %shard_map.270 = bf16[32,16,128]{2,1,0:T(8,128)(2,1)} custom-call(s32[1]{0:T(128)} %bitcast.half_ref, bf16[32,64,128]{2,1,0:T(8,128)(2,1)S(1)} %all_to_all.21.got_ref, f32[8,128]{1,0:T(8,128)S(1)} %get-tuple-element.15.consts_ref, bf16[128,128]{1,0:T(8,128)(2,1)S(1)} %copy-done.2, bf16[128,128]{1,0:T(8,128)(2,1)S(1)} %copy-done.3, ...), custom_call_target="tpu_custom_call" | custom-call | tf_op jit(solution)/shard_map/pallas_call | solution.py:323
  104.0 4.7 %all-to-all-start.3 = ((bf16[32,16,128]{2,1,0:T(8,128)(2,1)}), bf16[32,16,128]{2,1,0:T(8,128)(2,1)S(1)}, u32[]{:S(2)}, u32[]{:S(2)}) async-start(bf16[32,16,128]{2,1,0:T(8,128)(2,1)} %shard_map.270), calls=%async_computation.3 | async-start | bytes 262144 | tf_op jit(solution)/shard_map/all_to_all | solution.py:436
  108.7 0.0 copy-start.12
  108.7 0.6 copy-done.12
  109.4 0.1 copy.29.penalty_ref
  109.5 0.1 copy.30.step_ref
  109.6 0.5 copy-done.10
  110.1 0.1 copy-done.8
  110.1 0.0 copy-done.9
  110.2 2.4 %shard_map.271 = (bf16[8,64]{1,0:T(8,128)(2,1)}, f32[3,8]{1,0:T(4,128)}) custom-call(s32[8]{0:T(128)S(1)} %copy-done.11, bf16[32,96,128]{2,1,0:T(8,128)(2,1)S(1)} %all_to_all.20.got_ref, s32[8,64]{1,0:T(8,128)S(1)} %copy-done.10, f32[64,8]{1,0:T(8,128)S(1)} %get-tuple-element.16.query_ref, bf16[8,64]{1,0:T(8,128)(2,1)S(1)} %copy-done.8, ...), custom_call_target="tpu_custom_call" | custom-call | tf_op jit(solution)/shard_map/pallas_call | solution.py:323
  112.5 3.8 %all-to-all-done.3 = bf16[32,16,128]{2,1,0:T(8,128)(2,1)S(1)} async-done(((bf16[32,16,128]{2,1,0:T(8,128)(2,1)}), bf16[32,16,128]{2,1,0:T(8,128)(2,1)S(1)}, u32[]{:S(2)}, u32[]{:S(2)}) %all-to-all-start.3) | async-done | bytes 131104 | tf_op jit(solution)/shard_map/all_to_all | solution.py:436
  116.4 0.7 copy.32
  (17 shorter events, 0.0 us)
Async XLA Ops:
  2.5 20.5 %collective-permute-start = (bf16[656,128]{1,0:T(8,128)(2,1)S(1)}, bf16[656,128]{1,0:T(8,128)(2,1)S(1)}, u32[]{:S(2)}, u32[]{:S(2)}) collective-permute-start(bf16[656,128]{1,0:T(8,128)(2,1)S(1)} %get-tuple-element.11.own_ref), channel_id=1, source_target_pairs={{0,1},{1,0},{2,3},{3,2},{4,5},{5,4},{6,7},{7,6},{8,9},{9,8},{10,11... | collective-permute-start | bytes 503816 | tf_op jit(solution)/shard_map/ppermute | solution.py:388
  47.1 29.1 %all-to-all-start.1 = ((bf16[8,128,128]{2,1,0:T(8,128)(2,1)}), bf16[8,128,128]{2,1,0:T(8,128)(2,1)S(1)}, u32[]{:S(2)}, u32[]{:S(2)}) async-start(bf16[8,128,128]{2,1,0:T(8,128)(2,1)} %get-tuple-element.14), calls=%async_computation.1 | async-start | bytes 524288 | tf_op jit(solution)/shard_map/all_to_all | solution.py:396
  64.4 11.8 %copy-start = (bf16[64,8,128]{2,1,0:T(8,128)(2,1)S(1)}, bf16[64,8,128]{2,1,0:T(8,128)(2,1)}, u32[]{:S(2)}) copy-start(bf16[64,8,128]{2,1,0:T(8,128)(2,1)} %pair_ref.1) | copy-start | bytes 393220
  64.4 11.8 %copy-start.1 = (bf16[1024,128]{1,0:T(8,128)(2,1)S(1)}, bf16[1024,128]{1,0:T(8,128)(2,1)}, u32[]{:S(2)}) copy-start(bf16[1024,128]{1,0:T(8,128)(2,1)} %weight_ref.1) | copy-start | bytes 786436
  65.0 4.8 %collective-permute-start.1 = (bf16[1024,256]{1,0:T(8,128)(2,1)S(1)}, bf16[1024,256]{1,0:T(8,128)(2,1)S(1)}, u32[]{:S(2)}, u32[]{:S(2)}) collective-permute-start(bf16[1024,256]{1,0:T(8,128)(2,1)S(1)} %shard_map.268.own_ref), channel_id=1, source_target_pairs={{0,64},{64,0},{1,65},{65,1},{2,66},{66,2},{3,67},{67,3},{4,68},{68... | collective-permute-start | bytes 1572872 | tf_op jit(solution)/shard_map/ppermute | solution.py:400
  79.3 20.8 %copy-start.2 = (bf16[128,128]{1,0:T(8,128)(2,1)S(1)}, bf16[128,128]{1,0:T(8,128)(2,1)}, u32[]{:S(2)}) copy-start(bf16[128,128]{1,0:T(8,128)(2,1)} %wq_ref.1) | copy-start | bytes 98308
  79.3 20.8 %copy-start.3 = (bf16[128,128]{1,0:T(8,128)(2,1)S(1)}, bf16[128,128]{1,0:T(8,128)(2,1)}, u32[]{:S(2)}) copy-start(bf16[128,128]{1,0:T(8,128)(2,1)} %wk_ref.1) | copy-start | bytes 98308
  79.3 20.8 %copy-start.4 = (bf16[128,128]{1,0:T(8,128)(2,1)S(1)}, bf16[128,128]{1,0:T(8,128)(2,1)}, u32[]{:S(2)}) copy-start(bf16[128,128]{1,0:T(8,128)(2,1)} %wv_ref.1) | copy-start | bytes 98308
  79.3 20.8 %copy-start.5 = (bf16[128,128]{1,0:T(8,128)(2,1)S(1)}, bf16[128,128]{1,0:T(8,128)(2,1)}, u32[]{:S(2)}) copy-start(bf16[128,128]{1,0:T(8,128)(2,1)} %wg_ref.1) | copy-start | bytes 98308
  79.4 20.8 %copy-start.6 = (bf16[128,128]{1,0:T(8,128)(2,1)S(1)}, bf16[128,128]{1,0:T(8,128)(2,1)}, u32[]{:S(2)}) copy-start(bf16[128,128]{1,0:T(8,128)(2,1)} %wo_ref.2) | copy-start | bytes 98308
  104.0 5.4 %copy-start.13 = (f32[4]{0:T(128)S(1)}, f32[4]{0:T(128)}, u32[]{:S(2)}) copy-start(f32[4]{0:T(128)} %param.51) | copy-start | bytes 52
  104.0 5.5 %copy-start.7 = (bf16[64,64]{1,0:T(8,128)(2,1)S(1)}, bf16[64,64]{1,0:T(8,128)(2,1)}, u32[]{:S(2)}) copy-start(bf16[64,64]{1,0:T(8,128)(2,1)} %wo_ref.3) | copy-start | bytes 24580
  104.0 5.5 %copy-start.11 = (s32[8]{0:T(128)S(1)}, s32[8]{0:T(128)}, u32[]{:S(2)}) copy-start(s32[8]{0:T(128)} %count_ref.1) | copy-start | bytes 100
  104.0 12.3 %all-to-all-start.3 = ((bf16[32,16,128]{2,1,0:T(8,128)(2,1)}), bf16[32,16,128]{2,1,0:T(8,128)(2,1)S(1)}, u32[]{:S(2)}, u32[]{:S(2)}) async-start(bf16[32,16,128]{2,1,0:T(8,128)(2,1)} %shard_map.270), calls=%async_computation.3 | async-start | bytes 262144 | tf_op jit(solution)/shard_map/all_to_all | solution.py:436
  108.7 0.7 copy-start.12
  109.4 0.7 copy-start.10
  109.5 0.7 copy-start.8
  109.5 0.7 copy-start.9

commit v8 on v7

--- a/solution.py
+++ b/solution.py
@@ -104,71 +104,60 @@
     swap_ref[128:144] = jnp.concatenate([kv, placed], 0).astype(BF16)
 
 
-def spread_kernel(half_ref, own_ref, got_ref, factor_ref, out_ref):
-    mine = half_ref[0] == 0
-    own, came = own_ref[0:144].astype(F32), got_ref[0:144].astype(F32)
-    one = jnp.where(mine, own, came)
-    two = jnp.where(mine, came, own)
+def spread_kernel(after_ref, block_ref, factor_ref, out_ref):
+    packed = block_ref[0:128]
     row, lane = iota((128, 64), 0), iota((128, 64), 1)
-    planes = []
-    for block in (one, two):
-        packed = block[:128].astype(BF16)
-        parts = [dot(packed, one_where(row == lane)), dot(packed, one_where(row == lane + 64))]
-        planes.append(jnp.concatenate(parts, 0).astype(BF16))
+    parts = [dot(packed, one_where(row == lane)), dot(packed, one_where(row == lane + 64))]
+    plane = jnp.concatenate(parts, 0).astype(BF16)
 
     row, source = iota((128, 1), 0), iota((128, 256), 1)
     low, even = lane_masks(8)
     for core in range(2):
         pick = one_where(source == ((row >> 5) << 6) + ((row & 31) << 1) + core)
-        parts = []
-        for p in range(2):
-            rows = dot(pick, planes[p]).astype(BF16)
-            left = dot(factor_ref[0:32], rows, 1, 1).astype(BF16).astype(F32)
-            parts += swap_lane_groups([left[k * 8 : (k + 1) * 8] for k in range(4)], low, even)
+        rows = dot(pick, plane).astype(BF16)
+        left = dot(factor_ref[0:32], rows, 1, 1).astype(BF16).astype(F32)
+        parts = swap_lane_groups([left[k * 8 : (k + 1) * 8] for k in range(4)], low, even)
         block = jnp.concatenate(parts, 0).astype(BF16)
         for to in range(32):
             if (to // 4) % 2 == core:
-                out_ref[to, 0:64] = block
-
-    kv = jnp.concatenate([one[128:136], two[128:136]], 0).astype(BF16)
-    out_ref[:, 64:80] = jnp.broadcast_to(kv[None], (32, 16, 128))
-    place = jnp.concatenate([one[136:144], two[136:144]], 0)
+                out_ref[to, 0:32] = block
+
+    nodes = block_ref[128:144].astype(F32)
     widened = dot(factor_ref[32:64], one_where(iota((32, 128), 1) == iota((32, 128), 0) + 32), 0, 0).astype(BF16)
-    both = jnp.concatenate(planes, 0)
-    for g in range(4):
-        row, source = iota((128, 1), 0) + g * 128, iota((128, 512), 1)
-        wanted = (((row >> 3) & 1) << 8) + (((row >> 1) & 3) << 6) + ((row >> 4) << 1) + (row & 1)
-        moved = dot(one_where(source == wanted), both).astype(BF16)
-        right = dot(moved, widened).reshape(8, 16, 128) + place[None]
-        out_ref[g * 8 : (g + 1) * 8, 80:96] = right.astype(BF16)
-
-
-def right_kernel(got_ref, out_ref, token_ref):
+    row, source = iota((256, 1), 0), iota((256, 256), 1)
+    wanted = (((row >> 1) & 3) << 6) + ((row >> 3) << 1) + (row & 1)
+    moved = dot(one_where(source == wanted), plane).astype(BF16)
+    right = dot(moved, widened).reshape(32, 8, 128) + nodes[None, 8:16]
+    kv = jnp.broadcast_to(nodes[None, 0:8], (32, 8, 128))
+    out_ref[:, 32:48] = jnp.concatenate([kv, right], 1).astype(BF16)
+
+
+def right_kernel(own_ref, came_ref, out_ref, token_ref):
     token_ref[...] = jnp.zeros_like(token_ref)
-    rows = got_ref[:, 80:96].reshape(512, 128)
     row, source = iota((128, 1), 0), iota((128, 512), 1)
-    start = ((row >> 2) << 4) + ((row & 3) << 1)
+    start = ((row >> 2) << 4) + ((row & 3) << 1) + 8
     at, lane = iota((128, 128), 0), iota((128, 128), 1)
     total = jnp.zeros((128, 128), F32)
-    for plane in range(2):
+    for plane, got_ref in enumerate((own_ref, came_ref)):
+        rows = got_ref[:, 32:48].reshape(512, 128)
         for column in range(2):
-            picked = dot(one_where(source == start + plane * 8 + column), rows).astype(BF16)
+            picked = dot(one_where(source == start + column), rows).astype(BF16)
             shift = (plane * 2 + column) * 32
             keep = (lane >= shift) & (lane < shift + 32)
             total = total + dot(picked, one_where((at + shift == lane + 32) & keep))
     out_ref[...] = jnp.broadcast_to(total.astype(BF16)[None], out_ref.shape)
 
 
-def left_kernel(after_ref, got_ref, out_ref, left):
+def left_kernel(after_ref, own_ref, came_ref, out_ref, left):
     row = iota((256, 1), 0)
-    wanted = (((row >> 2) & 3) << 6) + (((row >> 4) & 1) << 5) + ((row & 3) << 3) + (row >> 5)
+    wanted = (((row >> 2) & 7) << 5) + ((row & 3) << 3) + (row >> 5)
     turn = one_where(iota((256, 256), 1) == wanted)
-    for g in range(8):
-        part = dot(turn, got_ref[g * 4 : (g + 1) * 4, 0:64].reshape(256, 128))
-        for q in range(8):
-            for p in range(2):
-                at = p * 128 + g * 16
-                left[at : at + 16, q * 128 : (q + 1) * 128] = part[q * 32 + p * 16 : q * 32 + p * 16 + 16]
+    for p, got_ref in enumerate((own_ref, came_ref)):
+        for g in range(4):
+            part = dot(turn, got_ref[g * 8 : (g + 1) * 8, 0:32].reshape(256, 128))
+            at = p * 128 + g * 32
+            for q in range(8):
+                left[at : at + 32, q * 128 : (q + 1) * 128] = part[q * 32 : (q + 1) * 32]
     for q in range(8):
         out_ref[q * 128 : (q + 1) * 128] = left[:, q * 128 : (q + 1) * 128].T.astype(BF16)
 
@@ -233,11 +222,11 @@
         split = normed.reshape(32, 2, 8, 128)
         asking = jnp.where(mine, split[:, 0], split[:, 1]).reshape(256, 128).astype(BF16)
         normed = normed.astype(BF16)
-        q_s[...] = dot(asking, wq_ref[...]).astype(BF16)
-        gate_s[...] = dot(asking, wg_ref[...])
-        k_s[...] = dot(normed, wk_ref[...]).astype(BF16)
-        v_s[...] = dot(normed, wv_ref[...]).astype(BF16)
-        keys, values = k_s[...], v_s[...]
+        asked = dot(asking, jnp.concatenate([wq_ref[...], wg_ref[...]], 1))
+        q_s[...] = asked[:, :128].astype(BF16)
+        gate_s[...] = asked[:, 128:]
+        given = dot(normed, jnp.concatenate([wk_ref[...], wv_ref[...]], 1)).astype(BF16)
+        keys, values = given[:, :128], given[:, 128:]
         head_keys = [jnp.where(head_of == h, keys, zero) for h in range(PAIR_HEADS)]
         head_values = [
             jnp.concatenate(
@@ -259,10 +248,17 @@
 
 
 def node_kernel(
-    count_ref, got_ref, index_ref, query_ref, nodes_ref, coords_ref, wo_ref, penalty_ref, step_ref, nodes_out, coords_out
+    count_ref, half_ref, after_ref, own_ref, came_ref, index_ref, query_ref, nodes_ref, coords_ref, wo_ref, penalty_ref, step_ref, nodes_out, coords_out, token_ref
 ):
-    kv_table = got_ref[:, 64:80].reshape(512, 128)
-    place_table = got_ref[:, 80:96].reshape(512, 128)
+    token_ref[...] = after_ref[...]
+    tables = [[], []]
+    for got_ref in (own_ref, came_ref):
+        both = got_ref[:, 32:48].reshape(32, 2, 8, 128)
+        for n in range(2):
+            tables[n].append(both[:, n].reshape(256, 128))
+    kv_table, place_table = [jnp.concatenate(t, 0) for t in tables]
+    index = index_ref[...]
+    index = ((index >> 4) << 3) + (index & 7) + ((((index >> 3) & 1) ^ half_ref[0]) << 8)
     local, slots = index_ref.shape
     width, dim = nodes_ref.shape[1], nodes_ref.shape[1] // NODE_HEADS
     lane = iota((1, slots), 1)
@@ -270,7 +266,7 @@
     mixed = jnp.zeros((width, local), F32)
     moved = jnp.zeros((3, local), F32)
     for i in range(local):
-        picked = one_where(iota((512, slots), 0) == index_ref[i : i + 1, :])
+        picked = one_where(iota((512, slots), 0) == index[i : i + 1, :])
         near = dot(kv_table, picked, 0, 0)
         where = dot(place_table, picked, 0, 0)
         position = [
@@ -311,7 +307,7 @@
     return kernel
 
 
-def call(body, out_shape, args, scratch=(), fetch=False, hbm=0):
+def call(body, out_shape, args, scratch=(), fetch=False, hbm=0, cost=None):
     scratch, args = list(scratch), list(args)
     if fetch:
         body = with_fetch(body, len(args))
@@ -327,6 +323,7 @@
         out_specs=jax.tree.map(lambda _: pl.BlockSpec(memory_space=pltpu.VMEM), out_shape),
         scratch_shapes=scratch,
         compiler_params=pltpu.CompilerParams(vmem_limit_bytes=VMEM_LIMIT),
+        cost_estimate=cost,
     )(*args)
 
 
@@ -386,16 +383,33 @@
         fetch=True,
     )
     swapped = lax.ppermute(swap, "zh", [(0, 1), (1, 0)])
-    spread = call(
-        spread_kernel,
-        shape((32, 96, 128)),
-        (half, swap, swapped, factors),
-    )
+    spread = call(spread_kernel, shape((32, 48, 128)), (consts, swap, factors))
+    own = lax.all_to_all(spread, PLANE, split_axis=0, concat_axis=0, tiled=True)
+    long = pl.CostEstimate(flops=1 << 36, bytes_accessed=1 << 28, transcendentals=0)
+    spread = call(spread_kernel, shape((32, 48, 128)), (consts, swapped, factors), cost=long)
     got = lax.all_to_all(spread, PLANE, split_axis=0, concat_axis=0, tiled=True)
-    right, token = call(right_kernel, (shape((8, 128, 128)), shape((8, 128), F32)), (got,))
+    right, token = call(right_kernel, (shape((8, 128, 128)), shape((8, 128), F32)), (own, got))
     right = lax.all_to_all(right, "row", split_axis=0, concat_axis=0, tiled=True)
+    nodes_out, coords_out, token = call(
+        node_kernel,
+        (shape(nodes.shape), shape(coords.shape, F32), shape((8, 128), F32)),
+        (
+            neighbour_count,
+            half,
+            token,
+            own,
+            got,
+            neighbour_index,
+            node_query,
+            nodes,
+            coords,
+            node_output_weight,
+            distance_penalty.reshape(-1, 1),
+            coordinate_step.reshape(-1, 1),
+        ),
+    )
     left = call(
-        left_kernel, shape((1024, 256)), (token, got), scratch=(pltpu.VMEM((256, 1024), F32),)
+        left_kernel, shape((1024, 256)), (token, own, got), scratch=(pltpu.VMEM((256, 1024), F32),)
     )
     other = lax.ppermute(left, "core", [(0, 1), (1, 0)])
     place = jnp.stack([lax.axis_index("zh"), lax.axis_index("core")]).astype(jnp.int32)
@@ -435,21 +449,6 @@
     )
     done = lax.all_to_all(done, PLANE, split_axis=0, concat_axis=0, tiled=True)
     pair_out = done.reshape(pair.shape)
-    nodes_out, coords_out = call(
-        node_kernel,
-        (shape(nodes.shape), shape(coords.shape, F32)),
-        (
-            neighbour_count,
-            got,
-            neighbour_index,
-            node_query,
-            nodes,
-            coords,
-            node_output_weight,
-            distance_penalty.reshape(-1, 1),
-            coordinate_step.reshape(-1, 1),
-        ),
-    )
     return (pair_out, nodes_out, coords_out)
 
 

time: 118 us -> 112 us (0.949)
  starting transfers between devices: 41.4 us -> 34.1 us
  blocking collectives: 42.4 us -> 45.6 us
  waiting for transfers between devices: 15.9 us -> 14.7 us
    all_to_all x0 -> x1, blocking collectives: none -> 11.9 us  [on_device(): done = lax.all_to_all(done, PLANE, split_axis=0, concat_axis=0, tiled=True)]
    all_to_all x1, starting transfers between devices: 17.2 us -> 6.86 us  [on_device(): lax.all_to_all(right, 'row', split_axis=0, concat_axis=0, tiled=True)]
    all_to_all x1, blocking collectives: 21.7 us -> 14 us  [on_device(): got = lax.all_to_all(spread, PLANE, split_axis=0, concat_axis=0, tiled=True)]
    all_to_all x1, waiting for transfers between devices: 3.83 us -> 9.35 us  [on_device(): own = lax.all_to_all(spread, PLANE, split_axis=0, concat_axis=0, tiled=True)]
    ppermute x1, waiting for transfers between devices: 4.21 us -> 0.01 us  [on_device(): swapped = lax.ppermute(swap, 'zh', [(0, 1), (1, 0)])]
    all_to_all x1, starting transfers between devices: 4.65 us -> 8.04 us  [on_device(): own = lax.all_to_all(spread, PLANE, split_axis=0, concat_axis=0, tiled=True)]
    all_to_all x1, waiting for transfers between devices: 6.44 us -> 3.9 us  [on_device(): lax.all_to_all(right, 'row', split_axis=0, concat_axis=0, tiled=True)]
    pallas_call x7 -> x8, Pallas kernels: 14.2 us -> 14.3 us  [call(): pl.pallas_call(body, out_shape=out_shape, in_specs=[pl.BlockSpec(memory_s...]
  transfers between devices with their start and end apart: 4 -> 4, of which waited for: 4 -> 3; matrix products, arithmetic and copies ran while one was open for 0% -> 0% of each run, Pallas kernels for 3% -> 4%
where the time goes in v8:
time: 112 us; the launch traced here: 111 us
  blocking collectives  45.6 us (41%)
  starting transfers between devices  34.1 us (30%)
  waiting for transfers between devices  14.7 us (13%)
  Pallas kernels  14.3 us (13%)
  local copies, waits for them, and re-layouts  1.59 us (1%)
    all_to_all x1, blocking collectives, on_device(): rows = lax.all_to_all(rows, PLANE, split_axis=0, concat_axis=0, tiled=True)  19.7 us
    ppermute x1, starting transfers between devices, on_device(): swapped = lax.ppermute(swap, 'zh', [(0, 1), (1, 0)])  16.3 us
    pallas_call x8, Pallas kernels, call(): pl.pallas_call(body, out_shape=out_shape, in_specs=[pl.BlockSpec(memory_s...  14.3 us
    all_to_all x1, blocking collectives, on_device(): got = lax.all_to_all(spread, PLANE, split_axis=0, concat_axis=0, tiled=True)  14 us
    all_to_all x1, blocking collectives, on_device(): done = lax.all_to_all(done, PLANE, split_axis=0, concat_axis=0, tiled=True)  11.9 us
    all_to_all x1, waiting for transfers between devices, on_device(): own = lax.all_to_all(spread, PLANE, split_axis=0, concat_axis=0, tiled=True)  9.35 us
    all_to_all x1, starting transfers between devices, on_device(): own = lax.all_to_all(spread, PLANE, split_axis=0, concat_axis=0, tiled=True)  8.04 us
    all_to_all x1, starting transfers between devices, on_device(): lax.all_to_all(right, 'row', split_axis=0, concat_axis=0, tiled=True)  6.86 us
  transfers between devices with their start and end apart: 4, of which 3 were waited for; matrix products, arithmetic and copies ran while one was open for 0% of the time, Pallas kernels for 4%

profile of v8, /device:TPU:1, one launch (start us, length us, event | category | flops | bytes accessed | tf_op | source)
XLA Modules:
  0.0 111.2 jit_solution(16926102817921159559)
XLA Ops:
  0.6 1.9 %shard_map.265 = (bf16[656,128]{1,0:T(8,128)(2,1)S(1)}, f32[64,8]{1,0:T(8,128)S(1)}, f32[8,128]{1,0:T(8,128)S(1)}, bf16[64,64]{1,0:T(8,128)(2,1)S(1)}) custom-call(bf16[4,64,64]{2,1,0:T(8,128)(2,1)} %refs_0_.1, s32[4,64]{1,0:T(4,128)} %refs_1_.1, bf16[64,80]{1,0:T(8,128)(2,1)} %bitcast.15, f32[1,64]{1,0:T(1,128)} %bitcast.18, bf16[8,64]{1,0:T(8,128)(2,1)} %nodes_ref.1, ...), custom_call_target="tpu_custom_call" | custom-call | tf_op jit(solution)/shard_map/pallas_call | solution.py:319
  2.5 16.3 %collective-permute-start = (bf16[656,128]{1,0:T(8,128)(2,1)S(1)}, bf16[656,128]{1,0:T(8,128)(2,1)S(1)}, u32[]{:S(2)}, u32[]{:S(2)}) collective-permute-start(bf16[656,128]{1,0:T(8,128)(2,1)S(1)} %get-tuple-element.13.block_ref), channel_id=1, source_target_pairs={{0,1},{1,0},{2,3},{3,2},{4,5},{5,4},{6,7},{7,6},{8,9},{9,8},{10,11... | collective-permute-start | bytes 503816 | tf_op jit(solution)/shard_map/ppermute | solution.py:385
  18.8 1.4 %shard_map.266 = bf16[32,48,128]{2,1,0:T(8,128)(2,1)} custom-call(f32[8,128]{1,0:T(8,128)S(1)} %get-tuple-element.12.after_ref.consts_ref, bf16[656,128]{1,0:T(8,128)(2,1)S(1)} %get-tuple-element.13.block_ref, bf16[64,64]{1,0:T(8,128)(2,1)S(1)} %get-tuple-element.14.factor_ref), custom_call_target="tpu_custom_call" | custom-call | tf_op jit(solution)/shard_map/pallas_call | solution.py:319
  20.2 8.0 %all-to-all-start = ((bf16[32,48,128]{2,1,0:T(8,128)(2,1)}), bf16[32,48,128]{2,1,0:T(8,128)(2,1)S(1)}, u32[]{:S(2)}, u32[]{:S(2)}) async-start(bf16[32,48,128]{2,1,0:T(8,128)(2,1)} %shard_map.266), calls=%async_computation | async-start | bytes 786432 | tf_op jit(solution)/shard_map/all_to_all | solution.py:387
  28.2 0.0 copy-start.12
  28.2 0.0 copy-start.13
  28.3 0.0 copy-start.10
  28.3 0.0 copy-start.11
  28.3 0.6 shard_map.267
  28.9 9.3 %all-to-all-done.own_ref = bf16[32,48,128]{2,1,0:T(8,128)(2,1)S(1)} async-done(((bf16[32,48,128]{2,1,0:T(8,128)(2,1)}), bf16[32,48,128]{2,1,0:T(8,128)(2,1)S(1)}, u32[]{:S(2)}, u32[]{:S(2)}) %all-to-all-start) | async-done | bytes 393248 | tf_op jit(solution)/shard_map/all_to_all | solution.py:387
  38.3 14.0 %all_to_all.25.came_ref = bf16[32,48,128]{2,1,0:T(8,128)(2,1)S(1)} all-to-all(bf16[32,48,128]{2,1,0:T(8,128)(2,1)S(1)} %shard_map.267), channel_id=1, replica_groups=mesh['x'=4,'core'=2,'row'=8,'y'=4,'zh'=2] {'x','core','y'}, dimensions={0} | all-to-all | bytes 786432 | tf_op jit(solution)/shard_map/all_to_all | solution.py:390
  52.3 1.2 %shard_map.268 = (bf16[8,128,128]{2,1,0:T(8,128)(2,1)}, f32[8,128]{1,0:T(8,128)S(1)}) custom-call(bf16[32,48,128]{2,1,0:T(8,128)(2,1)S(1)} %all-to-all-done.own_ref, bf16[32,48,128]{2,1,0:T(8,128)(2,1)S(1)} %all_to_all.25.came_ref), custom_call_target="tpu_custom_call" | custom-call | tf_op jit(solution)/shard_map/pallas_call | solution.py:319
  53.5 6.9 %all-to-all-start.2 = ((bf16[8,128,128]{2,1,0:T(8,128)(2,1)}), bf16[8,128,128]{2,1,0:T(8,128)(2,1)S(1)}, u32[]{:S(2)}, u32[]{:S(2)}) async-start(bf16[8,128,128]{2,1,0:T(8,128)(2,1)} %get-tuple-element.18), calls=%async_computation.2 | async-start | bytes 524288 | tf_op jit(solution)/shard_map/all_to_all | solution.py:392
  60.4 0.1 copy.29.penalty_ref
  60.5 0.1 copy.30.step_ref
  60.6 0.5 copy-done.7
  61.1 0.2 copy-done.9
  61.3 0.0 copy-done.8
  61.3 2.4 %shard_map.269 = (bf16[8,64]{1,0:T(8,128)(2,1)}, f32[3,8]{1,0:T(4,128)}, f32[8,128]{1,0:T(8,128)S(1)}) custom-call(s32[8]{0:T(128)S(1)} %copy-done.11, s32[1]{0:T(128)} %bitcast.half_ref, f32[8,128]{1,0:T(8,128)S(1)} %get-tuple-element.15.after_ref, bf16[32,48,128]{2,1,0:T(8,128)(2,1)S(1)} %all-to-all-done.own_ref, ...), custom_call_target="tpu_custom_call" | custom-call | tf_op jit(solution)/shard_map/pallas_call | solution.py:319
  63.7 0.6 shard_map.270.own_ref
  64.2 2.9 %collective-permute-start.1 = (bf16[1024,256]{1,0:T(8,128)(2,1)S(1)}, bf16[1024,256]{1,0:T(8,128)(2,1)S(1)}, u32[]{:S(2)}, u32[]{:S(2)}) collective-permute-start(bf16[1024,256]{1,0:T(8,128)(2,1)S(1)} %shard_map.270.own_ref), channel_id=1, source_target_pairs={{0,64},{64,0},{1,65},{65,1},{2,66},{66,2},{3,67},{67,3},{4,68},{68... | collective-permute-start | bytes 1572872 | tf_op jit(solution)/shard_map/ppermute | solution.py:414
  67.2 0.1 pad_add_fusion.place_ref
  67.2 1.4 %collective-permute-done.1.other_ref = bf16[1024,256]{1,0:T(8,128)(2,1)S(1)} collective-permute-done((bf16[1024,256]{1,0:T(8,128)(2,1)S(1)}, bf16[1024,256]{1,0:T(8,128)(2,1)S(1)}, u32[]{:S(2)}, u32[]{:S(2)}) %collective-permute-start.1) | collective-permute-done | bytes 524320 | tf_op jit(solution)/shard_map/ppermute | solution.py:414
  68.7 3.9 %all-to-all-done.2.right_in = bf16[8,128,128]{2,1,0:T(8,128)(2,1)S(1)} async-done(((bf16[8,128,128]{2,1,0:T(8,128)(2,1)}), bf16[8,128,128]{2,1,0:T(8,128)(2,1)S(1)}, u32[]{:S(2)}, u32[]{:S(2)}) %all-to-all-start.2) | async-done | bytes 262176 | tf_op jit(solution)/shard_map/all_to_all | solution.py:392
  72.6 3.1 %shard_map.271 = bf16[32,64,128]{2,1,0:T(8,128)(2,1)S(1)} custom-call(s32[2]{0:T(128)S(1)} %pad_add_fusion.place_ref, bf16[1024,256]{1,0:T(8,128)(2,1)S(1)} %shard_map.270.own_ref, bf16[1024,256]{1,0:T(8,128)(2,1)S(1)} %collective-permute-done.1.other_ref, bf16[8,128,128]{2,1,0:T(8,128)(2,1)S(1)} %all-to-all-done.2.right_in, ...), custom_call_target="tpu_custom_call" | custom-call | tf_op jit(solution)/shard_map/pallas_call | solution.py:319
  75.7 0.0 copy-start.2
  75.7 0.0 copy-start.5
  75.7 0.0 copy-start.6
  75.7 19.7 %all_to_all.26.got_ref = bf16[32,64,128]{2,1,0:T(8,128)(2,1)S(1)} all-to-all(bf16[32,64,128]{2,1,0:T(8,128)(2,1)S(1)} %shard_map.271), channel_id=1, replica_groups=mesh['x'=4,'core'=2,'row'=8,'y'=4,'zh'=2] {'x','core','y'}, dimensions={0} | all-to-all | bytes 1048576 | tf_op jit(solution)/shard_map/all_to_all | solution.py:427
  95.5 3.2 %shard_map.272 = bf16[32,16,128]{2,1,0:T(8,128)(2,1)S(1)} custom-call(s32[1]{0:T(128)} %bitcast.half_ref, bf16[32,64,128]{2,1,0:T(8,128)(2,1)S(1)} %all_to_all.26.got_ref, f32[8,128]{1,0:T(8,128)S(1)} %get-tuple-element.12.after_ref.consts_ref, bf16[128,128]{1,0:T(8,128)(2,1)S(1)} %copy-done.2, bf16[128,128]{1,0:T(8,128)(2,1)S(1)} %copy-done.3, ...), custom_call_target="tpu_custom_call" | custom-call | tf_op jit(solution)/shard_map/pallas_call | solution.py:319
  98.7 11.9 %all_to_all.27 = bf16[32,16,128]{2,1,0:T(8,128)(2,1)S(1)} all-to-all(bf16[32,16,128]{2,1,0:T(8,128)(2,1)S(1)} %shard_map.272), channel_id=1, replica_groups=mesh['x'=4,'core'=2,'row'=8,'y'=4,'zh'=2] {'x','core','y'}, dimensions={0} | all-to-all | bytes 262144 | tf_op jit(solution)/shard_map/all_to_all | solution.py:450
  110.6 0.7 copy.32
  (19 shorter events, 0.0 us)
Async XLA Ops:
  2.5 25.7 %collective-permute-start = (bf16[656,128]{1,0:T(8,128)(2,1)S(1)}, bf16[656,128]{1,0:T(8,128)(2,1)S(1)}, u32[]{:S(2)}, u32[]{:S(2)}) collective-permute-start(bf16[656,128]{1,0:T(8,128)(2,1)S(1)} %get-tuple-element.13.block_ref), channel_id=1, source_target_pairs={{0,1},{1,0},{2,3},{3,2},{4,5},{5,4},{6,7},{7,6},{8,9},{9,8},{10,11... | collective-permute-start | bytes 503816 | tf_op jit(solution)/shard_map/ppermute | solution.py:385
  20.2 18.1 %all-to-all-start = ((bf16[32,48,128]{2,1,0:T(8,128)(2,1)}), bf16[32,48,128]{2,1,0:T(8,128)(2,1)S(1)}, u32[]{:S(2)}, u32[]{:S(2)}) async-start(bf16[32,48,128]{2,1,0:T(8,128)(2,1)} %shard_map.266), calls=%async_computation | async-start | bytes 786432 | tf_op jit(solution)/shard_map/all_to_all | solution.py:387
  28.2 32.2 %copy-start.12 = (f32[4]{0:T(128)S(1)}, f32[4]{0:T(128)}, u32[]{:S(2)}) copy-start(f32[4]{0:T(128)} %param.50) | copy-start | bytes 52
  28.2 32.3 %copy-start.13 = (f32[4]{0:T(128)S(1)}, f32[4]{0:T(128)}, u32[]{:S(2)}) copy-start(f32[4]{0:T(128)} %param.51) | copy-start | bytes 52
  28.3 32.3 %copy-start.10 = (s32[8,64]{1,0:T(8,128)S(1)}, s32[8,64]{1,0:T(8,128)}, u32[]{:S(2)}) copy-start(s32[8,64]{1,0:T(8,128)} %index_ref.1) | copy-start | bytes 6148
  28.3 32.3 %copy-start.11 = (s32[8]{0:T(128)S(1)}, s32[8]{0:T(128)}, u32[]{:S(2)}) copy-start(s32[8]{0:T(128)} %count_ref.1) | copy-start | bytes 100
  53.5 19.0 %all-to-all-start.2 = ((bf16[8,128,128]{2,1,0:T(8,128)(2,1)}), bf16[8,128,128]{2,1,0:T(8,128)(2,1)S(1)}, u32[]{:S(2)}, u32[]{:S(2)}) async-start(bf16[8,128,128]{2,1,0:T(8,128)(2,1)} %get-tuple-element.18), calls=%async_computation.2 | async-start | bytes 524288 | tf_op jit(solution)/shard_map/all_to_all | solution.py:392
  60.4 0.7 copy-start.7
  60.6 0.7 copy-start.9
  60.6 0.7 copy-start.8
  63.7 8.9 %copy-start = (bf16[64,8,128]{2,1,0:T(8,128)(2,1)S(1)}, bf16[64,8,128]{2,1,0:T(8,128)(2,1)}, u32[]{:S(2)}) copy-start(bf16[64,8,128]{2,1,0:T(8,128)(2,1)} %pair_ref.1) | copy-start | bytes 393220
  63.7 8.9 %copy-start.1 = (bf16[1024,128]{1,0:T(8,128)(2,1)S(1)}, bf16[1024,128]{1,0:T(8,128)(2,1)}, u32[]{:S(2)}) copy-start(bf16[1024,128]{1,0:T(8,128)(2,1)} %weight_ref.1) | copy-start | bytes 786436
  64.2 4.4 %collective-permute-start.1 = (bf16[1024,256]{1,0:T(8,128)(2,1)S(1)}, bf16[1024,256]{1,0:T(8,128)(2,1)S(1)}, u32[]{:S(2)}, u32[]{:S(2)}) collective-permute-start(bf16[1024,256]{1,0:T(8,128)(2,1)S(1)} %shard_map.270.own_ref), channel_id=1, source_target_pairs={{0,64},{64,0},{1,65},{65,1},{2,66},{66,2},{3,67},{67,3},{4,68},{68... | collective-permute-start | bytes 1572872 | tf_op jit(solution)/shard_map/ppermute | solution.py:414
  75.7 19.8 %copy-start.2 = (bf16[128,128]{1,0:T(8,128)(2,1)S(1)}, bf16[128,128]{1,0:T(8,128)(2,1)}, u32[]{:S(2)}) copy-start(bf16[128,128]{1,0:T(8,128)(2,1)} %wq_ref.1) | copy-start | bytes 98308
  75.7 19.8 %copy-start.3 = (bf16[128,128]{1,0:T(8,128)(2,1)S(1)}, bf16[128,128]{1,0:T(8,128)(2,1)}, u32[]{:S(2)}) copy-start(bf16[128,128]{1,0:T(8,128)(2,1)} %wk_ref.1) | copy-start | bytes 98308
  75.7 19.7 %copy-start.4 = (bf16[128,128]{1,0:T(8,128)(2,1)S(1)}, bf16[128,128]{1,0:T(8,128)(2,1)}, u32[]{:S(2)}) copy-start(bf16[128,128]{1,0:T(8,128)(2,1)} %wv_ref.1) | copy-start | bytes 98308
  75.7 19.7 %copy-start.5 = (bf16[128,128]{1,0:T(8,128)(2,1)S(1)}, bf16[128,128]{1,0:T(8,128)(2,1)}, u32[]{:S(2)}) copy-start(bf16[128,128]{1,0:T(8,128)(2,1)} %wg_ref.1) | copy-start | bytes 98308
  75.7 19.7 %copy-start.6 = (bf16[128,128]{1,0:T(8,128)(2,1)S(1)}, bf16[128,128]{1,0:T(8,128)(2,1)}, u32[]{:S(2)}) copy-start(bf16[128,128]{1,0:T(8,128)(2,1)} %wo_ref.3) | copy-start | bytes 98308

commit v9 on v8

--- a/solution.py
+++ b/solution.py
@@ -104,7 +104,12 @@
     swap_ref[128:144] = jnp.concatenate([kv, placed], 0).astype(BF16)
 
 
-def spread_kernel(after_ref, block_ref, factor_ref, out_ref):
+def own_spread_kernel(pair_ref, block_ref, factor_ref, out_ref):
+    out_ref[:, 48:64] = pair_ref[...]
+    spread_kernel(block_ref, factor_ref, out_ref)
+
+
+def spread_kernel(block_ref, factor_ref, out_ref):
     packed = block_ref[0:128]
     row, lane = iota((128, 64), 0), iota((128, 64), 1)
     parts = [dot(packed, one_where(row == lane)), dot(packed, one_where(row == lane + 64))]
@@ -163,7 +168,7 @@
 
 
 def outer_kernel(
-    place_ref, own_ref, other_ref, right_in, pair_ref, came_ref, weight_ref, out_ref, right, joined, update, weight
+    place_ref, own_ref, other_ref, right_in, came_ref, weight_ref, out_ref, right, joined, update, weight
 ):
     weight[...] = jnp.zeros_like(weight)
     for q in range(8):
@@ -186,21 +191,18 @@
                     joined[to : to + 32, at : at + 128] = product[
                         k * 32 : (k + 1) * 32, t * 128 : (t + 1) * 128
                     ]
-    first = iota((64, 16, 128), 1) // 8 == place_ref[0]
-    kept, came = pair_ref[...].astype(F32), came_ref[144:656].reshape(64, 8, 128).astype(F32)
-    pairs = jnp.where(first, jnp.concatenate([kept, kept], 1), jnp.concatenate([came, came], 1))
-    out_ref[:, 32:64] = pairs.reshape(32, 32, 128).astype(BF16)
+    out_ref[:, 32:48] = came_ref[144:656].reshape(32, 16, 128)
     rows = dot(joined[...], weight[...])
     for t in range(8):
         for j in range(4):
             update[:, t * 4 + j, :] = rows[t * 32 : (t + 1) * 32, j * 128 : (j + 1) * 128]
-    core = place_ref[1]
+    core = place_ref[0]
     out_ref[:, pl.ds(pl.multiple_of(core * 16, 16), 16)] = update[:, 0:16].astype(BF16)
     out_ref[:, pl.ds(pl.multiple_of((1 - core) * 16, 16), 16)] = update[:, 16:32].astype(BF16)
 
 
 def attend_kernel(
-    half_ref, got_ref, consts_ref, wq_ref, wk_ref, wv_ref, wg_ref, wo_ref, out_ref, q_s, k_s, v_s, mid_s, gate_s, done_s
+    half_ref, own_ref, got_ref, consts_ref, wq_ref, wk_ref, wv_ref, wg_ref, wo_ref, out_ref, q_s, k_s, v_s, mid_s, gate_s, done_s
 ):
     mine = half_ref[0] == 0
     factor = 32 ** (-0.5) * math.log2(math.e)
@@ -213,8 +215,10 @@
     updates = dot(turn, updates)
     for p in range(2):
         update = updates[:, p * 128 : (p + 1) * 128]
-        pair = got_ref[:, 32:64].reshape(32, 2, 16, 128)[:, p].reshape(512, 128)
-        pair_mid = update + pair.astype(F32) + consts_ref[0:1]
+        own = own_ref[:, 48:64].reshape(32, 2, 8, 128)[:, p].astype(F32)
+        came = got_ref[:, 32:48].reshape(32, 2, 8, 128)[:, p].astype(F32)
+        pair = [jnp.where(mine, own, came)[:, None], jnp.where(mine, came, own)[:, None]]
+        pair_mid = update + jnp.concatenate(pair, 1).reshape(512, 128) + consts_ref[0:1]
         pair_mid = pair_mid.astype(BF16).astype(F32)
         normed = layer_normalize(pair_mid, consts_ref[1:2])
         split = pair_mid.reshape(32, 2, 8, 128)
@@ -383,10 +387,10 @@
         fetch=True,
     )
     swapped = lax.ppermute(swap, "zh", [(0, 1), (1, 0)])
-    spread = call(spread_kernel, shape((32, 48, 128)), (consts, swap, factors))
+    spread = call(own_spread_kernel, shape((32, 64, 128)), (pair.reshape(32, 16, 128), swap, factors))
     own = lax.all_to_all(spread, PLANE, split_axis=0, concat_axis=0, tiled=True)
     long = pl.CostEstimate(flops=1 << 36, bytes_accessed=1 << 28, transcendentals=0)
-    spread = call(spread_kernel, shape((32, 48, 128)), (consts, swapped, factors), cost=long)
+    spread = call(spread_kernel, shape((32, 48, 128)), (swapped, factors), cost=long)
     got = lax.all_to_all(spread, PLANE, split_axis=0, concat_axis=0, tiled=True)
     right, token = call(right_kernel, (shape((8, 128, 128)), shape((8, 128), F32)), (own, got))
     right = lax.all_to_all(right, "row", split_axis=0, concat_axis=0, tiled=True)
@@ -412,11 +416,11 @@
         left_kernel, shape((1024, 256)), (token, own, got), scratch=(pltpu.VMEM((256, 1024), F32),)
     )
     other = lax.ppermute(left, "core", [(0, 1), (1, 0)])
-    place = jnp.stack([lax.axis_index("zh"), lax.axis_index("core")]).astype(jnp.int32)
+    place = lax.axis_index("core").reshape(1).astype(jnp.int32)
     rows = call(
         outer_kernel,
-        shape((32, 64, 128)),
-        (place, left, other, right, pair, swapped, outer_output_weight),
+        shape((32, 48, 128)),
+        (place, left, other, right, swapped, outer_output_weight),
         scratch=(
             pltpu.VMEM((256, 512), BF16),
             pltpu.VMEM((256, 4096), BF16),
@@ -430,6 +434,7 @@
         shape((32, 16, 128)),
         (
             half,
+            own,
             rows,
             consts,
             pair_query_weight,

time: 112 us -> 110 us (0.982)
  starting transfers between devices: 34.1 us -> 32.7 us
    all_to_all x1, starting transfers between devices: 6.86 us -> 5.47 us  [on_device(): lax.all_to_all(right, 'row', split_axis=0, concat_axis=0, tiled=True)]
  transfers between devices with their start and end apart: 4 -> 4, of which waited for: 3 -> 3; matrix products, arithmetic and copies ran while one was open for 0% -> 0% of each run, Pallas kernels for 4% -> 5%
where the time goes in v9:
time: 110 us; the launch traced here: 109 us
  blocking collectives  44.6 us (41%)
  starting transfers between devices  32.7 us (30%)
  waiting for transfers between devices  15.8 us (14%)
  Pallas kernels  13.7 us (12%)
  local copies, waits for them, and re-layouts  1.6 us (1%)
    all_to_all x1, blocking collectives, on_device(): rows = lax.all_to_all(rows, PLANE, split_axis=0, concat_axis=0, tiled=True)  18.7 us
    ppermute x1, starting transfers between devices, on_device(): swapped = lax.ppermute(swap, 'zh', [(0, 1), (1, 0)])  16.3 us
    all_to_all x1, blocking collectives, on_device(): got = lax.all_to_all(spread, PLANE, split_axis=0, concat_axis=0, tiled=True)  14.4 us
    pallas_call x8, Pallas kernels, call(): pl.pallas_call(body, out_shape=out_shape, in_specs=[pl.BlockSpec(memory_s...  13.7 us
    all_to_all x1, blocking collectives, on_device(): done = lax.all_to_all(done, PLANE, split_axis=0, concat_axis=0, tiled=True)  11.6 us
    all_to_all x1, waiting for transfers between devices, on_device(): own = lax.all_to_all(spread, PLANE, split_axis=0, concat_axis=0, tiled=True)  10.3 us
    all_to_all x1, starting transfers between devices, on_device(): own = lax.all_to_all(spread, PLANE, split_axis=0, concat_axis=0, tiled=True)  8.05 us
    all_to_all x1, starting transfers between devices, on_device(): lax.all_to_all(right, 'row', split_axis=0, concat_axis=0, tiled=True)  5.47 us
  transfers between devices with their start and end apart: 4, of which 3 were waited for; matrix products, arithmetic and copies ran while one was open for 0% of the time, Pallas kernels for 5%

profile of v9, /device:TPU:1, one launch (start us, length us, event | category | flops | bytes accessed | tf_op | source)
XLA Modules:
  0.0 109.3 jit_solution(17613226934289437516)
XLA Ops:
  0.6 1.9 %shard_map.265 = (bf16[656,128]{1,0:T(8,128)(2,1)S(1)}, f32[64,8]{1,0:T(8,128)S(1)}, f32[8,128]{1,0:T(8,128)S(1)}, bf16[64,64]{1,0:T(8,128)(2,1)S(1)}) custom-call(bf16[4,64,64]{2,1,0:T(8,128)(2,1)} %refs_0_.1, s32[4,64]{1,0:T(4,128)} %refs_1_.1, bf16[64,80]{1,0:T(8,128)(2,1)} %bitcast.17, f32[1,64]{1,0:T(1,128)} %bitcast.20, bf16[8,64]{1,0:T(8,128)(2,1)} %nodes_ref.1, ...), custom_call_target="tpu_custom_call" | custom-call | tf_op jit(solution)/shard_map/pallas_call | solution.py:323
  2.5 16.3 %collective-permute-start = (bf16[656,128]{1,0:T(8,128)(2,1)S(1)}, bf16[656,128]{1,0:T(8,128)(2,1)S(1)}, u32[]{:S(2)}, u32[]{:S(2)}) collective-permute-start(bf16[656,128]{1,0:T(8,128)(2,1)S(1)} %get-tuple-element.12.block_ref), channel_id=1, source_target_pairs={{0,1},{1,0},{2,3},{3,2},{4,5},{5,4},{6,7},{7,6},{8,9},{9,8},{10,11... | collective-permute-start | bytes 503816 | tf_op jit(solution)/shard_map/ppermute | solution.py:389
  18.8 1.4 %shard_map.266 = bf16[32,64,128]{2,1,0:T(8,128)(2,1)} custom-call(bf16[32,16,128]{2,1,0:T(8,128)(2,1)S(1)} %bitcast.15, bf16[656,128]{1,0:T(8,128)(2,1)S(1)} %get-tuple-element.12.block_ref, bf16[64,64]{1,0:T(8,128)(2,1)S(1)} %get-tuple-element.13.factor_ref), custom_call_target="tpu_custom_call" | custom-call | tf_op jit(solution)/shard_map/pallas_call | solution.py:323
  20.3 8.0 %all-to-all-start = ((bf16[32,64,128]{2,1,0:T(8,128)(2,1)}), bf16[32,64,128]{2,1,0:T(8,128)(2,1)S(1)}, u32[]{:S(2)}, u32[]{:S(2)}) async-start(bf16[32,64,128]{2,1,0:T(8,128)(2,1)} %shard_map.266), calls=%async_computation | async-start | bytes 1048576 | tf_op jit(solution)/shard_map/all_to_all | solution.py:391
  28.3 0.0 copy-start.12
  28.3 0.0 copy-start.13
  28.4 0.0 copy-start.10
  28.4 0.0 copy-start.11
  28.4 0.6 shard_map.267
  29.0 10.3 %all-to-all-done.own_ref = bf16[32,64,128]{2,1,0:T(8,128)(2,1)S(1)} async-done(((bf16[32,64,128]{2,1,0:T(8,128)(2,1)}), bf16[32,64,128]{2,1,0:T(8,128)(2,1)S(1)}, u32[]{:S(2)}, u32[]{:S(2)}) %all-to-all-start) | async-done | bytes 524320 | tf_op jit(solution)/shard_map/all_to_all | solution.py:391
  39.4 14.4 %all_to_all.25.came_ref = bf16[32,48,128]{2,1,0:T(8,128)(2,1)S(1)} all-to-all(bf16[32,48,128]{2,1,0:T(8,128)(2,1)S(1)} %shard_map.267), channel_id=1, replica_groups=mesh['x'=4,'core'=2,'row'=8,'y'=4,'zh'=2] {'x','core','y'}, dimensions={0} | all-to-all | bytes 786432 | tf_op jit(solution)/shard_map/all_to_all | solution.py:394
  53.7 1.2 %shard_map.268 = (bf16[8,128,128]{2,1,0:T(8,128)(2,1)}, f32[8,128]{1,0:T(8,128)S(1)}) custom-call(bf16[32,64,128]{2,1,0:T(8,128)(2,1)S(1)} %all-to-all-done.own_ref, bf16[32,48,128]{2,1,0:T(8,128)(2,1)S(1)} %all_to_all.25.came_ref), custom_call_target="tpu_custom_call" | custom-call | tf_op jit(solution)/shard_map/pallas_call | solution.py:323
  54.9 5.5 %all-to-all-start.2 = ((bf16[8,128,128]{2,1,0:T(8,128)(2,1)}), bf16[8,128,128]{2,1,0:T(8,128)(2,1)S(1)}, u32[]{:S(2)}, u32[]{:S(2)}) async-start(bf16[8,128,128]{2,1,0:T(8,128)(2,1)} %get-tuple-element.17), calls=%async_computation.2 | async-start | bytes 524288 | tf_op jit(solution)/shard_map/all_to_all | solution.py:396
  60.4 0.1 copy.29.penalty_ref
  60.5 0.1 copy.30.step_ref
  60.6 0.5 copy-done.7
  61.1 0.2 copy-done.9
  61.3 0.0 copy-done.8
  61.3 2.3 %shard_map.269 = (bf16[8,64]{1,0:T(8,128)(2,1)}, f32[3,8]{1,0:T(4,128)}, f32[8,128]{1,0:T(8,128)S(1)}) custom-call(s32[8]{0:T(128)S(1)} %copy-done.11, s32[1]{0:T(128)} %bitcast.half_ref, f32[8,128]{1,0:T(8,128)S(1)} %get-tuple-element.14.after_ref, bf16[32,64,128]{2,1,0:T(8,128)(2,1)S(1)} %all-to-all-done.own_ref, ...), custom_call_target="tpu_custom_call" | custom-call | tf_op jit(solution)/shard_map/pallas_call | solution.py:323
  63.6 0.6 shard_map.270.own_ref
  64.2 2.9 %collective-permute-start.1 = (bf16[1024,256]{1,0:T(8,128)(2,1)S(1)}, bf16[1024,256]{1,0:T(8,128)(2,1)S(1)}, u32[]{:S(2)}, u32[]{:S(2)}) collective-permute-start(bf16[1024,256]{1,0:T(8,128)(2,1)S(1)} %shard_map.270.own_ref), channel_id=1, source_target_pairs={{0,64},{64,0},{1,65},{65,1},{2,66},{66,2},{3,67},{67,3},{4,68},{68... | collective-permute-start | bytes 1572872 | tf_op jit(solution)/shard_map/ppermute | solution.py:418
  67.1 1.5 %collective-permute-done.1.other_ref = bf16[1024,256]{1,0:T(8,128)(2,1)S(1)} collective-permute-done((bf16[1024,256]{1,0:T(8,128)(2,1)S(1)}, bf16[1024,256]{1,0:T(8,128)(2,1)S(1)}, u32[]{:S(2)}, u32[]{:S(2)}) %collective-permute-start.1) | collective-permute-done | bytes 524320 | tf_op jit(solution)/shard_map/ppermute | solution.py:418
  68.6 4.0 %all-to-all-done.2.right_in = bf16[8,128,128]{2,1,0:T(8,128)(2,1)S(1)} async-done(((bf16[8,128,128]{2,1,0:T(8,128)(2,1)}), bf16[8,128,128]{2,1,0:T(8,128)(2,1)S(1)}, u32[]{:S(2)}, u32[]{:S(2)}) %all-to-all-start.2) | async-done | bytes 262176 | tf_op jit(solution)/shard_map/all_to_all | solution.py:396
  72.6 2.4 %shard_map.271 = bf16[32,48,128]{2,1,0:T(8,128)(2,1)S(1)} custom-call(s32[1]{0:T(128)} %bitcast.10.place_ref, bf16[1024,256]{1,0:T(8,128)(2,1)S(1)} %shard_map.270.own_ref, bf16[1024,256]{1,0:T(8,128)(2,1)S(1)} %collective-permute-done.1.other_ref, bf16[8,128,128]{2,1,0:T(8,128)(2,1)S(1)} %all-to-all-done.2.right_in, ...), custom_call_target="tpu_custom_call" | custom-call | tf_op jit(solution)/shard_map/pallas_call | solution.py:323
  75.1 0.0 copy-start.2
  75.1 0.0 copy-start.3
  75.1 0.0 copy-start.5
  75.1 0.0 copy-start.6
  75.1 18.7 %all_to_all.26.got_ref = bf16[32,48,128]{2,1,0:T(8,128)(2,1)S(1)} all-to-all(bf16[32,48,128]{2,1,0:T(8,128)(2,1)S(1)} %shard_map.271), channel_id=1, replica_groups=mesh['x'=4,'core'=2,'row'=8,'y'=4,'zh'=2] {'x','core','y'}, dimensions={0} | all-to-all | bytes 786432 | tf_op jit(solution)/shard_map/all_to_all | solution.py:431
  93.8 3.2 %shard_map.272 = bf16[32,16,128]{2,1,0:T(8,128)(2,1)S(1)} custom-call(s32[1]{0:T(128)} %bitcast.half_ref, bf16[32,64,128]{2,1,0:T(8,128)(2,1)S(1)} %all-to-all-done.own_ref, bf16[32,48,128]{2,1,0:T(8,128)(2,1)S(1)} %all_to_all.26.got_ref, f32[8,128]{1,0:T(8,128)S(1)} %get-tuple-element.18.consts_ref, bf16[128,128]{1,0:T(8,128)(2,1)S(1)} %copy-done.2, ...), custom_call_target="tpu_custom_call" | custom-call | tf_op jit(solution)/shard_map/pallas_call | solution.py:323
  97.1 11.6 %all_to_all.27 = bf16[32,16,128]{2,1,0:T(8,128)(2,1)S(1)} all-to-all(bf16[32,16,128]{2,1,0:T(8,128)(2,1)S(1)} %shard_map.272), channel_id=1, replica_groups=mesh['x'=4,'core'=2,'row'=8,'y'=4,'zh'=2] {'x','core','y'}, dimensions={0} | all-to-all | bytes 262144 | tf_op jit(solution)/shard_map/all_to_all | solution.py:455
  108.6 0.7 copy.32
  (18 shorter events, 0.0 us)
Async XLA Ops:
  0.6 18.2 %copy-start = (bf16[64,8,128]{2,1,0:T(8,128)(2,1)S(1)}, bf16[64,8,128]{2,1,0:T(8,128)(2,1)}, u32[]{:S(2)}) copy-start(bf16[64,8,128]{2,1,0:T(8,128)(2,1)} %param.34) | copy-start | bytes 393220
  2.5 25.8 %collective-permute-start = (bf16[656,128]{1,0:T(8,128)(2,1)S(1)}, bf16[656,128]{1,0:T(8,128)(2,1)S(1)}, u32[]{:S(2)}, u32[]{:S(2)}) collective-permute-start(bf16[656,128]{1,0:T(8,128)(2,1)S(1)} %get-tuple-element.12.block_ref), channel_id=1, source_target_pairs={{0,1},{1,0},{2,3},{3,2},{4,5},{5,4},{6,7},{7,6},{8,9},{9,8},{10,11... | collective-permute-start | bytes 503816 | tf_op jit(solution)/shard_map/ppermute | solution.py:389
  20.3 19.1 %all-to-all-start = ((bf16[32,64,128]{2,1,0:T(8,128)(2,1)}), bf16[32,64,128]{2,1,0:T(8,128)(2,1)S(1)}, u32[]{:S(2)}, u32[]{:S(2)}) async-start(bf16[32,64,128]{2,1,0:T(8,128)(2,1)} %shard_map.266), calls=%async_computation | async-start | bytes 1048576 | tf_op jit(solution)/shard_map/all_to_all | solution.py:391
  28.3 32.1 %copy-start.12 = (f32[4]{0:T(128)S(1)}, f32[4]{0:T(128)}, u32[]{:S(2)}) copy-start(f32[4]{0:T(128)} %param.50) | copy-start | bytes 52
  28.3 32.2 %copy-start.13 = (f32[4]{0:T(128)S(1)}, f32[4]{0:T(128)}, u32[]{:S(2)}) copy-start(f32[4]{0:T(128)} %param.51) | copy-start | bytes 52
  28.4 32.3 %copy-start.10 = (s32[8,64]{1,0:T(8,128)S(1)}, s32[8,64]{1,0:T(8,128)}, u32[]{:S(2)}) copy-start(s32[8,64]{1,0:T(8,128)} %index_ref.1) | copy-start | bytes 6148
  28.4 32.3 %copy-start.11 = (s32[8]{0:T(128)S(1)}, s32[8]{0:T(128)}, u32[]{:S(2)}) copy-start(s32[8]{0:T(128)} %count_ref.1) | copy-start | bytes 100
  54.9 17.7 %all-to-all-start.2 = ((bf16[8,128,128]{2,1,0:T(8,128)(2,1)}), bf16[8,128,128]{2,1,0:T(8,128)(2,1)S(1)}, u32[]{:S(2)}, u32[]{:S(2)}) async-start(bf16[8,128,128]{2,1,0:T(8,128)(2,1)} %get-tuple-element.17), calls=%async_computation.2 | async-start | bytes 524288 | tf_op jit(solution)/shard_map/all_to_all | solution.py:396
  60.4 0.7 copy-start.7
  60.6 0.7 copy-start.9
  60.6 0.7 copy-start.8
  63.6 9.0 %copy-start.1 = (bf16[1024,128]{1,0:T(8,128)(2,1)S(1)}, bf16[1024,128]{1,0:T(8,128)(2,1)}, u32[]{:S(2)}) copy-start(bf16[1024,128]{1,0:T(8,128)(2,1)} %weight_ref.1) | copy-start | bytes 786436
  64.2 4.4 %collective-permute-start.1 = (bf16[1024,256]{1,0:T(8,128)(2,1)S(1)}, bf16[1024,256]{1,0:T(8,128)(2,1)S(1)}, u32[]{:S(2)}, u32[]{:S(2)}) collective-permute-start(bf16[1024,256]{1,0:T(8,128)(2,1)S(1)} %shard_map.270.own_ref), channel_id=1, source_target_pairs={{0,64},{64,0},{1,65},{65,1},{2,66},{66,2},{3,67},{67,3},{4,68},{68... | collective-permute-start | bytes 1572872 | tf_op jit(solution)/shard_map/ppermute | solution.py:418
  75.1 18.8 %copy-start.2 = (bf16[128,128]{1,0:T(8,128)(2,1)S(1)}, bf16[128,128]{1,0:T(8,128)(2,1)}, u32[]{:S(2)}) copy-start(bf16[128,128]{1,0:T(8,128)(2,1)} %wq_ref.1) | copy-start | bytes 98308
  75.1 18.8 %copy-start.3 = (bf16[128,128]{1,0:T(8,128)(2,1)S(1)}, bf16[128,128]{1,0:T(8,128)(2,1)}, u32[]{:S(2)}) copy-start(bf16[128,128]{1,0:T(8,128)(2,1)} %wk_ref.1) | copy-start | bytes 98308
  75.1 18.7 %copy-start.4 = (bf16[128,128]{1,0:T(8,128)(2,1)S(1)}, bf16[128,128]{1,0:T(8,128)(2,1)}, u32[]{:S(2)}) copy-start(bf16[128,128]{1,0:T(8,128)(2,1)} %wv_ref.1) | copy-start | bytes 98308
  75.1 18.7 %copy-start.5 = (bf16[128,128]{1,0:T(8,128)(2,1)S(1)}, bf16[128,128]{1,0:T(8,128)(2,1)}, u32[]{:S(2)}) copy-start(bf16[128,128]{1,0:T(8,128)(2,1)} %wg_ref.1) | copy-start | bytes 98308
  75.1 18.7 %copy-start.6 = (bf16[128,128]{1,0:T(8,128)(2,1)S(1)}, bf16[128,128]{1,0:T(8,128)(2,1)}, u32[]{:S(2)}) copy-start(bf16[128,128]{1,0:T(8,128)(2,1)} %wo_ref.3) | copy-start | bytes 98308

commit v10 on v9

--- a/solution.py
+++ b/solution.py
@@ -139,14 +139,15 @@
 
 def right_kernel(own_ref, came_ref, out_ref, token_ref):
     token_ref[...] = jnp.zeros_like(token_ref)
-    row, source = iota((128, 1), 0), iota((128, 512), 1)
-    start = ((row >> 2) << 4) + ((row & 3) << 1) + 8
+    row, source = iota((64, 1), 0), iota((64, 128), 1)
+    turn = one_where(source == (((row >> 2) & 7) << 4) + ((row & 3) << 1) + (row >> 5) + 8)
     at, lane = iota((128, 128), 0), iota((128, 128), 1)
     total = jnp.zeros((128, 128), F32)
     for plane, got_ref in enumerate((own_ref, came_ref)):
         rows = got_ref[:, 32:48].reshape(512, 128)
+        parts = [dot(turn, rows[g * 128 : (g + 1) * 128]).astype(BF16) for g in range(4)]
         for column in range(2):
-            picked = dot(one_where(source == start + column), rows).astype(BF16)
+            picked = jnp.concatenate([part[column * 32 : column * 32 + 32] for part in parts], 0)
             shift = (plane * 2 + column) * 32
             keep = (lane >= shift) & (lane < shift + 32)
             total = total + dot(picked, one_where((at + shift == lane + 32) & keep))

time: 110 us -> 110 us (level)
  no operation moved by 1% of the time
where the time goes in v10:
time: 110 us; the launch traced here: 109 us
  blocking collectives  44.6 us (41%)
  starting transfers between devices  32.7 us (30%)
  waiting for transfers between devices  15.8 us (14%)
  Pallas kernels  13.6 us (12%)
  local copies, waits for them, and re-layouts  1.6 us (1%)
    all_to_all x1, blocking collectives, on_device(): rows = lax.all_to_all(rows, PLANE, split_axis=0, concat_axis=0, tiled=True)  18.7 us
    ppermute x1, starting transfers between devices, on_device(): swapped = lax.ppermute(swap, 'zh', [(0, 1), (1, 0)])  16.3 us
    all_to_all x1, blocking collectives, on_device(): got = lax.all_to_all(spread, PLANE, split_axis=0, concat_axis=0, tiled=True)  14.4 us
    pallas_call x8, Pallas kernels, call(): pl.pallas_call(body, out_shape=out_shape, in_specs=[pl.BlockSpec(memory_s...  13.6 us
    all_to_all x1, blocking collectives, on_device(): done = lax.all_to_all(done, PLANE, split_axis=0, concat_axis=0, tiled=True)  11.6 us
    all_to_all x1, waiting for transfers between devices, on_device(): own = lax.all_to_all(spread, PLANE, split_axis=0, concat_axis=0, tiled=True)  10.3 us
    all_to_all x1, starting transfers between devices, on_device(): own = lax.all_to_all(spread, PLANE, split_axis=0, concat_axis=0, tiled=True)  8.05 us
    all_to_all x1, starting transfers between devices, on_device(): lax.all_to_all(right, 'row', split_axis=0, concat_axis=0, tiled=True)  5.47 us
  transfers between devices with their start and end apart: 4, of which 3 were waited for; matrix products, arithmetic and copies ran while one was open for 0% of the time, Pallas kernels for 5%

profile of v10, /device:TPU:1, one launch (start us, length us, event | category | flops | bytes accessed | tf_op | source)
XLA Modules:
  0.0 109.2 jit_solution(5345623037058682257)
XLA Ops:
  0.6 1.9 %shard_map.265 = (bf16[656,128]{1,0:T(8,128)(2,1)S(1)}, f32[64,8]{1,0:T(8,128)S(1)}, f32[8,128]{1,0:T(8,128)S(1)}, bf16[64,64]{1,0:T(8,128)(2,1)S(1)}) custom-call(bf16[4,64,64]{2,1,0:T(8,128)(2,1)} %refs_0_.1, s32[4,64]{1,0:T(4,128)} %refs_1_.1, bf16[64,80]{1,0:T(8,128)(2,1)} %bitcast.17, f32[1,64]{1,0:T(1,128)} %bitcast.20, bf16[8,64]{1,0:T(8,128)(2,1)} %nodes_ref.1, ...), custom_call_target="tpu_custom_call" | custom-call | tf_op jit(solution)/shard_map/pallas_call | solution.py:324
  2.5 16.3 %collective-permute-start = (bf16[656,128]{1,0:T(8,128)(2,1)S(1)}, bf16[656,128]{1,0:T(8,128)(2,1)S(1)}, u32[]{:S(2)}, u32[]{:S(2)}) collective-permute-start(bf16[656,128]{1,0:T(8,128)(2,1)S(1)} %get-tuple-element.12.block_ref), channel_id=1, source_target_pairs={{0,1},{1,0},{2,3},{3,2},{4,5},{5,4},{6,7},{7,6},{8,9},{9,8},{10,11... | collective-permute-start | bytes 503816 | tf_op jit(solution)/shard_map/ppermute | solution.py:390
  18.8 1.4 %shard_map.266 = bf16[32,64,128]{2,1,0:T(8,128)(2,1)} custom-call(bf16[32,16,128]{2,1,0:T(8,128)(2,1)S(1)} %bitcast.15, bf16[656,128]{1,0:T(8,128)(2,1)S(1)} %get-tuple-element.12.block_ref, bf16[64,64]{1,0:T(8,128)(2,1)S(1)} %get-tuple-element.13.factor_ref), custom_call_target="tpu_custom_call" | custom-call | tf_op jit(solution)/shard_map/pallas_call | solution.py:324
  20.3 8.0 %all-to-all-start = ((bf16[32,64,128]{2,1,0:T(8,128)(2,1)}), bf16[32,64,128]{2,1,0:T(8,128)(2,1)S(1)}, u32[]{:S(2)}, u32[]{:S(2)}) async-start(bf16[32,64,128]{2,1,0:T(8,128)(2,1)} %shard_map.266), calls=%async_computation | async-start | bytes 1048576 | tf_op jit(solution)/shard_map/all_to_all | solution.py:392
  28.3 0.0 copy-start.12
  28.3 0.0 copy-start.13
  28.4 0.0 copy-start.10
  28.4 0.0 copy-start.11
  28.4 0.6 shard_map.267
  29.0 10.3 %all-to-all-done.own_ref = bf16[32,64,128]{2,1,0:T(8,128)(2,1)S(1)} async-done(((bf16[32,64,128]{2,1,0:T(8,128)(2,1)}), bf16[32,64,128]{2,1,0:T(8,128)(2,1)S(1)}, u32[]{:S(2)}, u32[]{:S(2)}) %all-to-all-start) | async-done | bytes 524320 | tf_op jit(solution)/shard_map/all_to_all | solution.py:392
  39.4 14.4 %all_to_all.25.came_ref = bf16[32,48,128]{2,1,0:T(8,128)(2,1)S(1)} all-to-all(bf16[32,48,128]{2,1,0:T(8,128)(2,1)S(1)} %shard_map.267), channel_id=1, replica_groups=mesh['x'=4,'core'=2,'row'=8,'y'=4,'zh'=2] {'x','core','y'}, dimensions={0} | all-to-all | bytes 786432 | tf_op jit(solution)/shard_map/all_to_all | solution.py:395
  53.7 1.2 %shard_map.268 = (bf16[8,128,128]{2,1,0:T(8,128)(2,1)}, f32[8,128]{1,0:T(8,128)S(1)}) custom-call(bf16[32,64,128]{2,1,0:T(8,128)(2,1)S(1)} %all-to-all-done.own_ref, bf16[32,48,128]{2,1,0:T(8,128)(2,1)S(1)} %all_to_all.25.came_ref), custom_call_target="tpu_custom_call" | custom-call | tf_op jit(solution)/shard_map/pallas_call | solution.py:324
  54.9 5.5 %all-to-all-start.2 = ((bf16[8,128,128]{2,1,0:T(8,128)(2,1)}), bf16[8,128,128]{2,1,0:T(8,128)(2,1)S(1)}, u32[]{:S(2)}, u32[]{:S(2)}) async-start(bf16[8,128,128]{2,1,0:T(8,128)(2,1)} %get-tuple-element.17), calls=%async_computation.2 | async-start | bytes 524288 | tf_op jit(solution)/shard_map/all_to_all | solution.py:397
  60.4 0.1 copy.29.penalty_ref
  60.5 0.1 copy.30.step_ref
  60.6 0.5 copy-done.7
  61.1 0.2 copy-done.9
  61.2 0.0 copy-done.8
  61.2 2.3 %shard_map.269 = (bf16[8,64]{1,0:T(8,128)(2,1)}, f32[3,8]{1,0:T(4,128)}, f32[8,128]{1,0:T(8,128)S(1)}) custom-call(s32[8]{0:T(128)S(1)} %copy-done.11, s32[1]{0:T(128)} %bitcast.half_ref, f32[8,128]{1,0:T(8,128)S(1)} %get-tuple-element.14.after_ref, bf16[32,64,128]{2,1,0:T(8,128)(2,1)S(1)} %all-to-all-done.own_ref, ...), custom_call_target="tpu_custom_call" | custom-call | tf_op jit(solution)/shard_map/pallas_call | solution.py:324
  63.6 0.6 shard_map.270.own_ref
  64.1 2.9 %collective-permute-start.1 = (bf16[1024,256]{1,0:T(8,128)(2,1)S(1)}, bf16[1024,256]{1,0:T(8,128)(2,1)S(1)}, u32[]{:S(2)}, u32[]{:S(2)}) collective-permute-start(bf16[1024,256]{1,0:T(8,128)(2,1)S(1)} %shard_map.270.own_ref), channel_id=1, source_target_pairs={{0,64},{64,0},{1,65},{65,1},{2,66},{66,2},{3,67},{67,3},{4,68},{68... | collective-permute-start | bytes 1572872 | tf_op jit(solution)/shard_map/ppermute | solution.py:419
  67.0 1.5 %collective-permute-done.1.other_ref = bf16[1024,256]{1,0:T(8,128)(2,1)S(1)} collective-permute-done((bf16[1024,256]{1,0:T(8,128)(2,1)S(1)}, bf16[1024,256]{1,0:T(8,128)(2,1)S(1)}, u32[]{:S(2)}, u32[]{:S(2)}) %collective-permute-start.1) | collective-permute-done | bytes 524320 | tf_op jit(solution)/shard_map/ppermute | solution.py:419
  68.6 4.0 %all-to-all-done.2.right_in = bf16[8,128,128]{2,1,0:T(8,128)(2,1)S(1)} async-done(((bf16[8,128,128]{2,1,0:T(8,128)(2,1)}), bf16[8,128,128]{2,1,0:T(8,128)(2,1)S(1)}, u32[]{:S(2)}, u32[]{:S(2)}) %all-to-all-start.2) | async-done | bytes 262176 | tf_op jit(solution)/shard_map/all_to_all | solution.py:397
  72.5 2.4 %shard_map.271 = bf16[32,48,128]{2,1,0:T(8,128)(2,1)S(1)} custom-call(s32[1]{0:T(128)} %bitcast.10.place_ref, bf16[1024,256]{1,0:T(8,128)(2,1)S(1)} %shard_map.270.own_ref, bf16[1024,256]{1,0:T(8,128)(2,1)S(1)} %collective-permute-done.1.other_ref, bf16[8,128,128]{2,1,0:T(8,128)(2,1)S(1)} %all-to-all-done.2.right_in, ...), custom_call_target="tpu_custom_call" | custom-call | tf_op jit(solution)/shard_map/pallas_call | solution.py:324
  75.0 0.0 copy-start.2
  75.0 0.0 copy-start.3
  75.0 0.0 copy-start.5
  75.0 0.0 copy-start.6
  75.0 18.7 %all_to_all.26.got_ref = bf16[32,48,128]{2,1,0:T(8,128)(2,1)S(1)} all-to-all(bf16[32,48,128]{2,1,0:T(8,128)(2,1)S(1)} %shard_map.271), channel_id=1, replica_groups=mesh['x'=4,'core'=2,'row'=8,'y'=4,'zh'=2] {'x','core','y'}, dimensions={0} | all-to-all | bytes 786432 | tf_op jit(solution)/shard_map/all_to_all | solution.py:432
  93.8 3.2 %shard_map.272 = bf16[32,16,128]{2,1,0:T(8,128)(2,1)S(1)} custom-call(s32[1]{0:T(128)} %bitcast.half_ref, bf16[32,64,128]{2,1,0:T(8,128)(2,1)S(1)} %all-to-all-done.own_ref, bf16[32,48,128]{2,1,0:T(8,128)(2,1)S(1)} %all_to_all.26.got_ref, f32[8,128]{1,0:T(8,128)S(1)} %get-tuple-element.18.consts_ref, bf16[128,128]{1,0:T(8,128)(2,1)S(1)} %copy-done.2, ...), custom_call_target="tpu_custom_call" | custom-call | tf_op jit(solution)/shard_map/pallas_call | solution.py:324
  97.0 11.6 %all_to_all.27 = bf16[32,16,128]{2,1,0:T(8,128)(2,1)S(1)} all-to-all(bf16[32,16,128]{2,1,0:T(8,128)(2,1)S(1)} %shard_map.272), channel_id=1, replica_groups=mesh['x'=4,'core'=2,'row'=8,'y'=4,'zh'=2] {'x','core','y'}, dimensions={0} | all-to-all | bytes 262144 | tf_op jit(solution)/shard_map/all_to_all | solution.py:456
  108.5 0.7 copy.32
  (18 shorter events, 0.0 us)
Async XLA Ops:
  0.6 18.2 %copy-start = (bf16[64,8,128]{2,1,0:T(8,128)(2,1)S(1)}, bf16[64,8,128]{2,1,0:T(8,128)(2,1)}, u32[]{:S(2)}) copy-start(bf16[64,8,128]{2,1,0:T(8,128)(2,1)} %param.34) | copy-start | bytes 393220
  2.5 25.8 %collective-permute-start = (bf16[656,128]{1,0:T(8,128)(2,1)S(1)}, bf16[656,128]{1,0:T(8,128)(2,1)S(1)}, u32[]{:S(2)}, u32[]{:S(2)}) collective-permute-start(bf16[656,128]{1,0:T(8,128)(2,1)S(1)} %get-tuple-element.12.block_ref), channel_id=1, source_target_pairs={{0,1},{1,0},{2,3},{3,2},{4,5},{5,4},{6,7},{7,6},{8,9},{9,8},{10,11... | collective-permute-start | bytes 503816 | tf_op jit(solution)/shard_map/ppermute | solution.py:390
  20.3 19.1 %all-to-all-start = ((bf16[32,64,128]{2,1,0:T(8,128)(2,1)}), bf16[32,64,128]{2,1,0:T(8,128)(2,1)S(1)}, u32[]{:S(2)}, u32[]{:S(2)}) async-start(bf16[32,64,128]{2,1,0:T(8,128)(2,1)} %shard_map.266), calls=%async_computation | async-start | bytes 1048576 | tf_op jit(solution)/shard_map/all_to_all | solution.py:392
  28.3 32.0 %copy-start.12 = (f32[4]{0:T(128)S(1)}, f32[4]{0:T(128)}, u32[]{:S(2)}) copy-start(f32[4]{0:T(128)} %param.50) | copy-start | bytes 52
  28.3 32.1 %copy-start.13 = (f32[4]{0:T(128)S(1)}, f32[4]{0:T(128)}, u32[]{:S(2)}) copy-start(f32[4]{0:T(128)} %param.51) | copy-start | bytes 52
  28.4 32.2 %copy-start.10 = (s32[8,64]{1,0:T(8,128)S(1)}, s32[8,64]{1,0:T(8,128)}, u32[]{:S(2)}) copy-start(s32[8,64]{1,0:T(8,128)} %index_ref.1) | copy-start | bytes 6148
  28.4 32.2 %copy-start.11 = (s32[8]{0:T(128)S(1)}, s32[8]{0:T(128)}, u32[]{:S(2)}) copy-start(s32[8]{0:T(128)} %count_ref.1) | copy-start | bytes 100
  54.9 17.7 %all-to-all-start.2 = ((bf16[8,128,128]{2,1,0:T(8,128)(2,1)}), bf16[8,128,128]{2,1,0:T(8,128)(2,1)S(1)}, u32[]{:S(2)}, u32[]{:S(2)}) async-start(bf16[8,128,128]{2,1,0:T(8,128)(2,1)} %get-tuple-element.17), calls=%async_computation.2 | async-start | bytes 524288 | tf_op jit(solution)/shard_map/all_to_all | solution.py:397
  60.3 0.7 copy-start.7
  60.5 0.7 copy-start.9
  60.5 0.7 copy-start.8
  63.6 9.0 %copy-start.1 = (bf16[1024,128]{1,0:T(8,128)(2,1)S(1)}, bf16[1024,128]{1,0:T(8,128)(2,1)}, u32[]{:S(2)}) copy-start(bf16[1024,128]{1,0:T(8,128)(2,1)} %weight_ref.1) | copy-start | bytes 786436
  64.1 4.4 %collective-permute-start.1 = (bf16[1024,256]{1,0:T(8,128)(2,1)S(1)}, bf16[1024,256]{1,0:T(8,128)(2,1)S(1)}, u32[]{:S(2)}, u32[]{:S(2)}) collective-permute-start(bf16[1024,256]{1,0:T(8,128)(2,1)S(1)} %shard_map.270.own_ref), channel_id=1, source_target_pairs={{0,64},{64,0},{1,65},{65,1},{2,66},{66,2},{3,67},{67,3},{4,68},{68... | collective-permute-start | bytes 1572872 | tf_op jit(solution)/shard_map/ppermute | solution.py:419
  75.0 18.8 %copy-start.2 = (bf16[128,128]{1,0:T(8,128)(2,1)S(1)}, bf16[128,128]{1,0:T(8,128)(2,1)}, u32[]{:S(2)}) copy-start(bf16[128,128]{1,0:T(8,128)(2,1)} %wq_ref.1) | copy-start | bytes 98308
  75.0 18.8 %copy-start.3 = (bf16[128,128]{1,0:T(8,128)(2,1)S(1)}, bf16[128,128]{1,0:T(8,128)(2,1)}, u32[]{:S(2)}) copy-start(bf16[128,128]{1,0:T(8,128)(2,1)} %wk_ref.1) | copy-start | bytes 98308
  75.0 18.7 %copy-start.4 = (bf16[128,128]{1,0:T(8,128)(2,1)S(1)}, bf16[128,128]{1,0:T(8,128)(2,1)}, u32[]{:S(2)}) copy-start(bf16[128,128]{1,0:T(8,128)(2,1)} %wv_ref.1) | copy-start | bytes 98308
  75.0 18.7 %copy-start.5 = (bf16[128,128]{1,0:T(8,128)(2,1)S(1)}, bf16[128,128]{1,0:T(8,128)(2,1)}, u32[]{:S(2)}) copy-start(bf16[128,128]{1,0:T(8,128)(2,1)} %wg_ref.1) | copy-start | bytes 98308
  75.0 18.7 %copy-start.6 = (bf16[128,128]{1,0:T(8,128)(2,1)S(1)}, bf16[128,128]{1,0:T(8,128)(2,1)}, u32[]{:S(2)}) copy-start(bf16[128,128]{1,0:T(8,128)(2,1)} %wo_ref.3) | copy-start | bytes 98308
